TPU v7x, 32 devices: a whole 2x2x4 slice. The times are simulated.
32 devices in a mesh: rep: 4 (over y, x), tp: 8 (over z, core).
Axes of the slice: x: 2, y: 2, z: 4, core: 2. Of those that a mesh axis runs over, the one named last changes fastest.
Arguments:
- embeds: bfloat16 [3136, 5120], P('rep', 'tp'), parts along dimension 0, may hold values from -6 to 6
- remask: int32 [3136], P('rep'), parts along dimension 0, may hold values 0 or 1
- lengths: int32 [16], P('rep'), parts along dimension 0, may hold values from 49 to 196, as said below
- mask_vec: bfloat16 [5120], P('tp'), may hold values from -6 to 6
- attn_gain: bfloat16 [5120], replicated, may hold values from 0.25 to 1.75
- w_query: bfloat16 [5120, 4096], P(None, 'tp'), may hold values from -0.078125 to 0.078125
- q_bias: bfloat16 [4096], P('tp'), may hold values from -200 to 200
- w_key: bfloat16 [5120, 1024], P(None, 'tp'), may hold values from -0.078125 to 0.078125
- w_value: bfloat16 [5120, 1024], P(None, 'tp'), may hold values from -0.078125 to 0.078125
- v_bias: bfloat16 [1024], P('tp'), may hold values from -3 to 3
- w_out: bfloat16 [4096, 5120], P('tp'), may hold values from -0.125 to 0.125
- head_gain: bfloat16 [5120], replicated, may hold values from 0.25 to 1.75
- w_head: bfloat16 [5120, 512], P(None, 'tp'), may hold values from -20 to 20
Outputs:
- hidden: bfloat16 [3136, 5120], P('rep', 'tp'), parts along dimension 0
- logprob: float32 [3136, 512], P('rep', 'tp'), parts along dimension 0
There are 4 independent parts, one for each index of `rep`. A program takes and returns all parts, laid end to end along the dimension named above; an argument that names none is the same for every part. Nothing has to cross between parts.
Inputs may be any that keep to these rules, and one draw needn't show every extreme that they name: `lengths`: every request has at least 49 tokens, and one request of each part has exactly 196.
All inputs are finite; a program needn't handle non-finite values.
Results may differ from a plain program's by a relative error of at most 0.018.
The roundings to bfloat16 on the way count: a program that leaves them out, or rounds other values in their place, can miss the bound.
Values may be sent and summed in bfloat16 or wider, within the bound.
No kernel may reach another device: no remote copies, remote signals or barrier semaphores. Data moves between devices by JAX's collectives and lax.ppermute only.
A program may use at most 128 MiB of HBM per device.

v0:
```python
import jax
import jax.numpy as jnp
from jax import lax
from jax.sharding import PartitionSpec as P

KVH = 8
HS = 128
L = 196


EPS = 1e-06


def swapped(value, axis, apart):
    mask = 2**apart
    pairs = [(source, source ^ mask) for source in range(lax.axis_size(axis))]
    return lax.ppermute(value, axis, pairs)


def combined_all(x, axis, combine):
    everything = jax.tree.map(lambda part: lax.all_gather(part, axis), x)
    initial = jax.tree.map(lambda part: part[0], everything)

    def lap(k, so_far):
        return combine(so_far, jax.tree.map(lambda part: part[k], everything))

    return lax.fori_loop(1, lax.axis_size(axis), lap, initial)


def rms_norm(matrix, gain):
    wide = matrix.astype(jnp.float32)
    inverse = lax.rsqrt(jnp.mean(wide * wide, axis=-1, keepdims=True) + EPS)
    return (wide * inverse * gain.astype(jnp.float32)).astype(jnp.bfloat16)


def combine_pair(first_pair, second_pair):
    top = jnp.maximum(first_pair[0], second_pair[0])
    total = first_pair[1] * jnp.exp(first_pair[0] - top) + second_pair[1] * jnp.exp(
        second_pair[0] - top
    )
    return (top, total)


def on_device(
    embeds,
    remask,
    lengths,
    mask_vec,
    attn_gain,
    w_query,
    q_bias,
    w_key,
    w_value,
    v_bias,
    w_out,
    head_gain,
    w_head,
):
    requests = lengths.shape[0]
    tokens_all = embeds.shape[0]
    masked_local = jnp.where(remask[:, None] == 1, mask_vec[None, :], embeds)
    gathered = lax.all_gather(masked_local, "tp", axis=1, tiled=True)
    normed = rms_norm(gathered, attn_gain)
    queries = (
        jnp.dot(normed, w_query, preferred_element_type=jnp.float32) + q_bias.astype(jnp.float32)
    ).astype(jnp.bfloat16)
    key_rows = jnp.dot(normed, w_key, preferred_element_type=jnp.float32).astype(jnp.bfloat16)
    value_rows = (
        jnp.dot(normed, w_value, preferred_element_type=jnp.float32) + v_bias.astype(jnp.float32)
    ).astype(jnp.bfloat16)
    tp_count = lax.axis_size("tp")
    span = max(1, tp_count // KVH)
    levels = span.bit_length() - 1
    my_index = lax.axis_index("tp")
    for level in range(levels):
        other_key, other_value = swapped((key_rows, value_rows), "tp", level)
        lower = jnp.bitwise_and(jnp.right_shift(my_index, level), 1) == 0
        key_rows = jnp.where(
            lower,
            jnp.concatenate([key_rows, other_key], axis=1),
            jnp.concatenate([other_key, key_rows], axis=1),
        )
        value_rows = jnp.where(
            lower,
            jnp.concatenate([value_rows, other_value], axis=1),
            jnp.concatenate([other_value, value_rows], axis=1),
        )
    heads_dev = queries.shape[1] // HS
    kv_count = key_rows.shape[1] // HS
    repeats = heads_dev // kv_count
    k_four = jnp.repeat(key_rows.reshape(requests, L, kv_count, HS), repeats, axis=2)
    v_four = jnp.repeat(value_rows.reshape(requests, L, kv_count, HS), repeats, axis=2)
    q_four = queries.reshape(requests, L, heads_dev, HS)
    scores = jnp.einsum(
        "rqhd,rkhd->rhqk", q_four, k_four, preferred_element_type=jnp.float32
    ) * HS ** (-0.5)
    valid = jnp.arange(L, dtype=jnp.int32)[None, :] < lengths[:, None]
    scores = jnp.where(valid[:, None, None, :], scores, jnp.float32(-1e30))
    peak = jnp.max(scores, axis=-1, keepdims=True)
    expo = jnp.exp(scores - peak)
    attn_prob = (expo / jnp.sum(expo, axis=-1, keepdims=True)).astype(jnp.bfloat16)
    context = jnp.einsum(
        "rhqk,rkhd->rqhd", attn_prob, v_four, preferred_element_type=jnp.float32
    ).astype(jnp.bfloat16)
    context = context.reshape(tokens_all, heads_dev * HS)
    portion = lax.psum_scatter(
        lax.dot_general(
            w_out, context, (((0,), (1,)), ((), ())), preferred_element_type=jnp.float32
        ).astype(jnp.bfloat16),
        "tp",
        scatter_dimension=0,
        tiled=True,
    ).astype(jnp.float32)
    hidden_local = (masked_local.astype(jnp.float32) + portion.T).astype(jnp.bfloat16)
    hidden_full = lax.all_gather(hidden_local, "tp", axis=1, tiled=True)
    normed_head = rms_norm(hidden_full, head_gain)
    logits = jnp.dot(normed_head, w_head, preferred_element_type=jnp.float32)
    local_top = jnp.max(logits, axis=-1)
    local_total = jnp.sum(jnp.exp(logits - local_top[:, None]), axis=-1)
    row_top, row_total = combined_all((local_top, local_total), "tp", combine_pair)
    log_total = row_top + jnp.log(row_total)
    return (hidden_local, logits - log_total[:, None])


def solution(mesh):
    placed = (
        P("rep", "tp"),
        P("rep"),
        P("rep"),
        P("tp"),
        P(),
        P(None, "tp"),
        P("tp"),
        P(None, "tp"),
        P(None, "tp"),
        P("tp"),
        P("tp", None),
        P(),
        P(None, "tp"),
    )
    return jax.shard_map(
        on_device,
        mesh=mesh,
        in_specs=placed,
        out_specs=(P("rep", "tp"), P("rep", "tp")),
        check_vma=False,
    )
```

profile of v0, /device:TPU:0, one launch (start us, length us, event | category | flops | bytes accessed | tf_op | source)
XLA Modules:
  0.0 361.0 jit_solution(12881601038346677541)
XLA Ops:
  7.2 0.8 broadcast_compare_fusion
  8.0 2.4 broadcast_select_fusion
  10.5 0.7 convert_element_type.57
  11.2 0.7 convert_element_type.61
  11.8 0.7 convert_element_type.59
  12.5 0.7 iota_compare_fusion
  13.2 79.1 %all-gather.5.cloned.1.call-done = bf16[784,5120]{1,0:T(8,128)(2,1)} async-done(((bf16[784,640]{1,0:T(8,128)(2,1)}), bf16[784,5120]{1,0:T(8,128)(2,1)}) %all-gather.5.cloned.1.call-update) | async-done | bytes 8028176 | tf_op jit(solution)/shard_map/all_gather | solution.py:62
  92.3 5.1 %fusion.1 = f32[784]{0:T(1024)S(1)} fusion(bf16[784,5120]{1,0:T(8,128)(2,1)} %all-gather.5.cloned.1.call-done), kind=kLoop, calls=%fused_computation.8 | loop fusion | flops 12041456 | bytes 8031296 | tf_op jit(solution)/shard_map/reduce_sum | solution.py:32
  97.4 0.5 copy-done.2
  97.9 6.9 %add_convert_fusion = bf16[784,512]{1,0:T(8,128)(2,1)S(1)} fusion(bf16[5120,512]{1,0:T(8,128)(2,1)} %param.20, f32[512]{0:T(512)S(1)} %convert_element_type.61, bf16[784,5120]{1,0:T(8,128)(2,1)S(1)} %copy-done.2, f32[5120]{0:T(1024)S(1)} %convert_element_type.57, f32[784]{0:T(1024)S(1)} %add_rsqrt_fusion.1), kind=kOutput, calls=%fused_computation.29 | convolution fusion | flops 4127277056 | bytes 14099520 | tf_op jit(solution)/shard_map/dot_general | solution.py:65
  105.0 5.6 %convolution_convert_fusion.1 = bf16[784,128]{1,0:T(8,128)(2,1)S(1)} fusion(bf16[5120,128]{1,0:T(8,128)(2,1)S(1)} %copy-done, bf16[784,5120]{1,0:T(8,128)(2,1)} %all-gather.5.cloned.1.call-done, f32[5120]{0:T(1024)S(1)} %convert_element_type.57, f32[784]{0:T(1024)S(1)} %add_rsqrt_fusion.1), kind=kOutput, calls=%fused_computation.34 | convolution fusion | flops 1043761152 | bytes 9563200 | tf_op jit(solution)/shard_map/dot_general | solution.py:67
  110.6 6.0 %fusion.20 = bf16[784,128]{1,0:T(8,128)(2,1)S(1)} fusion(bf16[5120,128]{1,0:T(8,128)(2,1)} %param.23, f32[128]{0:T(128)S(1)} %convert_element_type.59, bf16[784,5120]{1,0:T(8,128)(2,1)} %all-gather.5.cloned.1.call-done, f32[5120]{0:T(1024)S(1)} %convert_element_type.57, f32[784]{0:T(1024)S(1)} %add_rsqrt_fusion.1), kind=kOutput, calls=%fused_computation.33 | convolution fusion | flops 1043861504 | bytes 9563712 | tf_op jit(solution)/shard_map/dot_general | solution.py:69
  116.6 0.6 fusion.21
  117.2 1.7 fusion.32
  118.9 0.8 fusion.19
  119.7 0.3 copy.22
  120.0 1.1 slice-done
  121.1 0.3 slice-done.1
  121.4 6.6 %fusion.11 = bf16[5120,784]{0,1:T(8,128)(2,1)} fusion(bf16[512,5120]{1,0:T(8,128)(2,1)S(1)} %bitcast.22, bf16[98,8,4,128]{3,2,1,0:T(4,128)(2,1)S(1)} %bitcast.20), kind=kOutput, calls=%fused_computation.18 | convolution fusion | flops 4114432000 | bytes 14073856 | tf_op jit(solution)/shard_map/dot_general | solution.py:107
  128.0 12.5 %copy.24 = bf16[5120,784]{1,0:T(8,128)(2,1)} copy(bf16[5120,784]{0,1:T(8,128)(2,1)} %fusion.11) | data formatting | bytes 16056320
  140.6 95.7 %reduce-scatter.4.cloned.1.call-done = bf16[640,784]{1,0:T(8,128)(2,1)} async-done(((bf16[5120,784]{1,0:T(8,128)(2,1)}), bf16[640,784]{1,0:T(8,128)(2,1)}) %reduce-scatter.4.cloned.1.call-update) | async-done | bytes 1003536
  236.3 1.9 copy.25
  238.2 1.4 fusion.13
  239.7 0.6 dynamic-slice
  240.9 76.3 %all-gather.7.cloned.1.call-done = bf16[784,5120]{1,0:T(8,128)(2,1)} async-done(((bf16[784,640]{1,0:T(8,128)(2,1)}), bf16[784,5120]{1,0:T(8,128)(2,1)}) %all-gather.7.cloned.1.call-update) | async-done | bytes 8028176 | tf_op jit(solution)/shard_map/all_gather | solution.py:115
  317.2 5.1 %fusion.4 = f32[784]{0:T(1024)S(1)} fusion(bf16[784,5120]{1,0:T(8,128)(2,1)} %all-gather.7.cloned.1.call-done), kind=kLoop, calls=%fused_computation.11 | loop fusion | flops 12041456 | bytes 8031296 | tf_op jit(solution)/shard_map/reduce_sum | solution.py:32
  322.3 0.5 copy-done.1
  322.8 2.9 fusion.33
  325.7 0.3 dynamic-update-slice
  326.3 26.7 %all-reduce.2 = (f32[6272]{0:T(1024)S(1)}, f32[6272]{0:T(1024)S(1)}) all-reduce(f32[6272]{0:T(1024)S(1)} %dynamic-update-slice, f32[6272]{0:T(1024)S(1)} %dynamic-update-slice.1), channel_id=2, replica_groups=mesh['rep'=4,'tp'=8] {'tp'}, use_global_device_ids=true, to_apply=%add | all-reduce | flops 12544 | bytes 100352
  353.2 0.5 while.17
  353.8 0.7 broadcast_subtract_fusion
  (52 shorter events, 1.3 us)
Async XLA Ops:
  7.2 97.8 %copy-start = (bf16[5120,128]{1,0:T(8,128)(2,1)S(1)}, bf16[5120,128]{1,0:T(8,128)(2,1)}, u32[]{:S(2)}) copy-start(bf16[5120,128]{1,0:T(8,128)(2,1)} %param.22) | copy-start | bytes 3932164
  7.2 85.1 %all-gather.5.cloned.1.call-start = ((), (), s32[]{:S(2)}) async-start(), calls=%async_computation.1 | async-start | bytes 9031680 | tf_op jit(solution)/shard_map/all_gather | solution.py:62
  10.4 225.9 %reduce-scatter.4.cloned.1.call-start = ((), (), s32[]{:S(2)}) async-start(), calls=%async_computation.3 | async-start | bytes 10321920
  92.3 5.6 %copy-start.2 = (bf16[784,5120]{1,0:T(8,128)(2,1)S(1)}, bf16[784,5120]{1,0:T(8,128)(2,1)}, u32[]{:S(2)}) copy-start(bf16[784,5120]{1,0:T(8,128)(2,1)} %all-gather.5.cloned.1.call-done) | copy-start | bytes 24084484
  118.9 2.2 slice-start
  118.9 2.5 slice-start.1
  140.5 97.7 %copy-start.3 = (bf16[784,640]{1,0:T(8,128)(2,1)S(1)}, bf16[784,640]{1,0:T(8,128)(2,1)}, u32[]{:S(2)}) copy-start(bf16[784,640]{1,0:T(8,128)(2,1)} %param.15) | copy-start | bytes 3010564
  140.5 97.7 %copy-start.5 = (bf16[640]{0:T(1024)(128)(2,1)S(1)}, bf16[640]{0:T(1024)(128)(2,1)}, u32[]{:S(2)}) copy-start(bf16[640]{0:T(1024)(128)(2,1)} %param.18) | copy-start | bytes 3844
  140.5 99.1 %copy-start.4 = (bf16[5120]{0:T(1024)(128)(2,1)S(1)}, bf16[5120]{0:T(1024)(128)(2,1)}, u32[]{:S(2)}) copy-start(bf16[5120]{0:T(1024)(128)(2,1)} %param.26) | copy-start | bytes 30724
  140.5 99.1 %copy-start.7 = (u32[32]{0:T(128)S(1)}, u32[32]{0:T(128)}, u32[]{:S(2)}) copy-start(u32[32]{0:T(128)} %constant.56) | copy-start | bytes 388
  140.5 176.6 %all-gather.7.cloned.1.call-start = ((), (), s32[]{:S(2)}) async-start(), calls=%async_computation.2 | async-start | bytes 9031680 | tf_op jit(solution)/shard_map/all_gather | solution.py:115
  239.6 82.7 %copy-start.6 = (bf16[5120,64]{0,1:T(8,128)(2,1)S(1)}, bf16[5120,64]{0,1:T(8,128)(2,1)}, u32[]{:S(2)}) copy-start(bf16[5120,64]{0,1:T(8,128)(2,1)} %param.27) | copy-start | bytes 1966084
  317.2 5.6 %copy-start.1 = (bf16[784,5120]{1,0:T(8,128)(2,1)S(1)}, bf16[784,5120]{1,0:T(8,128)(2,1)}, u32[]{:S(2)}) copy-start(bf16[784,5120]{1,0:T(8,128)(2,1)} %all-gather.7.cloned.1.call-done) | copy-start | bytes 24084484
Sparse Core Ops, SparseCore 0:
  10.5 81.7 all-gather.4
  140.7 95.5 reduce-scatter.3
  239.7 77.4 all-gather.6
where the time goes:
time: 362 us; the launch traced here: 361 us
  waiting for transfers between devices  251 us (69%)
  matrix products  29.2 us (8%)
  blocking collectives  26.7 us (7%)
  other arithmetic  20 us (6%)
  local copies, waits for them, and re-layouts  19 us (5%)
  between operations  14.6 us (4%)
    unnamed x4, waiting for transfers between devices  95.7 us
    all_gather x1, waiting for transfers between devices, on_device(): gathered = lax.all_gather(masked_local, 'tp', axis=1, tiled=True)  79.1 us
    all_gather x1, waiting for transfers between devices, on_device(): hidden_full = lax.all_gather(hidden_local, 'tp', axis=1, tiled=True)  76.3 us
    unnamed x1, blocking collectives  26.7 us
    unnamed x27, local copies, waits for them, and re-layouts  18.1 us
    reduce_sum x2, other arithmetic, rms_norm(): inverse = lax.rsqrt(jnp.mean(wide * wide, axis=-1, keepdims=True) + EPS)  10.1 us
  transfers between devices with their start and end apart: 3, of which 3 were waited for; matrix products, arithmetic and copies ran while one was open for 1% of the time, Pallas kernels for 0%

commit v1 on v0

--- a/solution.py
+++ b/solution.py
@@ -1,14 +1,22 @@
+import functools
+
 import jax
 import jax.numpy as jnp
 from jax import lax
+from jax.experimental import pallas as pl
+from jax.experimental.pallas import tpu as pltpu
 from jax.sharding import PartitionSpec as P
 
 KVH = 8
 HS = 128
 L = 196
+CORES = 2
+CHIPS = 4
+EXTRA = 8
 
 
 EPS = 1e-06
+NT = (((1,), (1,)), ((), ()))
 
 
 def swapped(value, axis, apart):
@@ -39,6 +47,218 @@
         second_pair[0] - top
     )
     return (top, total)
+
+
+def between_chips(pairs):
+    return [(CORES * a + c, CORES * b + c) for a, b in pairs for c in range(CORES)]
+
+
+PARTNER = between_chips([(0, 1), (1, 0), (2, 3), (3, 2)])
+MIDDLE = between_chips([(1, 2), (2, 1)])
+OUTWARD = between_chips([(2, 3), (1, 0)])
+INWARD = between_chips([(3, 2), (0, 1)])
+
+
+def permuted(value, pairs):
+    return lax.ppermute(value, "tp", pairs)
+
+
+def gathered_shards(own):
+    partner = permuted(own, PARTNER)
+    middle = permuted(own, MIDDLE)
+    far_middle = permuted(partner, MIDDLE)
+    near = middle + permuted(middle, OUTWARD)
+    far = far_middle + permuted(far_middle, OUTWARD)
+    mine = [own, partner, near, far]
+    return mine + [swapped(shard, "tp", 0) for shard in mine]
+
+
+def attend_kernel(heads, order, length, *refs):
+    shards, (gain, w_q, w_kv, q_bias, v_bias, w_out, keep, send, context) = refs[:8], refs[8:]
+    width = shards[0].shape[1]
+    features = width * 8
+    total = None
+    for shard in shards:
+        wide = shard[...].astype(jnp.float32)
+        part = jnp.sum(wide * wide, axis=1, keepdims=True)
+        total = part if total is None else total + part
+    inverse = lax.rsqrt(total / features + EPS)
+    q_sum = kv_sum = None
+    for k, shard in enumerate(shards):
+        block = order[k]
+        rows = pl.ds(pl.multiple_of(block * width, width), width)
+        scaled = shard[...].astype(jnp.float32) * inverse * gain[pl.ds(block, 1), :]
+        normed = scaled.astype(jnp.bfloat16)
+        q_part = jnp.dot(normed, w_q[rows, :], preferred_element_type=jnp.float32)
+        kv_part = jnp.dot(normed, w_kv[rows, :], preferred_element_type=jnp.float32)
+        q_sum = q_part if q_sum is None else q_sum + q_part
+        kv_sum = kv_part if kv_sum is None else kv_sum + kv_part
+    queries = (q_sum + q_bias[...]).astype(jnp.bfloat16)
+    keys = kv_sum[:, :HS].astype(jnp.bfloat16)
+    values = (kv_sum[:, HS:] + v_bias[...]).astype(jnp.bfloat16)
+    count = keys.shape[0]
+    valid = lax.broadcasted_iota(jnp.int32, (count, count), 1) < length[0]
+    for h in range(heads):
+        scores = lax.dot_general(
+            queries[:, h * HS : (h + 1) * HS], keys, NT, preferred_element_type=jnp.float32
+        ) * HS ** (-0.5)
+        scores = jnp.where(valid, scores, jnp.float32(-1e30))
+        expo = jnp.exp(scores - jnp.max(scores, axis=1, keepdims=True))
+        prob = (expo / jnp.sum(expo, axis=1, keepdims=True)).astype(jnp.bfloat16)
+        context[:, h * HS : (h + 1) * HS] = jnp.dot(
+            prob, values, preferred_element_type=jnp.float32
+        ).astype(jnp.bfloat16)
+    for k in range(8):
+        columns = pl.ds(pl.multiple_of(order[k] * width, width), width)
+        part = jnp.dot(context[...], w_out[:, columns], preferred_element_type=jnp.float32)
+        target = keep if k < 4 else send
+        target[k % 4] = part.astype(jnp.bfloat16)
+
+
+def head_kernel(kept, other, partner, middle, masked, gain, w_rows, hidden, keep, send):
+    wide = lambda ref: ref[...].astype(jnp.float32)
+    summed = (wide(kept) + wide(other)) + (wide(partner) + wide(middle))
+    rounded = (wide(masked) + summed).astype(jnp.bfloat16)
+    hidden[...] = rounded
+    value = rounded.astype(jnp.float32)
+    scaled = (value * gain[...]).astype(jnp.bfloat16)
+    logits = lax.dot_general(w_rows[...], scaled, NT, preferred_element_type=jnp.float32)
+    ones = jnp.ones((EXTRA, value.shape[1]), jnp.float32)
+    squares = lax.dot_general(
+        ones, value * value, NT, preferred_element_type=jnp.float32, precision=lax.Precision.HIGHEST
+    )
+    entries = w_rows.shape[0] // 8
+    for place, k in enumerate((0, 4, 2, 6)):
+        for target, block in ((keep, k), (send, k + 1)):
+            target[place, 0:entries] = logits[block * entries : (block + 1) * entries]
+            target[place, entries : entries + EXTRA] = squares
+
+
+def whole(space=pltpu.VMEM):
+    return pl.BlockSpec(memory_space=space)
+
+
+def exchanged_head(w_head, index):
+    turned = w_head.T
+    entries = turned.shape[0]
+    width = turned.shape[1] // 8
+    parts = lax.axis_size("rep")
+    if entries % (16 * parts) == 0:
+        share = entries // parts
+        turned = lax.dynamic_slice_in_dim(turned, lax.axis_index("rep") * share, share, axis=0)
+    else:
+        parts, share = 1, entries
+    blocks = [
+        lax.dynamic_slice_in_dim(turned, jnp.bitwise_xor(index, k) * width, width, axis=1)
+        for k in range(8)
+    ]
+    blocks = jnp.stack(blocks)
+    for level in range(3):
+        bit = 1 << level
+        stay = [k for k in range(8) if not k & bit]
+        move = [k for k in range(8) if k & bit]
+        got = swapped(jnp.stack([blocks[k] for k in move]), "tp", level)
+        merged = [None] * 8
+        for place, k in enumerate(stay):
+            merged[k] = blocks[k]
+        for place, k in enumerate(move):
+            merged[k] = got[place]
+        blocks = jnp.stack(merged)
+    if parts > 1:
+        blocks = lax.all_gather(blocks, "rep", axis=1, tiled=True)
+    return blocks.reshape(8 * entries, width)
+
+
+def on_line(
+    embeds,
+    remask,
+    lengths,
+    mask_vec,
+    attn_gain,
+    w_query,
+    q_bias,
+    w_key,
+    w_value,
+    v_bias,
+    w_out,
+    head_gain,
+    w_head,
+):
+    requests = lengths.shape[0]
+    width = embeds.shape[1]
+    heads = w_query.shape[1] // HS
+    entries = w_head.shape[1]
+    index = lax.axis_index("tp")
+    chip, core = index // CORES, index % CORES
+    first_half = chip < 2
+    line = jnp.stack(
+        [chip, jnp.bitwise_xor(chip, 1), jnp.where(first_half, 2, 1), jnp.where(first_half, 3, 0)]
+    )
+    order = jnp.concatenate([line * CORES + core, line * CORES + (1 - core)]).astype(jnp.int32)
+    w_kv = jnp.concatenate([w_key, w_value], axis=1)
+    gain = attn_gain.astype(jnp.float32).reshape(8, width)
+    q_row = q_bias.astype(jnp.float32)[None, :]
+    v_row = v_bias.astype(jnp.float32)[None, :]
+    gain_local = lax.dynamic_slice_in_dim(head_gain, index * width, width).astype(jnp.float32)[None, :]
+    w_rows = exchanged_head(w_head, index)
+
+    attend = pl.pallas_call(
+        functools.partial(attend_kernel, heads),
+        out_shape=[jax.ShapeDtypeStruct((4, L, width), jnp.bfloat16)] * 2,
+        in_specs=[whole(pltpu.SMEM)] * 2 + [whole()] * 14,
+        out_specs=[whole()] * 2,
+        scratch_shapes=[pltpu.VMEM((L, heads * HS), jnp.bfloat16)],
+        compiler_params=pltpu.CompilerParams(vmem_limit_bytes=40 * 2**20),
+        cost_estimate=pl.CostEstimate(
+            flops=2 * L * width * 8 * (heads * HS * 2 + 2 * HS), bytes_accessed=16 * 2**20, transcendentals=heads * L * L
+        ),
+    )
+    head = pl.pallas_call(
+        head_kernel,
+        out_shape=[
+            jax.ShapeDtypeStruct((L, width), jnp.bfloat16),
+            jax.ShapeDtypeStruct((4, entries + EXTRA, L), jnp.float32),
+            jax.ShapeDtypeStruct((4, entries + EXTRA, L), jnp.float32),
+        ],
+        in_specs=[whole()] * 7,
+        out_specs=[whole()] * 3,
+        compiler_params=pltpu.CompilerParams(vmem_limit_bytes=16 * 2**20),
+        cost_estimate=pl.CostEstimate(
+            flops=2 * L * width * 8 * entries, bytes_accessed=3 * 2**20, transcendentals=0
+        ),
+    )
+
+    add = lambda *terms: sum(term.astype(jnp.float32) for term in terms).astype(jnp.bfloat16)
+    hiddens, logits_all, pairs_all = [], [], []
+    for r in range(requests):
+        rows = slice(r * L, (r + 1) * L)
+        masked = jnp.where(remask[rows, None] == 1, mask_vec[None, :], embeds[rows])
+        shards = gathered_shards(masked)
+        keep, send = attend(order, lengths[r : r + 1], *shards, gain, w_query, w_kv, q_row, v_row, w_out)
+        other = swapped(send, "tp", 0)
+        far = add(keep[3], other[3])
+        near = add(keep[2], other[2])
+        far_in = permuted(far, INWARD)
+        near_in = permuted(near, INWARD)
+        far_middle = permuted(add(far, far_in), MIDDLE)
+        near_middle = permuted(add(near, near_in), MIDDLE)
+        partner = permuted(add(keep[1], other[1], far_middle), PARTNER)
+        hidden, kept, sent = head(keep[0], other[0], partner, near_middle, masked, gain_local, w_rows)
+        hiddens.append(hidden)
+        held = kept + swapped(sent, "tp", 0)
+        held = held[:2] + swapped(held[2:], "tp", 1)
+        held = held[0] + swapped(held[1], "tp", 2)
+        inverse = lax.rsqrt(held[entries] / (8 * width) + EPS)
+        logits = held[:entries] * inverse[None, :]
+        top = jnp.max(logits, axis=0)
+        logits_all.append(logits)
+        pairs_all.append(jnp.stack([top, jnp.sum(jnp.exp(logits - top[None, :]), axis=0)]))
+    pair = jnp.concatenate(pairs_all, axis=1)
+    for level in range(3):
+        pair = jnp.stack(combine_pair(pair, swapped(pair, "tp", level)))
+    log_total = pair[0] + jnp.log(pair[1])
+    logits = jnp.concatenate(logits_all, axis=1)
+    return (jnp.concatenate(hiddens, axis=0), (logits - log_total[None, :]).T)
 
 
 def on_device(
@@ -138,8 +358,9 @@
         P(),
         P(None, "tp"),
     )
+    on_line_fits = mesh.shape["tp"] == CORES * CHIPS and mesh.shape["tp"] == KVH
     return jax.shard_map(
-        on_device,
+        on_line if on_line_fits else on_device,
         mesh=mesh,
         in_specs=placed,
         out_specs=(P("rep", "tp"), P("rep", "tp")),

time: 362 us -> 291 us (0.80); the launches traced: 361 us -> 286 us
  waiting for transfers between devices: 251 us -> 92.6 us
  starting transfers between devices: 0.12 us -> 95.8 us
  Pallas kernels: 0 us -> 44.9 us
  matrix products: 29.2 us -> 0 us
  blocking collectives: 26.7 us -> 12.8 us
  between operations: 14.6 us -> 2.37 us
    all_gather x2 -> x0, waiting for transfers between devices: 155 us -> none  [the longest x1 79.1 us: on_device(): gathered = lax.all_gather(masked_local, 'tp', axis=1, tiled=True)]
    ppermute x0 -> x78, starting transfers between devices: none -> 95.8 us  [the longest x40 71.9 us: permuted(): return lax.ppermute(value, 'tp', pairs)]
    unnamed x4 -> x0, waiting for transfers between devices: 95.7 us -> none
    ppermute x0 -> x78, waiting for transfers between devices: none -> 92.6 us  [the longest x40 59.9 us: permuted(): return lax.ppermute(value, 'tp', pairs)]
    pallas_call x0 -> x8, Pallas kernels: none -> 44.9 us  [the longest x4 41.5 us: on_line(): attend(order, lengths[r:r + 1], *shards, gain, w_query, w_kv, q_row, v_ro...]
    dot_general x7 -> x0, matrix products: 29.2 us -> none  [the longest x1 6.88 us: on_device(): jnp.dot(normed, w_query, preferred_element_type=jnp.float32)]
    unnamed x1 -> x0, blocking collectives: 26.7 us -> none
    unnamed x27 -> x51, local copies, waits for them, and re-layouts: 18.1 us -> 5.03 us
  transfers between devices with their start and end apart: 3 -> 78, of which waited for: 3 -> 26; matrix products, arithmetic and copies ran while one was open for 1% -> 11% of each run, Pallas kernels for 0% -> 16%
where the time goes in v1:
time: 291 us; the launch traced here: 286 us
  starting transfers between devices  95.8 us (33%)
  waiting for transfers between devices  92.6 us (32%)
  Pallas kernels  44.9 us (15%)
  other arithmetic  19.3 us (7%)
  local copies, waits for them, and re-layouts  18 us (6%)
  blocking collectives  12.8 us (4%)
    ppermute x40, starting transfers between devices, permuted(): return lax.ppermute(value, 'tp', pairs)  71.9 us
    ppermute x40, waiting for transfers between devices, permuted(): return lax.ppermute(value, 'tp', pairs)  59.9 us
    pallas_call x4, Pallas kernels, on_line(): attend(order, lengths[r:r + 1], *shards, gain, w_query, w_kv, q_row, v_ro...  41.5 us
    ppermute x38, waiting for transfers between devices, swapped(): return lax.ppermute(value, axis, pairs)  32.7 us
    ppermute x38, starting transfers between devices, swapped(): return lax.ppermute(value, axis, pairs)  23.9 us
    all_gather x1, blocking collectives, exchanged_head(): blocks = lax.all_gather(blocks, 'rep', axis=1, tiled=True)  12.8 us
    slice x4, local copies, waits for them, and re-layouts, on_line(): near = add(keep[2], other[2])  6.21 us
  transfers between devices with their start and end apart: 78, of which 26 were waited for; matrix products, arithmetic and copies ran while one was open for 11% of the time, Pallas kernels for 16%

profile of v1, /device:TPU:0, one launch (start us, length us, event | category | flops | bytes accessed | tf_op | source)
XLA Modules:
  0.0 285.9 jit_solution(4307891167614738239)
XLA Ops:
  3.4 3.0 %collective-permute-start.16 = (bf16[4,16,640]{2,1,0:T(8,128)(2,1)S(1)}, bf16[4,16,640]{2,1,0:T(8,128)(2,1)S(1)}, u32[]{:S(2)}, u32[]{:S(2)}) collective-permute-start(bf16[4,16,640]{2,1,0:T(8,128)(2,1)S(1)} %pad_maximum_fusion.3), channel_id=1, source_target_pairs={{0,2},{1,3},{2,0},{3,1},{4,6},{5,7},{6,4},{7,5},{8,10},{9,11},{10,... | collective-permute-start | bytes 245768 | tf_op jit(solution)/shard_map/ppermute | solution.py:25
  9.5 4.1 %collective-permute-start.17 = (bf16[4,16,640]{2,1,0:T(8,128)(2,1)S(1)}, bf16[4,16,640]{2,1,0:T(8,128)(2,1)}, u32[]{:S(2)}, u32[]{:S(2)}) collective-permute-start(bf16[4,16,640]{2,1,0:T(8,128)(2,1)S(1)} %pad_maximum_fusion.4), channel_id=1, source_target_pairs={{0,4},{1,5},{2,6},{3,7},{4,0},{5,1},{6,2},{7,3},{8,12},{9,13},{10,... | collective-permute-start | bytes 245768 | tf_op jit(solution)/shard_map/ppermute | solution.py:25
  14.1 8.7 %collective-permute-done.17 = bf16[4,16,640]{2,1,0:T(8,128)(2,1)} collective-permute-done((bf16[4,16,640]{2,1,0:T(8,128)(2,1)S(1)}, bf16[4,16,640]{2,1,0:T(8,128)(2,1)}, u32[]{:S(2)}, u32[]{:S(2)}) %collective-permute-start.17) | collective-permute-done | bytes 81952 | tf_op jit(solution)/shard_map/ppermute | solution.py:25
  27.1 3.7 %collective-permute-start.48 = (bf16[196,640]{1,0:T(8,128)(2,1)S(1)}, bf16[196,640]{1,0:T(8,128)(2,1)}, u32[]{:S(2)}, u32[]{:S(2)}) collective-permute-start(bf16[196,640]{1,0:T(8,128)(2,1)S(1)} %get-tuple-element.66.refs_0_.masked), channel_id=1, source_target_pairs={{0,2},{1,3},{2,0},{3,1},{4,6},{5,7},{6,4},{7,5},{8,10},{9,11},{10,... | collective-permute-start | bytes 752648 | tf_op jit(solution)/shard_map/ppermute | solution.py:63
  36.0 2.4 collective-permute-done.48.refs_1_
  55.0 19.8 %collective-permute-done.4 = bf16[196,640]{1,0:T(8,128)(2,1)S(1)} collective-permute-done((bf16[196,640]{1,0:T(8,128)(2,1)}, bf16[196,640]{1,0:T(8,128)(2,1)S(1)}, u32[]{:S(2)}, u32[]{:S(2)}) %collective-permute-start.4) | collective-permute-done | bytes 250912 | tf_op jit(solution)/shard_map/ppermute | solution.py:63
  82.8 2.9 %collective-permute-done.37 = bf16[196,640]{1,0:T(8,128)(2,1)S(1)} collective-permute-done((bf16[196,640]{1,0:T(8,128)(2,1)}, bf16[196,640]{1,0:T(8,128)(2,1)S(1)}, u32[]{:S(2)}, u32[]{:S(2)}) %collective-permute-start.37) | collective-permute-done | bytes 250912 | tf_op jit(solution)/shard_map/ppermute | solution.py:63
  88.8 12.8 %all_gather.3 = bf16[8,64,640]{2,1,0:T(8,128)(2,1)S(1)} all-gather(bf16[8,16,640]{2,1,0:T(8,128)(2,1)S(1)} %pad_maximum_fusion.1), channel_id=1, replica_groups=mesh['rep'=4,'tp'=8] {'rep'}, dimensions={1}, use_global_device_ids=true | all-gather | bytes 819200 | tf_op jit(solution)/shard_map/all_gather | solution.py:168
  106.9 2.5 copy-done
  109.4 10.6 %shard_map.140 = (bf16[4,196,640]{2,1,0:T(8,128)(2,1)S(1)}, bf16[4,196,640]{2,1,0:T(8,128)(2,1)S(1)}) custom-call(s32[8]{0:T(128)S(1)} %pad_add_fusion.order, s32[1]{0:T(128)} %get-tuple-element.102.length, bf16[196,640]{1,0:T(8,128)(2,1)S(1)} %copy-done.2, bf16[196,640]{1,0:T(8,128)(2,1)} %collective-permute-done.refs_1_, bf16[196,640]{1,0:T(8,128)(2,1)} %add.253.refs_2_, ...), custom_call_target="tpu_custom_call" | custom-call | flops 2569011200 | bytes 16777216 | tf_op jit(solution)/shard_map/pallas_call | solution.py:237
  121.4 10.4 %shard_map.142 = (bf16[4,196,640]{2,1,0:T(8,128)(2,1)S(1)}, bf16[4,196,640]{2,1,0:T(8,128)(2,1)S(1)}) custom-call(s32[8]{0:T(128)S(1)} %pad_add_fusion.order, s32[1]{0:T(128)} %get-tuple-element.103.length, bf16[196,640]{1,0:T(8,128)(2,1)S(1)} %get-tuple-element.65.refs_0_.masked, bf16[196,640]{1,0:T(8,128)(2,1)} %collective-permute-done.18.refs_1_, ...), custom_call_target="tpu_custom_call" | custom-call | flops 2569011200 | bytes 16777216 | tf_op jit(solution)/shard_map/pallas_call | solution.py:237
  133.0 10.6 %shard_map.144 = (bf16[4,196,640]{2,1,0:T(8,128)(2,1)S(1)}, bf16[4,196,640]{2,1,0:T(8,128)(2,1)S(1)}) custom-call(s32[8]{0:T(128)S(1)} %pad_add_fusion.order, s32[1]{0:T(128)} %get-tuple-element.105.length, bf16[196,640]{1,0:T(8,128)(2,1)S(1)} %get-tuple-element.67.refs_0_.masked, bf16[196,640]{1,0:T(8,128)(2,1)S(1)} %copy-done.4, ...), custom_call_target="tpu_custom_call" | custom-call | flops 2569011200 | bytes 16777216 | tf_op jit(solution)/shard_map/pallas_call | solution.py:237
  146.9 10.0 %shard_map.146 = (bf16[4,196,640]{2,1,0:T(8,128)(2,1)S(1)}, bf16[4,196,640]{2,1,0:T(8,128)(2,1)S(1)}) custom-call(s32[8]{0:T(128)S(1)} %pad_add_fusion.order, s32[1]{0:T(128)} %get-tuple-element.104.length, bf16[196,640]{1,0:T(8,128)(2,1)S(1)} %get-tuple-element.66.refs_0_.masked, bf16[196,640]{1,0:T(8,128)(2,1)} %collective-permute-done.48.refs_1_, ...), custom_call_target="tpu_custom_call" | custom-call | flops 2569011200 | bytes 16777216 | tf_op jit(solution)/shard_map/pallas_call | solution.py:237
  159.7 2.4 collective-permute-start.13
  174.1 4.4 %collective-permute-start.61 = (bf16[196,640]{1,0:T(8,128)(2,1)S(1)}, bf16[196,640]{1,0:T(8,128)(2,1)S(1)}, u32[]{:S(2)}, u32[]{:S(2)}) collective-permute-start(bf16[196,640]{1,0:T(8,128)(2,1)S(1)} %get-tuple-element.62), channel_id=1, source_target_pairs={{6,4},{7,5},{0,2},{1,3},{14,12},{15,13},{8,10},{9,11},{22,20},{23,... | collective-permute-start | bytes 752648 | tf_op jit(solution)/shard_map/ppermute | solution.py:63
  179.5 4.4 %collective-permute-start.58 = (bf16[196,640]{1,0:T(8,128)(2,1)S(1)}, bf16[196,640]{1,0:T(8,128)(2,1)S(1)}, u32[]{:S(2)}, u32[]{:S(2)}) collective-permute-start(bf16[196,640]{1,0:T(8,128)(2,1)S(1)} %get-tuple-element.63), channel_id=1, source_target_pairs={{6,4},{7,5},{0,2},{1,3},{14,12},{15,13},{8,10},{9,11},{22,20},{23,... | collective-permute-start | bytes 752648 | tf_op jit(solution)/shard_map/ppermute | solution.py:63
  185.8 4.7 %collective-permute-done.46 = bf16[196,640]{1,0:T(8,128)(2,1)S(1)} collective-permute-done((bf16[196,640]{1,0:T(8,128)(2,1)S(1)}, bf16[196,640]{1,0:T(8,128)(2,1)S(1)}, u32[]{:S(2)}, u32[]{:S(2)}) %collective-permute-start.46) | collective-permute-done | bytes 250912 | tf_op jit(solution)/shard_map/ppermute | solution.py:63
  191.3 4.7 %collective-permute-done.43 = bf16[196,640]{1,0:T(8,128)(2,1)S(1)} collective-permute-done((bf16[196,640]{1,0:T(8,128)(2,1)S(1)}, bf16[196,640]{1,0:T(8,128)(2,1)S(1)}, u32[]{:S(2)}, u32[]{:S(2)}) %collective-permute-start.43) | collective-permute-done | bytes 250912 | tf_op jit(solution)/shard_map/ppermute | solution.py:63
  196.8 4.7 %collective-permute-done.61 = bf16[196,640]{1,0:T(8,128)(2,1)S(1)} collective-permute-done((bf16[196,640]{1,0:T(8,128)(2,1)S(1)}, bf16[196,640]{1,0:T(8,128)(2,1)S(1)}, u32[]{:S(2)}, u32[]{:S(2)}) %collective-permute-start.61) | collective-permute-done | bytes 250912 | tf_op jit(solution)/shard_map/ppermute | solution.py:63
  202.2 4.0 %collective-permute-done.58 = bf16[196,640]{1,0:T(8,128)(2,1)S(1)} collective-permute-done((bf16[196,640]{1,0:T(8,128)(2,1)S(1)}, bf16[196,640]{1,0:T(8,128)(2,1)S(1)}, u32[]{:S(2)}, u32[]{:S(2)}) %collective-permute-start.58) | collective-permute-done | bytes 250912 | tf_op jit(solution)/shard_map/ppermute | solution.py:63
  208.5 16.6 %collective-permute-start.12 = (bf16[196,640]{1,0:T(8,128)(2,1)S(1)}, bf16[196,640]{1,0:T(8,128)(2,1)S(1)}, u32[]{:S(2)}, u32[]{:S(2)}) collective-permute-start(bf16[196,640]{1,0:T(8,128)(2,1)S(1)} %fusion.3), channel_id=1, source_target_pairs={{0,2},{1,3},{2,0},{3,1},{4,6},{5,7},{6,4},{7,5},{8,10},{9,11},{10,... | collective-permute-start | bytes 752648 | tf_op jit(solution)/shard_map/ppermute | solution.py:63
  225.3 3.7 %collective-permute-start.30 = (bf16[196,640]{1,0:T(8,128)(2,1)S(1)}, bf16[196,640]{1,0:T(8,128)(2,1)S(1)}, u32[]{:S(2)}, u32[]{:S(2)}) collective-permute-start(bf16[196,640]{1,0:T(8,128)(2,1)S(1)} %fusion.2), channel_id=1, source_target_pairs={{0,2},{1,3},{2,0},{3,1},{4,6},{5,7},{6,4},{7,5},{8,10},{9,11},{10,... | collective-permute-start | bytes 752648 | tf_op jit(solution)/shard_map/ppermute | solution.py:63
  230.6 2.3 collective-permute-start.45
  237.8 3.8 %collective-permute-done.45.partner = bf16[196,640]{1,0:T(8,128)(2,1)S(1)} collective-permute-done((bf16[196,640]{1,0:T(8,128)(2,1)S(1)}, bf16[196,640]{1,0:T(8,128)(2,1)S(1)}, u32[]{:S(2)}, u32[]{:S(2)}) %collective-permute-start.45) | collective-permute-done | bytes 250912 | tf_op jit(solution)/shard_map/ppermute | solution.py:63
  242.5 3.4 %collective-permute-done.60.partner = bf16[196,640]{1,0:T(8,128)(2,1)S(1)} collective-permute-done((bf16[196,640]{1,0:T(8,128)(2,1)S(1)}, bf16[196,640]{1,0:T(8,128)(2,1)S(1)}, u32[]{:S(2)}, u32[]{:S(2)}) %collective-permute-start.60) | collective-permute-done | bytes 250912 | tf_op jit(solution)/shard_map/ppermute | solution.py:63
  253.7 3.0 %collective-permute-start.65 = (f32[72,196]{1,0:T(8,128)S(1)}, f32[72,196]{1,0:T(8,128)S(1)}, u32[]{:S(2)}, u32[]{:S(2)}) collective-permute-start(f32[72,196]{1,0:T(8,128)S(1)} %slice_bitcast_fusion.10), channel_id=1, source_target_pairs={{0,4},{1,5},{2,6},{3,7},{4,0},{5,1},{6,2},{7,3},{8,12},{9,13},{10,... | collective-permute-start | bytes 169352 | tf_op jit(solution)/shard_map/ppermute | solution.py:25
  256.9 3.0 %collective-permute-start.68 = (f32[72,196]{1,0:T(8,128)S(1)}, f32[72,196]{1,0:T(8,128)S(1)}, u32[]{:S(2)}, u32[]{:S(2)}) collective-permute-start(f32[72,196]{1,0:T(8,128)S(1)} %slice_bitcast_fusion.8), channel_id=1, source_target_pairs={{0,4},{1,5},{2,6},{3,7},{4,0},{5,1},{6,2},{7,3},{8,12},{9,13},{10,... | collective-permute-start | bytes 169352 | tf_op jit(solution)/shard_map/ppermute | solution.py:25
  259.9 3.3 %collective-permute-done.70 = f32[2,72,196]{2,1,0:T(8,128)S(1)} collective-permute-done((f32[2,72,196]{2,1,0:T(8,128)S(1)}, f32[2,72,196]{2,1,0:T(8,128)S(1)}, u32[]{:S(2)}, u32[]{:S(2)}) %collective-permute-start.70) | collective-permute-done | bytes 112928 | tf_op jit(solution)/shard_map/ppermute | solution.py:25
  263.8 2.4 collective-permute-done.73
  266.9 6.2 %collective-permute-done.71 = f32[72,196]{1,0:T(8,128)S(1)} collective-permute-done((f32[72,196]{1,0:T(8,128)S(1)}, f32[72,196]{1,0:T(8,128)S(1)}, u32[]{:S(2)}, u32[]{:S(2)}) %collective-permute-start.71) | collective-permute-done | bytes 56480 | tf_op jit(solution)/shard_map/ppermute | solution.py:25
  276.3 3.6 %collective-permute-done.76 = f32[2,784]{1,0:T(2,128)S(1)} collective-permute-done((f32[2,784]{1,0:T(2,128)S(1)}, f32[2,784]{1,0:T(2,128)S(1)}, u32[]{:S(2)}, u32[]{:S(2)}) %collective-permute-start.76) | collective-permute-done | bytes 6304 | tf_op jit(solution)/shard_map/ppermute | solution.py:25
  281.1 3.4 %collective-permute-done.77 = f32[2,784]{1,0:T(2,128)S(1)} collective-permute-done((f32[2,784]{1,0:T(2,128)S(1)}, f32[2,784]{1,0:T(2,128)S(1)}, u32[]{:S(2)}, u32[]{:S(2)}) %collective-permute-start.77) | collective-permute-done | bytes 6304 | tf_op jit(solution)/shard_map/ppermute | solution.py:25
  (280 shorter events, 98.1 us)
Async XLA Ops:
  8.0 16.2 %collective-permute-start = (bf16[196,640]{1,0:T(8,128)(2,1)S(1)}, bf16[196,640]{1,0:T(8,128)(2,1)}, u32[]{:S(2)}, u32[]{:S(2)}) collective-permute-start(bf16[196,640]{1,0:T(8,128)(2,1)S(1)} %get-tuple-element.64.refs_0_.masked), channel_id=1, source_target_pairs={{0,2},{1,3},{2,0},{3,1},{4,6},{5,7},{6,4},{7,5},{8,10},{9,11},{10,... | collective-permute-start | bytes 752648 | tf_op jit(solution)/shard_map/ppermute | solution.py:63
  8.1 16.1 %collective-permute-start.1 = (bf16[196,640]{1,0:T(8,128)(2,1)S(1)}, bf16[196,640]{1,0:T(8,128)(2,1)}, u32[]{:S(2)}, u32[]{:S(2)}) collective-permute-start(bf16[196,640]{1,0:T(8,128)(2,1)S(1)} %get-tuple-element.64.refs_0_.masked), channel_id=1, source_target_pairs={{2,4},{3,5},{4,2},{5,3},{10,12},{11,13},{12,10},{13,11},{18,20},{1... | collective-permute-start | bytes 752648 | tf_op jit(solution)/shard_map/ppermute | solution.py:63
  46.1 36.0 %collective-permute-start.35 = (bf16[196,640]{1,0:T(8,128)(2,1)}, bf16[196,640]{1,0:T(8,128)(2,1)S(1)}, u32[]{:S(2)}, u32[]{:S(2)}) collective-permute-start(bf16[196,640]{1,0:T(8,128)(2,1)} %collective-permute-done.34), channel_id=1, source_target_pairs={{4,6},{5,7},{2,0},{3,1},{12,14},{13,15},{10,8},{11,9},{20,22},{21,... | collective-permute-start | bytes 752648 | tf_op jit(solution)/shard_map/ppermute | solution.py:63
  47.4 34.7 %collective-permute-start.50 = (bf16[196,640]{1,0:T(8,128)(2,1)}, bf16[196,640]{1,0:T(8,128)(2,1)S(1)}, u32[]{:S(2)}, u32[]{:S(2)}) collective-permute-start(bf16[196,640]{1,0:T(8,128)(2,1)} %collective-permute-done.49), channel_id=1, source_target_pairs={{4,6},{5,7},{2,0},{3,1},{12,14},{13,15},{10,8},{11,9},{20,22},{21,... | collective-permute-start | bytes 752648 | tf_op jit(solution)/shard_map/ppermute | solution.py:63
  50.4 24.3 %collective-permute-start.4 = (bf16[196,640]{1,0:T(8,128)(2,1)}, bf16[196,640]{1,0:T(8,128)(2,1)S(1)}, u32[]{:S(2)}, u32[]{:S(2)}) collective-permute-start(bf16[196,640]{1,0:T(8,128)(2,1)} %collective-permute-done.3), channel_id=1, source_target_pairs={{4,6},{5,7},{2,0},{3,1},{12,14},{13,15},{10,8},{11,9},{20,22},{21,... | collective-permute-start | bytes 752648 | tf_op jit(solution)/shard_map/ppermute | solution.py:63
  51.7 31.0 %collective-permute-start.22 = (bf16[196,640]{1,0:T(8,128)(2,1)}, bf16[196,640]{1,0:T(8,128)(2,1)}, u32[]{:S(2)}, u32[]{:S(2)}) collective-permute-start(bf16[196,640]{1,0:T(8,128)(2,1)} %collective-permute-done.21), channel_id=1, source_target_pairs={{4,6},{5,7},{2,0},{3,1},{12,14},{13,15},{10,8},{11,9},{20,22},{21,... | collective-permute-start | bytes 752648 | tf_op jit(solution)/shard_map/ppermute | solution.py:63
  53.0 32.7 %collective-permute-start.37 = (bf16[196,640]{1,0:T(8,128)(2,1)}, bf16[196,640]{1,0:T(8,128)(2,1)S(1)}, u32[]{:S(2)}, u32[]{:S(2)}) collective-permute-start(bf16[196,640]{1,0:T(8,128)(2,1)} %collective-permute-done.36), channel_id=1, source_target_pairs={{4,6},{5,7},{2,0},{3,1},{12,14},{13,15},{10,8},{11,9},{20,22},{21,... | collective-permute-start | bytes 752648 | tf_op jit(solution)/shard_map/ppermute | solution.py:63
  82.2 23.7 %collective-permute-start.24 = (bf16[196,640]{1,0:T(8,128)(2,1)}, bf16[196,640]{1,0:T(8,128)(2,1)}, u32[]{:S(2)}, u32[]{:S(2)}) collective-permute-start(bf16[196,640]{1,0:T(8,128)(2,1)} %collective-permute-done.18.refs_1_), channel_id=1, source_target_pairs={{0,1},{1,0},{2,3},{3,2},{4,5},{5,4},{6,7},{7,6},{8,9},{9,8},{10,11... | collective-permute-start | bytes 752648 | tf_op jit(solution)/shard_map/ppermute | solution.py:25
  82.2 23.7 %collective-permute-start.7 = (bf16[196,640]{1,0:T(8,128)(2,1)}, bf16[196,640]{1,0:T(8,128)(2,1)}, u32[]{:S(2)}, u32[]{:S(2)}) collective-permute-start(bf16[196,640]{1,0:T(8,128)(2,1)} %add.253.refs_2_), channel_id=1, source_target_pairs={{0,1},{1,0},{2,3},{3,2},{4,5},{5,4},{6,7},{7,6},{8,9},{9,8},{10,11... | collective-permute-start | bytes 752648 | tf_op jit(solution)/shard_map/ppermute | solution.py:25
  82.7 23.7 %collective-permute-start.25 = (bf16[196,640]{1,0:T(8,128)(2,1)}, bf16[196,640]{1,0:T(8,128)(2,1)}, u32[]{:S(2)}, u32[]{:S(2)}) collective-permute-start(bf16[196,640]{1,0:T(8,128)(2,1)} %add.271.refs_2_), channel_id=1, source_target_pairs={{0,1},{1,0},{2,3},{3,2},{4,5},{5,4},{6,7},{7,6},{8,9},{9,8},{10,11... | collective-permute-start | bytes 752648 | tf_op jit(solution)/shard_map/ppermute | solution.py:25
  85.7 20.9 %collective-permute-start.8 = (bf16[196,640]{1,0:T(8,128)(2,1)}, bf16[196,640]{1,0:T(8,128)(2,1)}, u32[]{:S(2)}, u32[]{:S(2)}) collective-permute-start(bf16[196,640]{1,0:T(8,128)(2,1)} %add.254.refs_3_), channel_id=1, source_target_pairs={{0,1},{1,0},{2,3},{3,2},{4,5},{5,4},{6,7},{7,6},{8,9},{9,8},{10,11... | collective-permute-start | bytes 752648 | tf_op jit(solution)/shard_map/ppermute | solution.py:25
  88.7 32.6 %collective-permute-start.26 = (bf16[196,640]{1,0:T(8,128)(2,1)S(1)}, bf16[196,640]{1,0:T(8,128)(2,1)S(1)}, u32[]{:S(2)}, u32[]{:S(2)}) collective-permute-start(bf16[196,640]{1,0:T(8,128)(2,1)S(1)} %add.272.refs_3_), channel_id=1, source_target_pairs={{0,1},{1,0},{2,3},{3,2},{4,5},{5,4},{6,7},{7,6},{8,9},{9,8},{10,11... | collective-permute-start | bytes 752648 | tf_op jit(solution)/shard_map/ppermute | solution.py:25
  105.8 26.0 %collective-permute-start.38 = (bf16[196,640]{1,0:T(8,128)(2,1)S(1)}, bf16[196,640]{1,0:T(8,128)(2,1)S(1)}, u32[]{:S(2)}, u32[]{:S(2)}) collective-permute-start(bf16[196,640]{1,0:T(8,128)(2,1)S(1)} %get-tuple-element.67.refs_0_.masked), channel_id=1, source_target_pairs={{0,1},{1,0},{2,3},{3,2},{4,5},{5,4},{6,7},{7,6},{8,9},{9,8},{10,11... | collective-permute-start | bytes 752648 | tf_op jit(solution)/shard_map/ppermute | solution.py:25
  105.9 26.4 %collective-permute-start.39 = (bf16[196,640]{1,0:T(8,128)(2,1)S(1)}, bf16[196,640]{1,0:T(8,128)(2,1)S(1)}, u32[]{:S(2)}, u32[]{:S(2)}) collective-permute-start(bf16[196,640]{1,0:T(8,128)(2,1)S(1)} %copy-done.4), channel_id=1, source_target_pairs={{0,1},{1,0},{2,3},{3,2},{4,5},{5,4},{6,7},{7,6},{8,9},{9,8},{10,11... | collective-permute-start | bytes 752648 | tf_op jit(solution)/shard_map/ppermute | solution.py:25
  106.4 26.0 %collective-permute-start.40 = (bf16[196,640]{1,0:T(8,128)(2,1)S(1)}, bf16[196,640]{1,0:T(8,128)(2,1)S(1)}, u32[]{:S(2)}, u32[]{:S(2)}) collective-permute-start(bf16[196,640]{1,0:T(8,128)(2,1)S(1)} %add.280.refs_2_), channel_id=1, source_target_pairs={{0,1},{1,0},{2,3},{3,2},{4,5},{5,4},{6,7},{7,6},{8,9},{9,8},{10,11... | collective-permute-start | bytes 752648 | tf_op jit(solution)/shard_map/ppermute | solution.py:25
  106.5 26.3 %collective-permute-start.41 = (bf16[196,640]{1,0:T(8,128)(2,1)S(1)}, bf16[196,640]{1,0:T(8,128)(2,1)S(1)}, u32[]{:S(2)}, u32[]{:S(2)}) collective-permute-start(bf16[196,640]{1,0:T(8,128)(2,1)S(1)} %add.281.refs_3_), channel_id=1, source_target_pairs={{0,1},{1,0},{2,3},{3,2},{4,5},{5,4},{6,7},{7,6},{8,9},{9,8},{10,11... | collective-permute-start | bytes 752648 | tf_op jit(solution)/shard_map/ppermute | solution.py:25
  121.4 24.9 %collective-permute-start.53 = (bf16[196,640]{1,0:T(8,128)(2,1)S(1)}, bf16[196,640]{1,0:T(8,128)(2,1)S(1)}, u32[]{:S(2)}, u32[]{:S(2)}) collective-permute-start(bf16[196,640]{1,0:T(8,128)(2,1)S(1)} %get-tuple-element.66.refs_0_.masked), channel_id=1, source_target_pairs={{0,1},{1,0},{2,3},{3,2},{4,5},{5,4},{6,7},{7,6},{8,9},{9,8},{10,11... | collective-permute-start | bytes 752648 | tf_op jit(solution)/shard_map/ppermute | solution.py:25
  131.8 14.9 %collective-permute-start.54 = (bf16[196,640]{1,0:T(8,128)(2,1)}, bf16[196,640]{1,0:T(8,128)(2,1)S(1)}, u32[]{:S(2)}, u32[]{:S(2)}) collective-permute-start(bf16[196,640]{1,0:T(8,128)(2,1)} %collective-permute-done.48.refs_1_), channel_id=1, source_target_pairs={{0,1},{1,0},{2,3},{3,2},{4,5},{5,4},{6,7},{7,6},{8,9},{9,8},{10,11... | collective-permute-start | bytes 752648 | tf_op jit(solution)/shard_map/ppermute | solution.py:25
  132.8 24.9 %collective-permute-start.9 = (bf16[4,196,640]{2,0,1:T(4,128)(2,1)}, bf16[4,196,640]{2,0,1:T(4,128)(2,1)S(1)}, u32[]{:S(2)}, u32[]{:S(2)}) collective-permute-start(bf16[4,196,640]{2,0,1:T(4,128)(2,1)} %copy.15), channel_id=1, source_target_pairs={{0,1},{1,0},{2,3},{3,2},{4,5},{5,4},{6,7},{7,6},{8,9},{9,8},{10,11... | collective-permute-start | bytes 3010568 | tf_op jit(solution)/shard_map/ppermute | solution.py:25
  146.3 17.1 %collective-permute-start.27 = (bf16[4,196,640]{2,0,1:T(4,128)(2,1)}, bf16[4,196,640]{2,0,1:T(4,128)(2,1)S(1)}, u32[]{:S(2)}, u32[]{:S(2)}) collective-permute-start(bf16[4,196,640]{2,0,1:T(4,128)(2,1)} %copy.20), channel_id=1, source_target_pairs={{0,1},{1,0},{2,3},{3,2},{4,5},{5,4},{6,7},{7,6},{8,9},{9,8},{10,11... | collective-permute-start | bytes 3010568 | tf_op jit(solution)/shard_map/ppermute | solution.py:25
  146.7 19.7 %collective-permute-start.42 = (bf16[4,196,640]{2,0,1:T(4,128)(2,1)}, bf16[4,196,640]{2,0,1:T(4,128)(2,1)S(1)}, u32[]{:S(2)}, u32[]{:S(2)}) collective-permute-start(bf16[4,196,640]{2,0,1:T(4,128)(2,1)} %copy.25), channel_id=1, source_target_pairs={{0,1},{1,0},{2,3},{3,2},{4,5},{5,4},{6,7},{7,6},{8,9},{9,8},{10,11... | collective-permute-start | bytes 3010568 | tf_op jit(solution)/shard_map/ppermute | solution.py:25
  166.4 18.7 %collective-permute-start.28 = (bf16[196,640]{1,0:T(8,128)(2,1)S(1)}, bf16[196,640]{1,0:T(8,128)(2,1)S(1)}, u32[]{:S(2)}, u32[]{:S(2)}) collective-permute-start(bf16[196,640]{1,0:T(8,128)(2,1)S(1)} %get-tuple-element.59), channel_id=1, source_target_pairs={{6,4},{7,5},{0,2},{1,3},{14,12},{15,13},{8,10},{9,11},{22,20},{23,... | collective-permute-start | bytes 752648 | tf_op jit(solution)/shard_map/ppermute | solution.py:63
  169.3 21.2 %collective-permute-start.46 = (bf16[196,640]{1,0:T(8,128)(2,1)S(1)}, bf16[196,640]{1,0:T(8,128)(2,1)S(1)}, u32[]{:S(2)}, u32[]{:S(2)}) collective-permute-start(bf16[196,640]{1,0:T(8,128)(2,1)S(1)} %get-tuple-element.60), channel_id=1, source_target_pairs={{6,4},{7,5},{0,2},{1,3},{14,12},{15,13},{8,10},{9,11},{22,20},{23,... | collective-permute-start | bytes 752648 | tf_op jit(solution)/shard_map/ppermute | solution.py:63
  172.2 23.8 %collective-permute-start.43 = (bf16[196,640]{1,0:T(8,128)(2,1)S(1)}, bf16[196,640]{1,0:T(8,128)(2,1)S(1)}, u32[]{:S(2)}, u32[]{:S(2)}) collective-permute-start(bf16[196,640]{1,0:T(8,128)(2,1)S(1)} %get-tuple-element.61), channel_id=1, source_target_pairs={{6,4},{7,5},{0,2},{1,3},{14,12},{15,13},{8,10},{9,11},{22,20},{23,... | collective-permute-start | bytes 752648 | tf_op jit(solution)/shard_map/ppermute | solution.py:63
  174.1 27.4 %collective-permute-start.61 = (bf16[196,640]{1,0:T(8,128)(2,1)S(1)}, bf16[196,640]{1,0:T(8,128)(2,1)S(1)}, u32[]{:S(2)}, u32[]{:S(2)}) collective-permute-start(bf16[196,640]{1,0:T(8,128)(2,1)S(1)} %get-tuple-element.62), channel_id=1, source_target_pairs={{6,4},{7,5},{0,2},{1,3},{14,12},{15,13},{8,10},{9,11},{22,20},{23,... | collective-permute-start | bytes 752648 | tf_op jit(solution)/shard_map/ppermute | solution.py:63
  179.5 26.7 %collective-permute-start.58 = (bf16[196,640]{1,0:T(8,128)(2,1)S(1)}, bf16[196,640]{1,0:T(8,128)(2,1)S(1)}, u32[]{:S(2)}, u32[]{:S(2)}) collective-permute-start(bf16[196,640]{1,0:T(8,128)(2,1)S(1)} %get-tuple-element.63), channel_id=1, source_target_pairs={{6,4},{7,5},{0,2},{1,3},{14,12},{15,13},{8,10},{9,11},{22,20},{23,... | collective-permute-start | bytes 752648 | tf_op jit(solution)/shard_map/ppermute | solution.py:63
  185.0 44.0 %collective-permute-start.14 = (bf16[196,640]{1,0:T(8,128)(2,1)S(1)}, bf16[196,640]{1,0:T(8,128)(2,1)S(1)}, u32[]{:S(2)}, u32[]{:S(2)}) collective-permute-start(bf16[196,640]{1,0:T(8,128)(2,1)S(1)} %add_convert_fusion.12), channel_id=1, source_target_pairs={{2,4},{3,5},{4,2},{5,3},{10,12},{11,13},{12,10},{13,11},{18,20},{1... | collective-permute-start | bytes 752648 | tf_op jit(solution)/shard_map/ppermute | solution.py:63
  190.5 16.4 %collective-permute-start.11 = (bf16[196,640]{1,0:T(8,128)(2,1)S(1)}, bf16[196,640]{1,0:T(8,128)(2,1)S(1)}, u32[]{:S(2)}, u32[]{:S(2)}) collective-permute-start(bf16[196,640]{1,0:T(8,128)(2,1)S(1)} %add_convert_fusion.14), channel_id=1, source_target_pairs={{2,4},{3,5},{4,2},{5,3},{10,12},{11,13},{12,10},{13,11},{18,20},{1... | collective-permute-start | bytes 752648 | tf_op jit(solution)/shard_map/ppermute | solution.py:63
  196.0 37.8 %collective-permute-start.32 = (bf16[196,640]{1,0:T(8,128)(2,1)S(1)}, bf16[196,640]{1,0:T(8,128)(2,1)S(1)}, u32[]{:S(2)}, u32[]{:S(2)}) collective-permute-start(bf16[196,640]{1,0:T(8,128)(2,1)S(1)} %add_convert_fusion.8), channel_id=1, source_target_pairs={{2,4},{3,5},{4,2},{5,3},{10,12},{11,13},{12,10},{13,11},{18,20},{1... | collective-permute-start | bytes 752648 | tf_op jit(solution)/shard_map/ppermute | solution.py:63
  206.2 30.9 %collective-permute-start.47 = (bf16[196,640]{1,0:T(8,128)(2,1)S(1)}, bf16[196,640]{1,0:T(8,128)(2,1)S(1)}, u32[]{:S(2)}, u32[]{:S(2)}) collective-permute-start(bf16[196,640]{1,0:T(8,128)(2,1)S(1)} %add_convert_fusion.4), channel_id=1, source_target_pairs={{2,4},{3,5},{4,2},{5,3},{10,12},{11,13},{12,10},{13,11},{18,20},{1... | collective-permute-start | bytes 752648 | tf_op jit(solution)/shard_map/ppermute | solution.py:63
  207.8 17.5 %collective-permute-start.59 = (bf16[196,640]{1,0:T(8,128)(2,1)S(1)}, bf16[196,640]{1,0:T(8,128)(2,1)S(1)}, u32[]{:S(2)}, u32[]{:S(2)}) collective-permute-start(bf16[196,640]{1,0:T(8,128)(2,1)S(1)} %add_convert_fusion.2), channel_id=1, source_target_pairs={{2,4},{3,5},{4,2},{5,3},{10,12},{11,13},{12,10},{13,11},{18,20},{1... | collective-permute-start | bytes 752648 | tf_op jit(solution)/shard_map/ppermute | solution.py:63
  208.5 22.1 %collective-permute-start.12 = (bf16[196,640]{1,0:T(8,128)(2,1)S(1)}, bf16[196,640]{1,0:T(8,128)(2,1)S(1)}, u32[]{:S(2)}, u32[]{:S(2)}) collective-permute-start(bf16[196,640]{1,0:T(8,128)(2,1)S(1)} %fusion.3), channel_id=1, source_target_pairs={{0,2},{1,3},{2,0},{3,1},{4,6},{5,7},{6,4},{7,5},{8,10},{9,11},{10,... | collective-permute-start | bytes 752648 | tf_op jit(solution)/shard_map/ppermute | solution.py:63
  (69 other events, 841.6 us)

commit v2 on v0

--- a/solution.py
+++ b/solution.py
@@ -1,14 +1,29 @@
+import functools
+
 import jax
 import jax.numpy as jnp
 from jax import lax
+from jax.experimental import pallas as pl
+from jax.experimental.pallas import tpu as pltpu
 from jax.sharding import PartitionSpec as P
 
 KVH = 8
 HS = 128
 L = 196
+CORES = 2
+CHIPS = 4
+EXTRA = 16
+LANES = 256
+HEAD_SPREAD = True
+SPLIT_OUT = True
+VMEM_A = 56
+STAGES = 2
+VMEM_B = 56
+GROUPS = [(0, 2), (2, 4)]
 
 
 EPS = 1e-06
+NT = (((1,), (1,)), ((), ()))
 
 
 def swapped(value, axis, apart):
@@ -39,6 +54,402 @@
         second_pair[0] - top
     )
     return (top, total)
+
+
+def between_chips(pairs):
+    return [(CORES * a + c, CORES * b + c) for a, b in pairs for c in range(CORES)]
+
+
+PARTNER = between_chips([(0, 1), (1, 0), (2, 3), (3, 2)])
+MIDDLE = between_chips([(1, 2), (2, 1)])
+OUTWARD = between_chips([(2, 3), (1, 0)])
+INWARD = between_chips([(3, 2), (0, 1)])
+
+
+def permuted(value, pairs):
+    return lax.ppermute(value, "tp", pairs)
+
+
+def after(value, *earlier):
+    return lax.optimization_barrier((value, earlier))[0]
+
+
+def attend_kernel(heads, order, length, *refs):
+    shards, (gain, w_q, w_kv, q_bias, v_bias, context, normed, q_rows, kv_rows, sems) = refs[:8], refs[8:]
+    width = shards[0].shape[1]
+    group, count = context.shape[:2]
+    copies = []
+    for k in range(8):
+        rows = pl.ds(pl.multiple_of(order[k] * width, width), width)
+        here = slice(k * width, (k + 1) * width)
+        copies.append(
+            (
+                pltpu.make_async_copy(w_q.at[rows, :], q_rows.at[here, :], sems.at[0, k]),
+                pltpu.make_async_copy(w_kv.at[rows, :], kv_rows.at[here, :], sems.at[1, k]),
+            )
+        )
+        for copy in copies[-1]:
+            copy.start()
+    total = None
+    for k in range(8):
+        wide = shards[k][...].astype(jnp.float32)
+        part = jnp.sum(wide * wide, axis=1, keepdims=True)
+        total = part if total is None else total + part
+    inverse = lax.rsqrt(total / (8 * width) + EPS)
+    for k in range(8):
+        scaled = shards[k][...].astype(jnp.float32) * inverse * gain[pl.ds(order[k], 1), :]
+        normed[:, k * width : (k + 1) * width] = scaled.astype(jnp.bfloat16)
+    q_sum = kv_sum = None
+    each = 8 // STAGES
+    for stage in range(STAGES):
+        for k in range(stage * each, (stage + 1) * each):
+            for copy in copies[k]:
+                copy.wait()
+        rows = slice(stage * each * width, (stage + 1) * each * width)
+        q_part = jnp.dot(normed[:, rows], q_rows[rows, :], preferred_element_type=jnp.float32)
+        kv_part = jnp.dot(normed[:, rows], kv_rows[rows, :], preferred_element_type=jnp.float32)
+        q_sum = q_part if q_sum is None else q_sum + q_part
+        kv_sum = kv_part if kv_sum is None else kv_sum + kv_part
+    q_sum += q_bias[...]
+    for g in range(group):
+        here = slice(g * count, (g + 1) * count)
+        queries = q_sum[here].astype(jnp.bfloat16)
+        keys = kv_sum[here, :HS].astype(jnp.bfloat16)
+        values = (kv_sum[here, HS:] + v_bias[...]).astype(jnp.bfloat16)
+        valid = lax.broadcasted_iota(jnp.int32, (1, count), 1) < length[g]
+        done = []
+        for h in range(heads):
+            scores = lax.dot_general(
+                queries[:, h * HS : (h + 1) * HS], keys, NT, preferred_element_type=jnp.float32
+            )
+            scores = jnp.where(valid, scores, jnp.float32(-1e30))
+            expo = jnp.exp((scores - jnp.max(scores, axis=1, keepdims=True)) * HS ** (-0.5))
+            share = 1.0 / jnp.sum(expo, axis=1, keepdims=True)
+            mixed = jnp.dot(expo.astype(jnp.bfloat16), values, preferred_element_type=jnp.float32)
+            done.append((mixed * share).astype(jnp.bfloat16))
+        for h in range(heads):
+            context[g, :, h * HS : (h + 1) * HS] = done[h]
+
+
+def out_kernel(places, own, other, w_own, w_other, *refs):
+    targets, (own_rows, other_rows, own_sems, other_sems) = refs[:-4], refs[-4:]
+    group, _, width = targets[0].shape
+    copies = []
+    for k in range(len(targets)):
+        columns = pl.ds(pl.multiple_of(places[k] * width, width), width)
+        copies.append(
+            (
+                pltpu.make_async_copy(w_own.at[:, columns], own_rows.at[k], own_sems.at[k]),
+                pltpu.make_async_copy(w_other.at[:, columns], other_rows.at[k], other_sems.at[k]),
+            )
+        )
+        for copy in copies[-1]:
+            copy.start()
+    for k in range(len(targets)):
+        for copy in copies[k]:
+            copy.wait()
+        for g in range(group):
+            part = jnp.dot(own[g], own_rows[k], preferred_element_type=jnp.float32)
+            part += jnp.dot(other[g], other_rows[k], preferred_element_type=jnp.float32)
+            targets[k][g] = part.astype(jnp.bfloat16)
+
+
+def head_kernel(groups, *refs):
+    chunks, refs = refs[: 4 * len(groups)], refs[4 * len(groups) :]
+    gain, w_rows = refs[:2]
+    hiddens, (keep, send) = refs[2:-2], refs[-2:]
+    entries = w_rows.shape[0] // 8
+    place = 0
+    for i, group in enumerate(groups):
+        kept, partner, middle, masked = chunks[4 * i : 4 * i + 4]
+        for g in range(group):
+            wide = lambda ref: ref[g].astype(jnp.float32)
+            summed = wide(kept) + (wide(partner) + wide(middle))
+            rounded = (wide(masked) + summed).astype(jnp.bfloat16)
+            hiddens[i][g] = rounded
+            value = rounded.astype(jnp.float32)
+            scaled = (value * gain[...]).astype(jnp.bfloat16)
+            logits = lax.dot_general(w_rows[...], scaled, NT, preferred_element_type=jnp.float32)
+            ones = jnp.ones((EXTRA // 2, value.shape[1]), jnp.float32)
+            squares = lax.dot_general(
+                ones, value * value, NT, preferred_element_type=jnp.float32, precision=lax.Precision.HIGHEST
+            )
+            coarse = squares.astype(jnp.bfloat16)
+            fine = (squares - coarse.astype(jnp.float32)).astype(jnp.bfloat16)
+            both = jnp.concatenate([coarse, fine], axis=0)
+            lanes = slice(place * LANES, place * LANES + value.shape[0])
+            place += 1
+            for row, k in enumerate((0, 4, 2, 6)):
+                for target, block in ((keep, k), (send, k + 1)):
+                    part = logits[block * entries : (block + 1) * entries]
+                    target[row, 0:entries, lanes] = part.astype(jnp.bfloat16)
+                    target[row, entries : entries + EXTRA, lanes] = both
+
+
+def whole(space=pltpu.VMEM):
+    return pl.BlockSpec(memory_space=space)
+
+
+def head_steps(w_head, index):
+    turned = w_head.T
+    entries = turned.shape[0]
+    width = turned.shape[1] // 8
+    parts = lax.axis_size("rep")
+    rep = lax.axis_index("rep")
+    shared = parts & (parts - 1) == 0 and entries % (16 * parts) == 0
+    if shared:
+        share = entries // parts
+        turned = lax.dynamic_slice_in_dim(turned, rep * share, share, axis=0)
+    blocks = jnp.stack(
+        [
+            lax.dynamic_slice_in_dim(turned, jnp.bitwise_xor(index, k) * width, width, axis=1)
+            for k in range(8)
+        ]
+    )
+    for level in range(3):
+        bit = 1 << level
+        stay = [k for k in range(8) if not k & bit]
+        move = [k for k in range(8) if k & bit]
+        got = yield swapped(jnp.stack([blocks[k] for k in move]), "tp", level)
+        merged = [None] * 8
+        for place, k in enumerate(stay):
+            merged[k] = blocks[k]
+        for place, k in enumerate(move):
+            merged[k] = got[place]
+        blocks = jnp.stack(merged)
+    if shared:
+        for level in range(parts.bit_length() - 1):
+            got = yield swapped(blocks, "rep", level)
+            lower = jnp.bitwise_and(jnp.right_shift(rep, level), 1) == 0
+            blocks = jnp.concatenate(
+                [jnp.where(lower, blocks, got), jnp.where(lower, got, blocks)], axis=1
+            )
+    yield blocks.reshape(8 * entries, width)
+
+
+def on_line(
+    embeds,
+    remask,
+    lengths,
+    mask_vec,
+    attn_gain,
+    w_query,
+    q_bias,
+    w_key,
+    w_value,
+    v_bias,
+    w_out,
+    head_gain,
+    w_head,
+):
+    requests = lengths.shape[0]
+    width = embeds.shape[1]
+    heads = w_query.shape[1] // HS
+    entries = w_head.shape[1]
+    index = lax.axis_index("tp")
+    chip, core = index // CORES, index % CORES
+    first_half = chip < 2
+    line = jnp.stack(
+        [chip, jnp.bitwise_xor(chip, 1), jnp.where(first_half, 2, 1), jnp.where(first_half, 3, 0)]
+    ).astype(jnp.int32)
+    places = jnp.concatenate([line * CORES + core, line * CORES + (1 - core)])
+    by_request = embeds.reshape(requests, L, width)
+    chosen = remask.reshape(requests, L, 1) == 1
+    masked, flat = [], []
+    for first, end in GROUPS:
+        rows = slice(first * L, end * L)
+        flat.append(jnp.where(remask[rows, None] == 1, mask_vec[None, :], embeds[rows]))
+        masked.append(jnp.where(chosen[first:end], mask_vec[None, None, :], by_request[first:end]))
+    sizes = [end - first for first, end in GROUPS]
+
+    def of_core(matrix, wanted):
+        return jnp.concatenate(
+            [
+                lax.dynamic_slice_in_dim(matrix, (CORES * z + wanted) * width, width, axis=1)
+                for z in range(CHIPS)
+            ],
+            axis=1,
+        )
+
+    w_own = of_core(w_out, core)
+    w_other = swapped(of_core(w_out, 1 - core), "tp", 0)
+    w_kv = jnp.concatenate([w_key, w_value], axis=1)
+    gain = attn_gain.astype(jnp.float32).reshape(8, width)
+    q_row = q_bias.astype(jnp.float32)[None, :]
+    v_row = v_bias.astype(jnp.float32)[None, :]
+    gain_local = lax.dynamic_slice_in_dim(head_gain, index * width, width).astype(jnp.float32)[None, :]
+
+    steps = head_steps(w_head, index)
+    moving = [next(steps)]
+
+    def step_head():
+        try:
+            moving[0] = steps.send(moving[0])
+        except StopIteration:
+            pass
+
+    def attend(i):
+        first, end = GROUPS[i]
+        return pl.pallas_call(
+            functools.partial(attend_kernel, heads),
+            out_shape=jax.ShapeDtypeStruct((sizes[i], L, heads * HS), jnp.bfloat16),
+            in_specs=[whole(pltpu.SMEM)] * 2 + [whole()] * 9 + [whole(pl.ANY)] * 2 + [whole()] * 2,
+            out_specs=whole(),
+            scratch_shapes=[
+                pltpu.VMEM((sizes[i] * L, 8 * width), jnp.bfloat16),
+                pltpu.VMEM((8 * width, heads * HS), jnp.bfloat16),
+                pltpu.VMEM((8 * width, 2 * HS), jnp.bfloat16),
+                pltpu.SemaphoreType.DMA((2, 8)),
+            ],
+            compiler_params=pltpu.CompilerParams(vmem_limit_bytes=VMEM_A * 2**20),
+            cost_estimate=pl.CostEstimate(
+                flops=sizes[i] * 2 * L * width * 8 * (heads * HS + 2 * HS),
+                bytes_accessed=sizes[i] * 12 * 2**20,
+                transcendentals=sizes[i] * heads * L * L,
+            ),
+        )(places, lengths[first:end], *shards[i], gain, w_query, w_kv, q_row, v_row)
+
+    def out(size, wanted, *operands):
+        count = wanted.shape[0]
+        return pl.pallas_call(
+            out_kernel,
+            out_shape=[jax.ShapeDtypeStruct((size, L, width), jnp.bfloat16)] * count,
+            in_specs=[whole(pltpu.SMEM)] + [whole()] * 2 + [whole(pl.ANY)] * 2,
+            out_specs=[whole()] * count,
+            scratch_shapes=[
+                pltpu.VMEM((count, heads * HS, width), jnp.bfloat16),
+                pltpu.VMEM((count, heads * HS, width), jnp.bfloat16),
+                pltpu.SemaphoreType.DMA((count,)),
+                pltpu.SemaphoreType.DMA((count,)),
+            ],
+            compiler_params=pltpu.CompilerParams(vmem_limit_bytes=VMEM_B * 2**20),
+            cost_estimate=pl.CostEstimate(
+                flops=size * 2 * L * width * 2 * count * heads * HS,
+                bytes_accessed=size * 4 * count * 2**20,
+                transcendentals=0,
+            ),
+        )(wanted, *operands)
+
+    def head(groups, chunks):
+        count = sum(groups)
+        return pl.pallas_call(
+            functools.partial(head_kernel, groups),
+            out_shape=[jax.ShapeDtypeStruct((size, L, width), jnp.bfloat16) for size in groups]
+            + [jax.ShapeDtypeStruct((4, entries + EXTRA, count * LANES), jnp.bfloat16)] * 2,
+            in_specs=[whole()] * (4 * len(groups) + 2),
+            out_specs=[whole()] * (len(groups) + 2),
+            compiler_params=pltpu.CompilerParams(vmem_limit_bytes=32 * 2**20),
+            cost_estimate=pl.CostEstimate(
+                flops=count * 2 * L * width * 8 * entries, bytes_accessed=count * 3 * 2**20, transcendentals=0
+            ),
+        )(*[value for chunk in chunks for value in chunk], gain_local, moving[0])
+
+    add = lambda *terms: sum(term.astype(jnp.float32) for term in terms).astype(jnp.bfloat16)
+    last = len(GROUPS) - 1
+    own, inward, middle, partner = ({} for _ in range(4))
+
+    def advance_middle(i, *earlier):
+        value = add(own[i][2], after(inward[i], *earlier))
+        middle[i] = permuted(value, MIDDLE)
+        return value
+
+    def advance_partner(i, *earlier):
+        value = add(own[i][1], after(middle[i][0], *earlier))
+        partner[i] = permuted(value, PARTNER)
+        return value
+
+    def add_sums(kept, got):
+        total = kept.astype(jnp.float32) + got.astype(jnp.float32)
+        logits, coarse, fine = jnp.split(total, [entries, entries + EXTRA // 2], axis=-2)
+        squares = coarse + fine
+        coarse = squares.astype(jnp.bfloat16)
+        fine = (squares - coarse.astype(jnp.float32)).astype(jnp.bfloat16)
+        return jnp.concatenate([logits.astype(jnp.bfloat16), coarse, fine], axis=-2)
+
+    def both_cores(*mine):
+        return [*mine, *(swapped(shard, "tp", 0) for shard in mine)]
+
+    own = flat[0]
+    partner, middle = permuted(own, PARTNER), permuted(own, MIDDLE)
+    far_middle, near_out = permuted(partner, MIDDLE), permuted(middle, OUTWARD)
+    if HEAD_SPREAD:
+        moving[0] = after(moving[0], partner)
+        step_head()
+        moving[0] = after(moving[0], far_middle)
+        step_head()
+    far_out = permuted(far_middle, OUTWARD)
+    shards = [both_cores(own, partner, middle + near_out, far_middle + far_out)]
+
+    own = after(flat[1], far_middle)
+    middle = permuted(own, MIDDLE)
+    own = after(own, far_out)
+    partner = permuted(own, PARTNER)
+    shards[0] = after(shards[0], own)
+    context = attend(0)
+    other = after(swapped(context, "tp", 0), partner, moving[0])
+    step_head()
+    far_middle, near_out = permuted(partner, MIDDLE), permuted(after(middle, partner), OUTWARD)
+    self_part, partner_part, near, far = out(sizes[0], line, context, other, w_own, w_other)
+    far_out = permuted(far_middle, OUTWARD)
+    shards.append(both_cores(own, partner, middle + near_out, far_middle + far_out))
+    far_in = permuted(after(far, far_middle), INWARD)
+    far = add(far, far_in)
+    far_middle = permuted(far, MIDDLE)
+    near_in = permuted(after(near, far_in), INWARD)
+
+    shards[1] = after(shards[1], far, moving[0])
+    step_head()
+    context = attend(1)
+    other = after(swapped(context, "tp", 0), far_middle, near_in)
+    partner_part, near = add(partner_part, far_middle), add(near, near_in)
+    first_parts = [self_part, permuted(partner_part, PARTNER), permuted(near, MIDDLE), masked[0]]
+    other = after(other, partner_part, near)
+    if SPLIT_OUT:
+        (far,) = out(sizes[1], line[3:], context, other, w_own, w_other)
+        far_in = permuted(far, INWARD)
+        other = after(other, far)
+        self_part, partner_part, near = out(sizes[1], line[:3], context, other, w_own, w_other)
+    else:
+        self_part, partner_part, near, far = out(sizes[1], line, context, other, w_own, w_other)
+        far_in = permuted(far, INWARD)
+    far_middle = permuted(add(far, after(far_in, first_parts)), MIDDLE)
+    near_in = permuted(after(near, far_in), INWARD)
+    while moving[0].shape != (8 * entries, width):
+        step_head()
+    hidden_first, kept, sent = head(sizes[:1], [after(first_parts, near)])
+    from_partner = permuted(add(partner_part, far_middle), PARTNER)
+    near_middle = permuted(add(near, after(near_in, far_middle)), MIDDLE)
+    sent = swapped(sent, "tp", 0)
+    held = add_sums(kept, sent)
+    move = swapped(held[2:], "tp", 1)
+    held = add_sums(held[:2], move)
+    move = swapped(held[1], "tp", 2)
+    from_partner = after(from_partner, move)
+    hidden, kept, sent = head(sizes[1:], [(self_part, from_partner, near_middle, masked[1])])
+    hiddens = [hidden_first, hidden]
+    held = add_sums(held[0], move)
+    held_last = add_sums(kept, swapped(sent, "tp", 0))
+    held_last = add_sums(held_last[:2], swapped(held_last[2:], "tp", 1))
+    held_last = add_sums(held_last[0], swapped(held_last[1], "tp", 2))
+
+    def finished(held):
+        held = held.astype(jnp.float32)
+        inverse = lax.rsqrt((held[entries] + held[entries + EXTRA // 2]) / (8 * width) + EPS)
+        logits = held[:entries] * inverse[None, :]
+        top = jnp.max(logits, axis=0)
+        return logits, jnp.stack([top, jnp.sum(jnp.exp(logits - top[None, :]), axis=0)])
+
+    logits, pairs = finished(held)
+    logits_last, pairs_last = finished(held_last)
+    logits = jnp.concatenate([logits, logits_last], axis=1)
+    pair = jnp.concatenate([pairs, pairs_last], axis=1)
+    for level in range(3):
+        pair = jnp.stack(combine_pair(pair, swapped(pair, "tp", level)))
+    logprob = logits - (pair[0] + jnp.log(pair[1]))[None, :]
+    logprob = jnp.concatenate(
+        [logprob[:, r * LANES : r * LANES + L] for r in range(requests)], axis=1
+    )
+    return (jnp.concatenate(hiddens, axis=0).reshape(requests * L, width), logprob.T)
 
 
 def on_device(
@@ -138,8 +549,9 @@
         P(),
         P(None, "tp"),
     )
+    on_line_fits = mesh.shape["tp"] == CORES * CHIPS and mesh.shape["tp"] == KVH
     return jax.shard_map(
-        on_device,
+        on_line if on_line_fits else on_device,
         mesh=mesh,
         in_specs=placed,
         out_specs=(P("rep", "tp"), P("rep", "tp")),

time: 362 us -> 228 us (0.63)
  waiting for transfers between devices: 251 us -> 77.8 us
  starting transfers between devices: 0.12 us -> 67.2 us
  Pallas kernels: 0 us -> 46 us
  matrix products: 29.2 us -> 0 us
  blocking collectives: 26.7 us -> 0 us
  between operations: 14.6 us -> 1.76 us
    all_gather x2 -> x0, waiting for transfers between devices: 155 us -> none  [the longest x1 79.1 us: on_device(): gathered = lax.all_gather(masked_local, 'tp', axis=1, tiled=True)]
    unnamed x4 -> x0, waiting for transfers between devices: 95.7 us -> none
    ppermute x0 -> x45, waiting for transfers between devices: none -> 77.8 us  [the longest x25 48.7 us: swapped(): return lax.ppermute(value, axis, pairs)]
    ppermute x0 -> x45, starting transfers between devices: none -> 67.2 us  [the longest x20 39.2 us: permuted(): return lax.ppermute(value, 'tp', pairs)]
    pallas_call x0 -> x7, Pallas kernels: none -> 46 us  [the longest x2 26.1 us: attend(): pl.pallas_call(functools.partial(attend_kernel, heads), out_shape=jax.Sha...]
    dot_general x7 -> x0, matrix products: 29.2 us -> none  [the longest x1 6.88 us: on_device(): jnp.dot(normed, w_query, preferred_element_type=jnp.float32)]
    unnamed x1 -> x0, blocking collectives: 26.7 us -> none
    unnamed x27 -> x81, local copies, waits for them, and re-layouts: 18.1 us -> 5.57 us
  transfers between devices with their start and end apart: 3 -> 45, of which waited for: 3 -> 15; matrix products, arithmetic and copies ran while one was open for 1% -> 11% of each run, Pallas kernels for 0% -> 20%
where the time goes in v2:
time: 228 us; the launch traced here: 227 us
  waiting for transfers between devices  77.8 us (34%)
  starting transfers between devices  67.2 us (29%)
  Pallas kernels  46 us (20%)
  other arithmetic  17.4 us (8%)
  local copies, waits for them, and re-layouts  16.7 us (7%)
    ppermute x25, waiting for transfers between devices, swapped(): return lax.ppermute(value, axis, pairs)  48.7 us
    ppermute x20, starting transfers between devices, permuted(): return lax.ppermute(value, 'tp', pairs)  39.2 us
    ppermute x20, waiting for transfers between devices, permuted(): return lax.ppermute(value, 'tp', pairs)  29.1 us
    ppermute x25, starting transfers between devices, swapped(): return lax.ppermute(value, axis, pairs)  27.9 us
    pallas_call x2, Pallas kernels, attend(): pl.pallas_call(functools.partial(attend_kernel, heads), out_shape=jax.Sha...  26.1 us
    pallas_call x3, Pallas kernels, out(): pl.pallas_call(out_kernel, out_shape=[jax.ShapeDtypeStruct((size, L, widt...  16.6 us
    unnamed x81, local copies, waits for them, and re-layouts  5.57 us
  transfers between devices with their start and end apart: 45, of which 15 were waited for; matrix products, arithmetic and copies ran while one was open for 11% of the time, Pallas kernels for 20%

profile of v2, /device:TPU:0, one launch (start us, length us, event | category | flops | bytes accessed | tf_op | source)
XLA Modules:
  0.0 226.8 jit_solution(11659065995883465577)
XLA Ops:
  1.5 2.4 %broadcast_select_fusion.3 = (bf16[392,640]{1,0:T(8,128)(2,1)}, bf16[392,640]{1,0:T(8,128)(2,1)S(1)}, bf16[392,640]{1,0:T(8,128)(2,1)}, bf16[392,640]{1,0:T(8,128)(2,1)}) fusion(pred[392]{0:T(512)(128)(4,1)S(1)} %get-tuple-element.154, bf16[640]{0:T(1024)(128)(2,1)} %param.16, bf16[784,640]{1,0:T(8,128)(2,1)} %param.13, pred[392]{0:T(512)(128)(4,1)S(1)} %get-tuple-element.155), kind=kLoop, calls=%fused_computation.17 | loop fusion | flops 501760 | bytes 3012624 | tf_op jit(solution)/shard_map/jit(_where)/select_n | solution.py:261
  3.9 3.0 %collective-permute-start = (bf16[392,640]{1,0:T(8,128)(2,1)}, bf16[392,640]{1,0:T(8,128)(2,1)}, u32[]{:S(2)}, u32[]{:S(2)}) collective-permute-start(bf16[392,640]{1,0:T(8,128)(2,1)} %get-tuple-element.52.refs_0_), channel_id=1, source_target_pairs={{0,2},{1,3},{2,0},{3,1},{4,6},{5,7},{6,4},{7,5},{8,10},{9,11},{10,... | collective-permute-start | bytes 1505288 | tf_op jit(solution)/shard_map/ppermute | solution.py:70
  8.4 3.0 %constant_dynamic-slice_fusion.3 = (bf16[512,640]{1,0:T(8,128)(2,1)S(1)}, bf16[512,640]{1,0:T(8,128)(2,1)S(1)}, bf16[512,640]{1,0:T(8,128)(2,1)S(1)}, bf16[512,6...) fusion(bf16[512,5120]{1,0:T(8,128)(2,1)} %param.23, ...), kind=kLoop, calls=%fused_computation.108 | loop fusion | bytes 10485792 | tf_op jit(solution)/shard_map/dynamic_slice | solution.py:268
  13.5 1.6 dynamic-slice_bitcast_fusion
  15.2 1.6 constant_dynamic-update-slice_fusion.1
  17.3 1.8 pad_maximum_fusion.w_own
  24.5 16.9 %collective-permute-start.12 = (bf16[4,16,640]{2,1,0:T(8,128)(2,1)S(1)}, bf16[4,16,640]{2,1,0:T(8,128)(2,1)}, u32[]{:S(2)}, u32[]{:S(2)}) collective-permute-start(bf16[4,16,640]{2,1,0:T(8,128)(2,1)S(1)} %pad_maximum_fusion.11), channel_id=1, source_target_pairs={{0,2},{1,3},{2,0},{3,1},{4,6},{5,7},{6,4},{7,5},{8,10},{9,11},{10,... | collective-permute-start | bytes 245768 | tf_op jit(solution)/shard_map/ppermute | solution.py:32
  43.1 9.7 %collective-permute-done.4 = bf16[392,640]{1,0:T(8,128)(2,1)S(1)} collective-permute-done((bf16[392,640]{1,0:T(8,128)(2,1)S(1)}, bf16[392,640]{1,0:T(8,128)(2,1)S(1)}, u32[]{:S(2)}, u32[]{:S(2)}) %collective-permute-start.4) | collective-permute-done | bytes 501792 | tf_op jit(solution)/shard_map/ppermute | solution.py:70
  59.5 7.5 %collective-permute-done.10.refs_1_ = bf16[392,640]{1,0:T(8,128)(2,1)} collective-permute-done((bf16[392,640]{1,0:T(8,128)(2,1)S(1)}, bf16[392,640]{1,0:T(8,128)(2,1)}, u32[]{:S(2)}, u32[]{:S(2)}) %collective-permute-start.10) | collective-permute-done | bytes 501792 | tf_op jit(solution)/shard_map/ppermute | solution.py:70
  68.5 13.1 %shard_map.140.own = bf16[2,196,512]{2,1,0:T(8,128)(2,1)} custom-call(s32[8]{0:T(128)} %pad_add_fusion.1.order, s32[2]{0:T(128)} %get-tuple-element.160.length, bf16[392,640]{1,0:T(8,128)(2,1)} %get-tuple-element.52.refs_0_, bf16[392,640]{1,0:T(8,128)(2,1)} %collective-permute-done.refs_1_, bf16[392,640]{1,0:T(8,128)(2,1)} %copy-done.7, ...), custom_call_target="tpu_custom_call" | custom-call | flops 3082813440 | bytes 25165824 | tf_op jit(solution)/shard_map/pallas_call | solution.py:293
  81.7 2.3 %collective-permute-start.13 = (bf16[4,16,640]{2,1,0:T(8,128)(2,1)S(1)}, bf16[4,16,640]{2,1,0:T(8,128)(2,1)S(1)}, u32[]{:S(2)}, u32[]{:S(2)}) collective-permute-start(bf16[4,16,640]{2,1,0:T(8,128)(2,1)S(1)} %pad_maximum_fusion.12), channel_id=1, source_target_pairs={{0,4},{1,5},{2,6},{3,7},{4,0},{5,1},{6,2},{7,3},{8,12},{9,13},{10,... | collective-permute-start | bytes 245768 | tf_op jit(solution)/shard_map/ppermute | solution.py:32
  87.0 2.2 collective-permute-done.13
  91.6 6.7 %shard_map.141 = (bf16[2,196,640]{2,1,0:T(8,128)(2,1)}, bf16[2,196,640]{2,1,0:T(8,128)(2,1)}, bf16[2,196,640]{2,1,0:T(8,128)(2,1)}, bf16[2,196,640]{2,1,0:T(8,128)(2,1)}) custom-call(s32[4]{0:T(128)} %copy-done.37, bf16[2,196,512]{2,1,0:T(8,128)(2,1)} %shard_map.140.own, bf16[2,196,512]{2,1,0:T(8,128)(2,1)} %copy-done.38, ...), custom_call_target="tpu_custom_call" | custom-call | flops 2055208960 | bytes 33554432 | tf_op jit(solution)/shard_map/pallas_call | solution.py:314
  98.4 3.9 %collective-permute-start.16 = (bf16[2,196,640]{2,1,0:T(8,128)(2,1)}, bf16[2,196,640]{2,1,0:T(8,128)(2,1)S(1)}, u32[]{:S(2)}, u32[]{:S(2)}) collective-permute-start(bf16[2,196,640]{2,1,0:T(8,128)(2,1)} %get-tuple-element.66), channel_id=1, source_target_pairs={{6,4},{7,5},{0,2},{1,3},{14,12},{15,13},{8,10},{9,11},{22,20},{23,... | collective-permute-start | bytes 1505288 | tf_op jit(solution)/shard_map/ppermute | solution.py:70
  106.8 4.1 %collective-permute-done.23 = bf16[392,640]{1,0:T(8,128)(2,1)} collective-permute-done((bf16[392,640]{1,0:T(8,128)(2,1)}, bf16[392,640]{1,0:T(8,128)(2,1)}, u32[]{:S(2)}, u32[]{:S(2)}) %collective-permute-start.23) | collective-permute-done | bytes 501792 | tf_op jit(solution)/shard_map/ppermute | solution.py:70
  113.3 4.3 %collective-permute-start.19 = (bf16[2,196,640]{2,1,0:T(8,128)(2,1)S(1)}, bf16[2,196,640]{2,1,0:T(8,128)(2,1)S(1)}, u32[]{:S(2)}, u32[]{:S(2)}) collective-permute-start(bf16[2,196,640]{2,1,0:T(8,128)(2,1)S(1)} %copy-done.14), channel_id=1, source_target_pairs={{6,4},{7,5},{0,2},{1,3},{14,12},{15,13},{8,10},{9,11},{22,20},{23,... | collective-permute-start | bytes 1505288 | tf_op jit(solution)/shard_map/ppermute | solution.py:70
  121.7 13.1 %shard_map.142.own = bf16[2,196,512]{2,1,0:T(8,128)(2,1)} custom-call(s32[8]{0:T(128)} %pad_add_fusion.1.order, s32[2]{0:T(128)} %get-tuple-element.161.length, bf16[392,640]{1,0:T(8,128)(2,1)} %copy-done.4, bf16[392,640]{1,0:T(8,128)(2,1)} %collective-permute-done.10.refs_1_, bf16[392,640]{1,0:T(8,128)(2,1)} %copy-done.8, bf16[392,640]{1,0:T(8,128)(2,1)} %copy-done.10, ...), custom_call_target="tpu_custom_call" | custom-call | flops 3082813440 | bytes 25165824 | tf_op jit(solution)/shard_map/pallas_call | solution.py:293
  135.8 3.9 %collective-permute-start.18 = (bf16[2,196,640]{2,1,0:T(8,128)(2,1)S(1)}, bf16[2,196,640]{2,1,0:T(8,128)(2,1)S(1)}, u32[]{:S(2)}, u32[]{:S(2)}) collective-permute-start(bf16[2,196,640]{2,1,0:T(8,128)(2,1)S(1)} %add_convert_fusion.4), channel_id=1, source_target_pairs={{0,2},{1,3},{2,0},{3,1},{4,6},{5,7},{6,4},{7,5},{8,10},{9,11},{10,... | collective-permute-start | bytes 1505288 | tf_op jit(solution)/shard_map/ppermute | solution.py:70
  140.5 4.1 %shard_map.143 = bf16[2,196,640]{2,1,0:T(8,128)(2,1)} custom-call(s32[1]{0:T(128)} %bitcast.3.places, bf16[2,196,512]{2,1,0:T(8,128)(2,1)} %shard_map.142.own, bf16[2,196,512]{2,1,0:T(8,128)(2,1)} %copy-done.11, bf16[512,2560]{1,0:T(8,128)(2,1)} %pad_maximum_fusion.w_own, bf16[512,2560]{1,0:T(8,128)(2,1)} %collective-permute-done.14.w_other), custom_call_target="tpu_custom_call" | custom-call | flops 513802240 | bytes 8388608 | tf_op jit(solution)/shard_map/pallas_call | solution.py:314
  144.6 2.2 collective-permute-start.31
  147.0 5.9 %shard_map.144 = (bf16[2,196,640]{2,1,0:T(8,128)(2,1)}, bf16[2,196,640]{2,1,0:T(8,128)(2,1)}, bf16[2,196,640]{2,1,0:T(8,128)(2,1)}) custom-call(s32[3]{0:T(128)} %pad_add_fusion.2.places, bf16[2,196,512]{2,1,0:T(8,128)(2,1)} %shard_map.142.own, bf16[2,196,512]{2,1,0:T(8,128)(2,1)} %copy-done.11, bf16[512,2560]{1,0:T(8,128)(2,1)} %pad_maximum_fusion.w_own, ...), custom_call_target="tpu_custom_call" | custom-call | flops 1541406720 | bytes 25165824 | tf_op jit(solution)/shard_map/pallas_call | solution.py:314
  152.9 1.6 shard_map.145
  154.7 7.4 %collective-permute-done.31 = bf16[2,196,640]{2,1,0:T(8,128)(2,1)S(1)} collective-permute-done((bf16[2,196,640]{2,1,0:T(8,128)(2,1)}, bf16[2,196,640]{2,1,0:T(8,128)(2,1)S(1)}, u32[]{:S(2)}, u32[]{:S(2)}) %collective-permute-start.31) | collective-permute-done | bytes 501792 | tf_op jit(solution)/shard_map/ppermute | solution.py:70
  162.1 4.3 %collective-permute-start.37 = (bf16[2,196,640]{2,1,0:T(8,128)(2,1)S(1)}, bf16[2,196,640]{2,1,0:T(8,128)(2,1)S(1)}, u32[]{:S(2)}, u32[]{:S(2)}) collective-permute-start(bf16[2,196,640]{2,1,0:T(8,128)(2,1)S(1)} %copy-done.17), channel_id=1, source_target_pairs={{6,4},{7,5},{0,2},{1,3},{14,12},{15,13},{8,10},{9,11},{22,20},{23,... | collective-permute-start | bytes 1505288 | tf_op jit(solution)/shard_map/ppermute | solution.py:70
  168.7 11.7 %collective-permute-done.35 = bf16[2,80,512]{2,1,0:T(8,128)(2,1)S(1)} collective-permute-done((bf16[2,80,512]{2,1,0:T(8,128)(2,1)S(1)}, bf16[2,80,512]{2,1,0:T(8,128)(2,1)S(1)}, u32[]{:S(2)}, u32[]{:S(2)}) %collective-permute-start.35) | collective-permute-done | bytes 163872 | tf_op jit(solution)/shard_map/ppermute | solution.py:32
  181.4 4.2 %collective-permute-start.33 = (bf16[2,196,640]{2,1,0:T(8,128)(2,1)S(1)}, bf16[2,196,640]{2,1,0:T(8,128)(2,1)S(1)}, u32[]{:S(2)}, u32[]{:S(2)}) collective-permute-start(bf16[2,196,640]{2,1,0:T(8,128)(2,1)S(1)} %add_convert_fusion.1), channel_id=1, source_target_pairs={{0,2},{1,3},{2,0},{3,1},{4,6},{5,7},{6,4},{7,5},{8,10},{9,11},{10,... | collective-permute-start | bytes 1505288 | tf_op jit(solution)/shard_map/ppermute | solution.py:70
  186.7 13.1 %collective-permute-done.36 = bf16[80,512]{1,0:T(8,128)(2,1)S(1)} collective-permute-done((bf16[80,512]{1,0:T(8,128)(2,1)S(1)}, bf16[80,512]{1,0:T(8,128)(2,1)S(1)}, u32[]{:S(2)}, u32[]{:S(2)}) %collective-permute-start.36) | collective-permute-done | bytes 81952 | tf_op jit(solution)/shard_map/ppermute | solution.py:32
  199.9 1.6 shard_map.146
  203.9 5.9 %collective-permute-done.40 = bf16[2,80,512]{2,1,0:T(8,128)(2,1)S(1)} collective-permute-done((bf16[2,80,512]{2,1,0:T(8,128)(2,1)S(1)}, bf16[2,80,512]{2,1,0:T(8,128)(2,1)S(1)}, u32[]{:S(2)}, u32[]{:S(2)}) %collective-permute-start.40) | collective-permute-done | bytes 163872 | tf_op jit(solution)/shard_map/ppermute | solution.py:32
  210.1 5.9 %collective-permute-done.41 = bf16[80,512]{1,0:T(8,128)(2,1)S(1)} collective-permute-done((bf16[80,512]{1,0:T(8,128)(2,1)S(1)}, bf16[80,512]{1,0:T(8,128)(2,1)S(1)}, u32[]{:S(2)}, u32[]{:S(2)}) %collective-permute-start.41) | collective-permute-done | bytes 81952 | tf_op jit(solution)/shard_map/ppermute | solution.py:32
  217.6 3.6 %collective-permute-done.43 = f32[2,1024]{1,0:T(2,128)S(1)} collective-permute-done((f32[2,1024]{1,0:T(2,128)S(1)}, f32[2,1024]{1,0:T(2,128)S(1)}, u32[]{:S(2)}, u32[]{:S(2)}) %collective-permute-start.43) | collective-permute-done | bytes 8224 | tf_op jit(solution)/shard_map/ppermute | solution.py:32
  222.6 3.3 %collective-permute-done.44 = f32[2,1024]{1,0:T(2,128)S(1)} collective-permute-done((f32[2,1024]{1,0:T(2,128)S(1)}, f32[2,1024]{1,0:T(2,128)S(1)}, u32[]{:S(2)}, u32[]{:S(2)}) %collective-permute-start.44) | collective-permute-done | bytes 8224 | tf_op jit(solution)/shard_map/ppermute | solution.py:32
  (234 shorter events, 49.3 us)
Async XLA Ops:
  3.9 15.7 %collective-permute-start = (bf16[392,640]{1,0:T(8,128)(2,1)}, bf16[392,640]{1,0:T(8,128)(2,1)}, u32[]{:S(2)}, u32[]{:S(2)}) collective-permute-start(bf16[392,640]{1,0:T(8,128)(2,1)} %get-tuple-element.52.refs_0_), channel_id=1, source_target_pairs={{0,2},{1,3},{2,0},{3,1},{4,6},{5,7},{6,4},{7,5},{8,10},{9,11},{10,... | collective-permute-start | bytes 1505288 | tf_op jit(solution)/shard_map/ppermute | solution.py:70
  6.9 14.3 %collective-permute-start.1 = (bf16[392,640]{1,0:T(8,128)(2,1)}, bf16[392,640]{1,0:T(8,128)(2,1)}, u32[]{:S(2)}, u32[]{:S(2)}) collective-permute-start(bf16[392,640]{1,0:T(8,128)(2,1)} %get-tuple-element.52.refs_0_), channel_id=1, source_target_pairs={{2,4},{3,5},{4,2},{5,3},{10,12},{11,13},{12,10},{13,11},{18,20},{1... | collective-permute-start | bytes 1505288 | tf_op jit(solution)/shard_map/ppermute | solution.py:70
  8.4 44.5 %collective-permute-start.5 = (bf16[392,640]{1,0:T(8,128)(2,1)}, bf16[392,640]{1,0:T(8,128)(2,1)}, u32[]{:S(2)}, u32[]{:S(2)}) collective-permute-start(bf16[392,640]{1,0:T(8,128)(2,1)} %get-tuple-element.52.refs_0_), channel_id=1, source_target_pairs={{0,1},{1,0},{2,3},{3,2},{4,5},{5,4},{6,7},{7,6},{8,9},{9,8},{10,11... | collective-permute-start | bytes 1505288 | tf_op jit(solution)/shard_map/ppermute | solution.py:32
  13.0 77.9 %collective-permute-start.14 = (bf16[512,2560]{1,0:T(8,128)(2,1)}, bf16[512,2560]{1,0:T(8,128)(2,1)}, u32[]{:S(2)}, u32[]{:S(2)}) collective-permute-start(bf16[512,2560]{1,0:T(8,128)(2,1)} %pad_maximum_fusion.1), channel_id=1, source_target_pairs={{0,1},{1,0},{2,3},{3,2},{4,5},{5,4},{6,7},{7,6},{8,9},{9,8},{10,11... | collective-permute-start | bytes 7864328 | tf_op jit(solution)/shard_map/ppermute | solution.py:32
  21.2 20.7 %collective-permute-start.2 = (bf16[392,640]{1,0:T(8,128)(2,1)}, bf16[392,640]{1,0:T(8,128)(2,1)S(1)}, u32[]{:S(2)}, u32[]{:S(2)}) collective-permute-start(bf16[392,640]{1,0:T(8,128)(2,1)} %collective-permute-done.1), channel_id=1, source_target_pairs={{4,6},{5,7},{2,0},{3,1},{12,14},{13,15},{10,8},{11,9},{20,22},{21,... | collective-permute-start | bytes 1505288 | tf_op jit(solution)/shard_map/ppermute | solution.py:70
  22.5 30.2 %collective-permute-start.4 = (bf16[392,640]{1,0:T(8,128)(2,1)S(1)}, bf16[392,640]{1,0:T(8,128)(2,1)S(1)}, u32[]{:S(2)}, u32[]{:S(2)}) collective-permute-start(bf16[392,640]{1,0:T(8,128)(2,1)S(1)} %collective-permute-done.3), channel_id=1, source_target_pairs={{4,6},{5,7},{2,0},{3,1},{12,14},{13,15},{10,8},{11,9},{20,22},{21,... | collective-permute-start | bytes 1505288 | tf_op jit(solution)/shard_map/ppermute | solution.py:70
  24.5 29.3 %collective-permute-start.12 = (bf16[4,16,640]{2,1,0:T(8,128)(2,1)S(1)}, bf16[4,16,640]{2,1,0:T(8,128)(2,1)}, u32[]{:S(2)}, u32[]{:S(2)}) collective-permute-start(bf16[4,16,640]{2,1,0:T(8,128)(2,1)S(1)} %pad_maximum_fusion.11), channel_id=1, source_target_pairs={{0,2},{1,3},{2,0},{3,1},{4,6},{5,7},{6,4},{7,5},{8,10},{9,11},{10,... | collective-permute-start | bytes 245768 | tf_op jit(solution)/shard_map/ppermute | solution.py:32
  41.9 16.1 %collective-permute-start.6 = (bf16[392,640]{1,0:T(8,128)(2,1)}, bf16[392,640]{1,0:T(8,128)(2,1)}, u32[]{:S(2)}, u32[]{:S(2)}) collective-permute-start(bf16[392,640]{1,0:T(8,128)(2,1)} %collective-permute-done.refs_1_), channel_id=1, source_target_pairs={{0,1},{1,0},{2,3},{3,2},{4,5},{5,4},{6,7},{7,6},{8,9},{9,8},{10,11... | collective-permute-start | bytes 1505288 | tf_op jit(solution)/shard_map/ppermute | solution.py:32
  53.7 13.3 %collective-permute-start.10 = (bf16[392,640]{1,0:T(8,128)(2,1)S(1)}, bf16[392,640]{1,0:T(8,128)(2,1)}, u32[]{:S(2)}, u32[]{:S(2)}) collective-permute-start(bf16[392,640]{1,0:T(8,128)(2,1)S(1)} %get-tuple-element.70.refs_0_), channel_id=1, source_target_pairs={{0,2},{1,3},{2,0},{3,1},{4,6},{5,7},{6,4},{7,5},{8,10},{9,11},{10,... | collective-permute-start | bytes 1505288 | tf_op jit(solution)/shard_map/ppermute | solution.py:70
  58.1 26.2 %collective-permute-start.21 = (bf16[392,640]{1,0:T(8,128)(2,1)S(1)}, bf16[392,640]{1,0:T(8,128)(2,1)}, u32[]{:S(2)}, u32[]{:S(2)}) collective-permute-start(bf16[392,640]{1,0:T(8,128)(2,1)S(1)} %get-tuple-element.70.refs_0_), channel_id=1, source_target_pairs={{2,4},{3,5},{4,2},{5,3},{10,12},{11,13},{12,10},{13,11},{18,20},{1... | collective-permute-start | bytes 1505288 | tf_op jit(solution)/shard_map/ppermute | solution.py:70
  67.0 18.5 %collective-permute-start.15 = (bf16[392,640]{1,0:T(8,128)(2,1)}, bf16[392,640]{1,0:T(8,128)(2,1)}, u32[]{:S(2)}, u32[]{:S(2)}) collective-permute-start(bf16[392,640]{1,0:T(8,128)(2,1)} %collective-permute-done.10.refs_1_), channel_id=1, source_target_pairs={{2,4},{3,5},{4,2},{5,3},{10,12},{11,13},{12,10},{13,11},{18,20},{1... | collective-permute-start | bytes 1505288 | tf_op jit(solution)/shard_map/ppermute | solution.py:70
  81.6 9.3 %collective-permute-start.9 = (bf16[2,196,512]{2,1,0:T(8,128)(2,1)}, bf16[2,196,512]{2,1,0:T(8,128)(2,1)S(1)}, u32[]{:S(2)}, u32[]{:S(2)}) collective-permute-start(bf16[2,196,512]{2,1,0:T(8,128)(2,1)} %shard_map.140.own), channel_id=1, source_target_pairs={{0,1},{1,0},{2,3},{3,2},{4,5},{5,4},{6,7},{7,6},{8,9},{9,8},{10,11... | collective-permute-start | bytes 1204232 | tf_op jit(solution)/shard_map/ppermute | solution.py:32
  84.3 20.7 %collective-permute-start.22 = (bf16[392,640]{1,0:T(8,128)(2,1)}, bf16[392,640]{1,0:T(8,128)(2,1)}, u32[]{:S(2)}, u32[]{:S(2)}) collective-permute-start(bf16[392,640]{1,0:T(8,128)(2,1)} %collective-permute-done.21), channel_id=1, source_target_pairs={{4,6},{5,7},{2,0},{3,1},{12,14},{13,15},{10,8},{11,9},{20,22},{21,... | collective-permute-start | bytes 1505288 | tf_op jit(solution)/shard_map/ppermute | solution.py:70
  85.6 25.3 %collective-permute-start.23 = (bf16[392,640]{1,0:T(8,128)(2,1)}, bf16[392,640]{1,0:T(8,128)(2,1)}, u32[]{:S(2)}, u32[]{:S(2)}) collective-permute-start(bf16[392,640]{1,0:T(8,128)(2,1)} %collective-permute-done.15), channel_id=1, source_target_pairs={{4,6},{5,7},{2,0},{3,1},{12,14},{13,15},{10,8},{11,9},{20,22},{21,... | collective-permute-start | bytes 1505288 | tf_op jit(solution)/shard_map/ppermute | solution.py:70
  89.3 22.9 %collective-permute-start.28 = (bf16[8,16,640]{2,1,0:T(8,128)(2,1)S(1)}, bf16[8,16,640]{2,1,0:T(8,128)(2,1)S(1)}, u32[]{:S(2)}, u32[]{:S(2)}) collective-permute-start(bf16[8,16,640]{2,1,0:T(8,128)(2,1)S(1)} %pad_maximum_fusion.7), channel_id=1, source_target_pairs={{0,8},{8,0},{16,24},{24,16},{1,9},{9,1},{17,25},{25,17},{2,10},{10... | collective-permute-start | bytes 491528 | tf_op jit(solution)/shard_map/ppermute | solution.py:32
  98.4 14.9 %collective-permute-start.16 = (bf16[2,196,640]{2,1,0:T(8,128)(2,1)}, bf16[2,196,640]{2,1,0:T(8,128)(2,1)S(1)}, u32[]{:S(2)}, u32[]{:S(2)}) collective-permute-start(bf16[2,196,640]{2,1,0:T(8,128)(2,1)} %get-tuple-element.66), channel_id=1, source_target_pairs={{6,4},{7,5},{0,2},{1,3},{14,12},{15,13},{8,10},{9,11},{22,20},{23,... | collective-permute-start | bytes 1505288 | tf_op jit(solution)/shard_map/ppermute | solution.py:70
  105.0 12.8 %collective-permute-start.24 = (bf16[392,640]{1,0:T(8,128)(2,1)S(1)}, bf16[392,640]{1,0:T(8,128)(2,1)S(1)}, u32[]{:S(2)}, u32[]{:S(2)}) collective-permute-start(bf16[392,640]{1,0:T(8,128)(2,1)S(1)} %get-tuple-element.70.refs_0_), channel_id=1, source_target_pairs={{0,1},{1,0},{2,3},{3,2},{4,5},{5,4},{6,7},{7,6},{8,9},{9,8},{10,11... | collective-permute-start | bytes 1505288 | tf_op jit(solution)/shard_map/ppermute | solution.py:32
  105.0 14.4 %collective-permute-start.25 = (bf16[392,640]{1,0:T(8,128)(2,1)}, bf16[392,640]{1,0:T(8,128)(2,1)S(1)}, u32[]{:S(2)}, u32[]{:S(2)}) collective-permute-start(bf16[392,640]{1,0:T(8,128)(2,1)} %collective-permute-done.10.refs_1_), channel_id=1, source_target_pairs={{0,1},{1,0},{2,3},{3,2},{4,5},{5,4},{6,7},{7,6},{8,9},{9,8},{10,11... | collective-permute-start | bytes 1505288 | tf_op jit(solution)/shard_map/ppermute | solution.py:32
  110.9 9.2 %collective-permute-start.26 = (bf16[392,640]{1,0:T(8,128)(2,1)S(1)}, bf16[392,640]{1,0:T(8,128)(2,1)S(1)}, u32[]{:S(2)}, u32[]{:S(2)}) collective-permute-start(bf16[392,640]{1,0:T(8,128)(2,1)S(1)} %add.239.refs_2_), channel_id=1, source_target_pairs={{0,1},{1,0},{2,3},{3,2},{4,5},{5,4},{6,7},{7,6},{8,9},{9,8},{10,11... | collective-permute-start | bytes 1505288 | tf_op jit(solution)/shard_map/ppermute | solution.py:32
  113.3 21.6 %collective-permute-start.19 = (bf16[2,196,640]{2,1,0:T(8,128)(2,1)S(1)}, bf16[2,196,640]{2,1,0:T(8,128)(2,1)S(1)}, u32[]{:S(2)}, u32[]{:S(2)}) collective-permute-start(bf16[2,196,640]{2,1,0:T(8,128)(2,1)S(1)} %copy-done.14), channel_id=1, source_target_pairs={{6,4},{7,5},{0,2},{1,3},{14,12},{15,13},{8,10},{9,11},{22,20},{23,... | collective-permute-start | bytes 1505288 | tf_op jit(solution)/shard_map/ppermute | solution.py:70
  117.8 29.0 %collective-permute-start.30 = (bf16[8,32,640]{2,1,0:T(8,128)(2,1)S(1)}, bf16[8,32,640]{2,1,0:T(8,128)(2,1)S(1)}, u32[]{:S(2)}, u32[]{:S(2)}) collective-permute-start(bf16[8,32,640]{2,1,0:T(8,128)(2,1)S(1)} %pad_maximum_fusion.4), channel_id=1, source_target_pairs={{0,16},{8,24},{16,0},{24,8},{1,17},{9,25},{17,1},{25,9},{2,18},{10... | collective-permute-start | bytes 983048 | tf_op jit(solution)/shard_map/ppermute | solution.py:32
  119.4 16.3 %collective-permute-start.17 = (bf16[2,196,640]{2,1,0:T(8,128)(2,1)S(1)}, bf16[2,196,640]{2,1,0:T(8,128)(2,1)S(1)}, u32[]{:S(2)}, u32[]{:S(2)}) collective-permute-start(bf16[2,196,640]{2,1,0:T(8,128)(2,1)S(1)} %add_convert_fusion.5), channel_id=1, source_target_pairs={{2,4},{3,5},{4,2},{5,3},{10,12},{11,13},{12,10},{13,11},{18,20},{1... | collective-permute-start | bytes 1505288 | tf_op jit(solution)/shard_map/ppermute | solution.py:70
  135.0 17.9 %collective-permute-start.20 = (bf16[2,196,640]{2,1,0:T(8,128)(2,1)S(1)}, bf16[2,196,640]{2,1,0:T(8,128)(2,1)S(1)}, u32[]{:S(2)}, u32[]{:S(2)}) collective-permute-start(bf16[2,196,640]{2,1,0:T(8,128)(2,1)S(1)} %add_convert_fusion.3), channel_id=1, source_target_pairs={{2,4},{3,5},{4,2},{5,3},{10,12},{11,13},{12,10},{13,11},{18,20},{1... | collective-permute-start | bytes 1505288 | tf_op jit(solution)/shard_map/ppermute | solution.py:70
  135.8 17.1 %collective-permute-start.18 = (bf16[2,196,640]{2,1,0:T(8,128)(2,1)S(1)}, bf16[2,196,640]{2,1,0:T(8,128)(2,1)S(1)}, u32[]{:S(2)}, u32[]{:S(2)}) collective-permute-start(bf16[2,196,640]{2,1,0:T(8,128)(2,1)S(1)} %add_convert_fusion.4), channel_id=1, source_target_pairs={{0,2},{1,3},{2,0},{3,1},{4,6},{5,7},{6,4},{7,5},{8,10},{9,11},{10,... | collective-permute-start | bytes 1505288 | tf_op jit(solution)/shard_map/ppermute | solution.py:70
  144.6 17.5 %collective-permute-start.31 = (bf16[2,196,640]{2,1,0:T(8,128)(2,1)}, bf16[2,196,640]{2,1,0:T(8,128)(2,1)S(1)}, u32[]{:S(2)}, u32[]{:S(2)}) collective-permute-start(bf16[2,196,640]{2,1,0:T(8,128)(2,1)} %shard_map.143), channel_id=1, source_target_pairs={{6,4},{7,5},{0,2},{1,3},{14,12},{15,13},{8,10},{9,11},{22,20},{23,... | collective-permute-start | bytes 1505288 | tf_op jit(solution)/shard_map/ppermute | solution.py:70
  154.6 12.8 %collective-permute-start.34 = (bf16[4,80,512]{2,1,0:T(8,128)(2,1)S(1)}, bf16[4,80,512]{2,1,0:T(8,128)(2,1)S(1)}, u32[]{:S(2)}, u32[]{:S(2)}) collective-permute-start(bf16[4,80,512]{2,1,0:T(8,128)(2,1)S(1)} %get-tuple-element.91), channel_id=1, source_target_pairs={{0,1},{1,0},{2,3},{3,2},{4,5},{5,4},{6,7},{7,6},{8,9},{9,8},{10,11... | collective-permute-start | bytes 983048 | tf_op jit(solution)/shard_map/ppermute | solution.py:32
  162.1 18.3 %collective-permute-start.37 = (bf16[2,196,640]{2,1,0:T(8,128)(2,1)S(1)}, bf16[2,196,640]{2,1,0:T(8,128)(2,1)S(1)}, u32[]{:S(2)}, u32[]{:S(2)}) collective-permute-start(bf16[2,196,640]{2,1,0:T(8,128)(2,1)S(1)} %copy-done.17), channel_id=1, source_target_pairs={{6,4},{7,5},{0,2},{1,3},{14,12},{15,13},{8,10},{9,11},{22,20},{23,... | collective-permute-start | bytes 1505288 | tf_op jit(solution)/shard_map/ppermute | solution.py:70
  166.5 13.8 %collective-permute-start.32 = (bf16[2,196,640]{2,1,0:T(8,128)(2,1)S(1)}, bf16[2,196,640]{2,1,0:T(8,128)(2,1)S(1)}, u32[]{:S(2)}, u32[]{:S(2)}) collective-permute-start(bf16[2,196,640]{2,1,0:T(8,128)(2,1)S(1)} %add_convert_fusion.2), channel_id=1, source_target_pairs={{2,4},{3,5},{4,2},{5,3},{10,12},{11,13},{12,10},{13,11},{18,20},{1... | collective-permute-start | bytes 1505288 | tf_op jit(solution)/shard_map/ppermute | solution.py:70
  167.6 12.7 %collective-permute-start.35 = (bf16[2,80,512]{2,1,0:T(8,128)(2,1)S(1)}, bf16[2,80,512]{2,1,0:T(8,128)(2,1)S(1)}, u32[]{:S(2)}, u32[]{:S(2)}) collective-permute-start(bf16[2,80,512]{2,1,0:T(8,128)(2,1)S(1)} %slice.188), channel_id=1, source_target_pairs={{0,2},{1,3},{2,0},{3,1},{4,6},{5,7},{6,4},{7,5},{8,10},{9,11},{10,... | collective-permute-start | bytes 491528 | tf_op jit(solution)/shard_map/ppermute | solution.py:32
  180.5 19.4 %collective-permute-start.38 = (bf16[2,196,640]{2,1,0:T(8,128)(2,1)S(1)}, bf16[2,196,640]{2,1,0:T(8,128)(2,1)S(1)}, u32[]{:S(2)}, u32[]{:S(2)}) collective-permute-start(bf16[2,196,640]{2,1,0:T(8,128)(2,1)S(1)} %add_convert_fusion), channel_id=1, source_target_pairs={{2,4},{3,5},{4,2},{5,3},{10,12},{11,13},{12,10},{13,11},{18,20},{1... | collective-permute-start | bytes 1505288 | tf_op jit(solution)/shard_map/ppermute | solution.py:70
  181.4 18.5 %collective-permute-start.33 = (bf16[2,196,640]{2,1,0:T(8,128)(2,1)S(1)}, bf16[2,196,640]{2,1,0:T(8,128)(2,1)S(1)}, u32[]{:S(2)}, u32[]{:S(2)}) collective-permute-start(bf16[2,196,640]{2,1,0:T(8,128)(2,1)S(1)} %add_convert_fusion.1), channel_id=1, source_target_pairs={{0,2},{1,3},{2,0},{3,1},{4,6},{5,7},{6,4},{7,5},{8,10},{9,11},{10,... | collective-permute-start | bytes 1505288 | tf_op jit(solution)/shard_map/ppermute | solution.py:70
  185.6 14.3 %collective-permute-start.36 = (bf16[80,512]{1,0:T(8,128)(2,1)S(1)}, bf16[80,512]{1,0:T(8,128)(2,1)S(1)}, u32[]{:S(2)}, u32[]{:S(2)}) collective-permute-start(bf16[80,512]{1,0:T(8,128)(2,1)S(1)} %slice_bitcast_fusion.3), channel_id=1, source_target_pairs={{0,4},{1,5},{2,6},{3,7},{4,0},{5,1},{6,2},{7,3},{8,12},{9,13},{10,... | collective-permute-start | bytes 245768 | tf_op jit(solution)/shard_map/ppermute | solution.py:32
  (53 other events, 780.2 us)

commit v3 on v2

--- a/solution.py
+++ b/solution.py
@@ -14,8 +14,13 @@
 CHIPS = 4
 EXTRA = 16
 LANES = 256
-HEAD_SPREAD = True
-SPLIT_OUT = True
+OUT_AFTER = False
+PARTNER_EARLY = False
+HEAD_LATE = True
+REP_EARLY = True
+SECOND_EARLY = True
+FIRST_DEMAND = False
+DEMAND = True
 VMEM_A = 56
 STAGES = 2
 VMEM_B = 56
@@ -75,7 +80,7 @@
 
 
 def attend_kernel(heads, order, length, *refs):
-    shards, (gain, w_q, w_kv, q_bias, v_bias, context, normed, q_rows, kv_rows, sems) = refs[:8], refs[8:]
+    shards, (gain, w_q, w_k, w_v, q_bias, v_bias, context, normed, q_rows, kv_rows, sems) = refs[:8], refs[8:]
     width = shards[0].shape[1]
     group, count = context.shape[:2]
     copies = []
@@ -85,7 +90,8 @@
         copies.append(
             (
                 pltpu.make_async_copy(w_q.at[rows, :], q_rows.at[here, :], sems.at[0, k]),
-                pltpu.make_async_copy(w_kv.at[rows, :], kv_rows.at[here, :], sems.at[1, k]),
+                pltpu.make_async_copy(w_k.at[rows, :], kv_rows.at[here, :HS], sems.at[1, k]),
+                pltpu.make_async_copy(w_v.at[rows, :], kv_rows.at[here, HS:], sems.at[2, k]),
             )
         )
         for copy in copies[-1]:
@@ -131,16 +137,17 @@
             context[g, :, h * HS : (h + 1) * HS] = done[h]
 
 
-def out_kernel(places, own, other, w_own, w_other, *refs):
+def out_kernel(chips, blocks, own, other, w_own, w_other, *refs):
     targets, (own_rows, other_rows, own_sems, other_sems) = refs[:-4], refs[-4:]
     group, _, width = targets[0].shape
     copies = []
     for k in range(len(targets)):
-        columns = pl.ds(pl.multiple_of(places[k] * width, width), width)
+        here = pl.ds(pl.multiple_of(blocks[k] * width, width), width)
+        there = pl.ds(pl.multiple_of(chips[k] * width, width), width)
         copies.append(
             (
-                pltpu.make_async_copy(w_own.at[:, columns], own_rows.at[k], own_sems.at[k]),
-                pltpu.make_async_copy(w_other.at[:, columns], other_rows.at[k], other_sems.at[k]),
+                pltpu.make_async_copy(w_own.at[:, here], own_rows.at[k], own_sems.at[k]),
+                pltpu.make_async_copy(w_other.at[:, there], other_rows.at[k], other_sems.at[k]),
             )
         )
         for copy in copies[-1]:
@@ -165,7 +172,9 @@
         for g in range(group):
             wide = lambda ref: ref[g].astype(jnp.float32)
             summed = wide(kept) + (wide(partner) + wide(middle))
-            rounded = (wide(masked) + summed).astype(jnp.bfloat16)
+            count = summed.shape[0]
+            rows = masked[...].astype(jnp.float32)[g * count : (g + 1) * count]
+            rounded = (rows + summed).astype(jnp.bfloat16)
             hiddens[i][g] = rounded
             value = rounded.astype(jnp.float32)
             scaled = (value * gain[...]).astype(jnp.bfloat16)
@@ -210,7 +219,7 @@
         bit = 1 << level
         stay = [k for k in range(8) if not k & bit]
         move = [k for k in range(8) if k & bit]
-        got = yield swapped(jnp.stack([blocks[k] for k in move]), "tp", level)
+        got = yield jnp.stack([blocks[k] for k in move]), "tp", level
         merged = [None] * 8
         for place, k in enumerate(stay):
             merged[k] = blocks[k]
@@ -219,12 +228,12 @@
         blocks = jnp.stack(merged)
     if shared:
         for level in range(parts.bit_length() - 1):
-            got = yield swapped(blocks, "rep", level)
+            got = yield blocks, "rep", level
             lower = jnp.bitwise_and(jnp.right_shift(rep, level), 1) == 0
             blocks = jnp.concatenate(
                 [jnp.where(lower, blocks, got), jnp.where(lower, got, blocks)], axis=1
             )
-    yield blocks.reshape(8 * entries, width)
+    yield blocks.reshape(8 * entries, width), None, None
 
 
 def on_line(
@@ -253,13 +262,11 @@
         [chip, jnp.bitwise_xor(chip, 1), jnp.where(first_half, 2, 1), jnp.where(first_half, 3, 0)]
     ).astype(jnp.int32)
     places = jnp.concatenate([line * CORES + core, line * CORES + (1 - core)])
-    by_request = embeds.reshape(requests, L, width)
-    chosen = remask.reshape(requests, L, 1) == 1
-    masked, flat = [], []
+    masked = []
     for first, end in GROUPS:
         rows = slice(first * L, end * L)
-        flat.append(jnp.where(remask[rows, None] == 1, mask_vec[None, :], embeds[rows]))
-        masked.append(jnp.where(chosen[first:end], mask_vec[None, None, :], by_request[first:end]))
+        masked.append(jnp.where(remask[rows, None] == 1, mask_vec[None, :], embeds[rows]))
+        embeds = after(embeds, masked[0])
     sizes = [end - first for first, end in GROUPS]
 
     def of_core(matrix, wanted):
@@ -271,35 +278,31 @@
             axis=1,
         )
 
-    w_own = of_core(w_out, core)
-    w_other = swapped(of_core(w_out, 1 - core), "tp", 0)
-    w_kv = jnp.concatenate([w_key, w_value], axis=1)
     gain = attn_gain.astype(jnp.float32).reshape(8, width)
     q_row = q_bias.astype(jnp.float32)[None, :]
     v_row = v_bias.astype(jnp.float32)[None, :]
     gain_local = lax.dynamic_slice_in_dim(head_gain, index * width, width).astype(jnp.float32)[None, :]
 
     steps = head_steps(w_head, index)
-    moving = [next(steps)]
-
-    def step_head():
-        try:
-            moving[0] = steps.send(moving[0])
-        except StopIteration:
-            pass
+
+    def travelled(value, axis, level):
+        return value if axis is None else swapped(value, axis, level)
+
+    def next_step(step, arrived):
+        return step if step[1] is None else steps.send(arrived)
 
     def attend(i):
         first, end = GROUPS[i]
         return pl.pallas_call(
             functools.partial(attend_kernel, heads),
             out_shape=jax.ShapeDtypeStruct((sizes[i], L, heads * HS), jnp.bfloat16),
-            in_specs=[whole(pltpu.SMEM)] * 2 + [whole()] * 9 + [whole(pl.ANY)] * 2 + [whole()] * 2,
+            in_specs=[whole(pltpu.SMEM)] * 2 + [whole()] * 9 + [whole(pl.ANY)] * 3 + [whole()] * 2,
             out_specs=whole(),
             scratch_shapes=[
                 pltpu.VMEM((sizes[i] * L, 8 * width), jnp.bfloat16),
                 pltpu.VMEM((8 * width, heads * HS), jnp.bfloat16),
                 pltpu.VMEM((8 * width, 2 * HS), jnp.bfloat16),
-                pltpu.SemaphoreType.DMA((2, 8)),
+                pltpu.SemaphoreType.DMA((3, 8)),
             ],
             compiler_params=pltpu.CompilerParams(vmem_limit_bytes=VMEM_A * 2**20),
             cost_estimate=pl.CostEstimate(
@@ -307,14 +310,15 @@
                 bytes_accessed=sizes[i] * 12 * 2**20,
                 transcendentals=sizes[i] * heads * L * L,
             ),
-        )(places, lengths[first:end], *shards[i], gain, w_query, w_kv, q_row, v_row)
-
-    def out(size, wanted, *operands):
-        count = wanted.shape[0]
+        )(places, lengths[first:end], *shards[i], gain, w_query, w_key, w_value, q_row, v_row)
+
+    def out(size, wanted, context, other):
+        chips, blocks = wanted
+        count = chips.shape[0]
         return pl.pallas_call(
             out_kernel,
             out_shape=[jax.ShapeDtypeStruct((size, L, width), jnp.bfloat16)] * count,
-            in_specs=[whole(pltpu.SMEM)] + [whole()] * 2 + [whole(pl.ANY)] * 2,
+            in_specs=[whole(pltpu.SMEM)] * 2 + [whole()] * 2 + [whole(pl.ANY)] * 2,
             out_specs=[whole()] * count,
             scratch_shapes=[
                 pltpu.VMEM((count, heads * HS, width), jnp.bfloat16),
@@ -328,7 +332,7 @@
                 bytes_accessed=size * 4 * count * 2**20,
                 transcendentals=0,
             ),
-        )(wanted, *operands)
+        )(chips, blocks, context, other, w_out, w_other)
 
     def head(groups, chunks):
         count = sum(groups)
@@ -342,10 +346,9 @@
             cost_estimate=pl.CostEstimate(
                 flops=count * 2 * L * width * 8 * entries, bytes_accessed=count * 3 * 2**20, transcendentals=0
             ),
-        )(*[value for chunk in chunks for value in chunk], gain_local, moving[0])
+        )(*[value for chunk in chunks for value in chunk], gain_local, w_rows)
 
     add = lambda *terms: sum(term.astype(jnp.float32) for term in terms).astype(jnp.bfloat16)
-    last = len(GROUPS) - 1
     own, inward, middle, partner = ({} for _ in range(4))
 
     def advance_middle(i, *earlier):
@@ -369,68 +372,85 @@
     def both_cores(*mine):
         return [*mine, *(swapped(shard, "tp", 0) for shard in mine)]
 
-    own = flat[0]
+    tables = [(line[here], places[:4][here]) for here in (slice(0, 4), slice(3, 4), slice(0, 3))]
+    own = masked[0]
     partner, middle = permuted(own, PARTNER), permuted(own, MIDDLE)
+    step = next(steps)
+    moved = travelled(*step)
+    theirs = of_core(w_out, 1 - core)
+    partner, middle, moved, theirs = lax.optimization_barrier((partner, middle, moved, theirs))
     far_middle, near_out = permuted(partner, MIDDLE), permuted(middle, OUTWARD)
-    if HEAD_SPREAD:
-        moving[0] = after(moving[0], partner)
-        step_head()
-        moving[0] = after(moving[0], far_middle)
-        step_head()
+    step = next_step(step, moved)
+    moved = travelled(*step)
+    far_middle, near_out, moved, ready = lax.optimization_barrier(
+        (far_middle, near_out, moved, (places, line, lengths, gain, q_row, v_row, gain_local, tables))
+    )
+    places, line, lengths, gain, q_row, v_row, gain_local, tables = ready
     far_out = permuted(far_middle, OUTWARD)
-    shards = [both_cores(own, partner, middle + near_out, far_middle + far_out)]
-
-    own = after(flat[1], far_middle)
-    middle = permuted(own, MIDDLE)
-    own = after(own, far_out)
-    partner = permuted(own, PARTNER)
-    shards[0] = after(shards[0], own)
+    own = after(masked[1], partner)
+    next_partner = permuted(own, PARTNER)
+    next_middle = permuted(after(own, far_middle), MIDDLE)
+    step = next_step(step, moved)
+    if SECOND_EARLY:
+        far_out, next_middle, next_partner = lax.optimization_barrier((far_out, next_middle, next_partner))
+    else:
+        far_out, next_middle = lax.optimization_barrier((far_out, next_middle))
+    w_other = swapped(theirs, "tp", 0)
+    shards = [both_cores(masked[0], partner, middle + near_out, far_middle + far_out)]
+
+    partner, middle = next_partner, next_middle
+    far_middle, near_out = permuted(partner, MIDDLE), permuted(middle, OUTWARD)
+    shards[0] = after(shards[0], partner, middle)
     context = attend(0)
-    other = after(swapped(context, "tp", 0), partner, moving[0])
-    step_head()
-    far_middle, near_out = permuted(partner, MIDDLE), permuted(after(middle, partner), OUTWARD)
-    self_part, partner_part, near, far = out(sizes[0], line, context, other, w_own, w_other)
-    far_out = permuted(far_middle, OUTWARD)
+    other = after(swapped(context, "tp", 0), far_middle, near_out)
+    self_part, partner_part, near, far = out(sizes[0], tables[0], context, other)
+    far_out = permuted(after(far_middle, context), OUTWARD)
+    far_out, near = lax.optimization_barrier((far_out, near))
+    far_in, near_in = permuted(far, INWARD), permuted(near, INWARD)
+    moved = travelled(after(step[0], far_middle), *step[1:])
     shards.append(both_cores(own, partner, middle + near_out, far_middle + far_out))
-    far_in = permuted(after(far, far_middle), INWARD)
+
+    shards[1] = after(shards[1], near)
+    context = attend(1)
+    context, far_in = lax.optimization_barrier((context, far_in))
     far = add(far, far_in)
     far_middle = permuted(far, MIDDLE)
-    near_in = permuted(after(near, far_in), INWARD)
-
-    shards[1] = after(shards[1], far, moving[0])
-    step_head()
-    context = attend(1)
-    other = after(swapped(context, "tp", 0), far_middle, near_in)
-    partner_part, near = add(partner_part, far_middle), add(near, near_in)
-    first_parts = [self_part, permuted(partner_part, PARTNER), permuted(near, MIDDLE), masked[0]]
-    other = after(other, partner_part, near)
-    if SPLIT_OUT:
-        (far,) = out(sizes[1], line[3:], context, other, w_own, w_other)
-        far_in = permuted(far, INWARD)
-        other = after(other, far)
-        self_part, partner_part, near = out(sizes[1], line[:3], context, other, w_own, w_other)
-    else:
-        self_part, partner_part, near, far = out(sizes[1], line, context, other, w_own, w_other)
-        far_in = permuted(far, INWARD)
-    far_middle = permuted(add(far, after(far_in, first_parts)), MIDDLE)
-    near_in = permuted(after(near, far_in), INWARD)
-    while moving[0].shape != (8 * entries, width):
-        step_head()
-    hidden_first, kept, sent = head(sizes[:1], [after(first_parts, near)])
-    from_partner = permuted(add(partner_part, far_middle), PARTNER)
-    near_middle = permuted(add(near, after(near_in, far_middle)), MIDDLE)
-    sent = swapped(sent, "tp", 0)
-    held = add_sums(kept, sent)
-    move = swapped(held[2:], "tp", 1)
-    held = add_sums(held[:2], move)
-    move = swapped(held[1], "tp", 2)
-    from_partner = after(from_partner, move)
-    hidden, kept, sent = head(sizes[1:], [(self_part, from_partner, near_middle, masked[1])])
+    step = next_step(step, after(moved, context))
+    moved = travelled(*step)
+    other = swapped(context, "tp", 0)
+    first_far, first_near, first_partner, first_self = far_middle, add(near, near_in), partner_part, self_part
+    near_in_first = near_in
+    (far,) = out(sizes[1], tables[1], context, other)
+    far_in = permuted(far, INWARD)
+    first_partner = add(first_partner, after(first_far, far))
+    first_near = after(first_near, first_partner)
+    first_parts = [first_self, permuted(first_partner, PARTNER), permuted(first_near, MIDDLE), masked[0]]
+    step = next_step(step, moved)
+    moved = travelled(*step)
+    other = after(other, far, *(first_parts[1:3] if OUT_AFTER else ()))
+    self_part, partner_part, near = out(sizes[1], tables[2], context, other)
+    far_in = after(far_in, near, *((moved,) if REP_EARLY else ()), *((first_far, near_in_first) if DEMAND else ()))
+    far = add(far, far_in)
+    far_middle = permuted(far, MIDDLE)
+    near_in = permuted(after(near, far), INWARD)
+    while step[1] is not None:
+        step = next_step(step, moved)
+        moved = travelled(*step)
+    w_rows = step[0]
+    partner_sum = add(partner_part, after(far_middle, *(first_parts[1:3] if FIRST_DEMAND else ())))
+    from_partner = permuted(partner_sum, PARTNER)
+    near_middle = permuted(add(near, after(near_in, partner_sum)), MIDDLE)
+    if HEAD_LATE:
+        first_parts = after(first_parts, partner_sum)
+    hidden_first, kept, sent = head(sizes[:1], [first_parts])
+    near_middle = after(near_middle, kept)
+    hidden, kept_last, sent_last = head(sizes[1:], [(self_part, from_partner, near_middle, masked[1])])
     hiddens = [hidden_first, hidden]
-    held = add_sums(held[0], move)
-    held_last = add_sums(kept, swapped(sent, "tp", 0))
-    held_last = add_sums(held_last[:2], swapped(held_last[2:], "tp", 1))
-    held_last = add_sums(held_last[0], swapped(held_last[1], "tp", 2))
+    kept = jnp.concatenate([kept, kept_last], axis=2)
+    sent = jnp.concatenate([sent, sent_last], axis=2)
+    held = add_sums(kept, swapped(sent, "tp", 0))
+    held = add_sums(held[:2], swapped(held[2:], "tp", 1))
+    held = add_sums(held[0], swapped(held[1], "tp", 2))
 
     def finished(held):
         held = held.astype(jnp.float32)
@@ -439,10 +459,7 @@
         top = jnp.max(logits, axis=0)
         return logits, jnp.stack([top, jnp.sum(jnp.exp(logits - top[None, :]), axis=0)])
 
-    logits, pairs = finished(held)
-    logits_last, pairs_last = finished(held_last)
-    logits = jnp.concatenate([logits, logits_last], axis=1)
-    pair = jnp.concatenate([pairs, pairs_last], axis=1)
+    logits, pair = finished(held)
     for level in range(3):
         pair = jnp.stack(combine_pair(pair, swapped(pair, "tp", level)))
     logprob = logits - (pair[0] + jnp.log(pair[1]))[None, :]

time: 228 us -> 216 us (0.947)
  starting transfers between devices: 67.2 us -> 52.7 us
  waiting for transfers between devices: 77.8 us -> 91.6 us
  local copies, waits for them, and re-layouts: 16.7 us -> 9.7 us
  other arithmetic: 17.4 us -> 12.8 us
    ppermute x20, waiting for transfers between devices: 29.1 us -> 52.3 us  [permuted(): return lax.ppermute(value, 'tp', pairs)]
    ppermute x25 -> x22, starting transfers between devices: 27.9 us -> 17.9 us  [swapped(): return lax.ppermute(value, axis, pairs)]
    ppermute x25 -> x22, waiting for transfers between devices: 48.7 us -> 39.4 us  [swapped(): return lax.ppermute(value, axis, pairs)]
    ppermute x20, starting transfers between devices: 39.2 us -> 34.7 us  [permuted(): return lax.ppermute(value, 'tp', pairs)]
    convert_element_type x6, other arithmetic: 0.77 us -> 3.15 us  [on_line(): sum((term.astype(jnp.float32) for term in terms)).astype(jnp.bfloat16)]
    unnamed x81 -> x72, local copies, waits for them, and re-layouts: 5.57 us -> 3.5 us
  transfers between devices with their start and end apart: 45 -> 42, of which waited for: 15 -> 17; matrix products, arithmetic and copies ran while one was open for 11% -> 7% of each run, Pallas kernels for 20% -> 21%
where the time goes in v3:
time: 216 us; the launch traced here: 215 us
  waiting for transfers between devices  91.6 us (42%)
  starting transfers between devices  52.7 us (24%)
  Pallas kernels  46.8 us (22%)
  other arithmetic  12.8 us (6%)
  local copies, waits for them, and re-layouts  9.7 us (4%)
    ppermute x20, waiting for transfers between devices, permuted(): return lax.ppermute(value, 'tp', pairs)  52.3 us
    ppermute x22, waiting for transfers between devices, swapped(): return lax.ppermute(value, axis, pairs)  39.4 us
    ppermute x20, starting transfers between devices, permuted(): return lax.ppermute(value, 'tp', pairs)  34.7 us
    pallas_call x2, Pallas kernels, attend(): pl.pallas_call(functools.partial(attend_kernel, heads), out_shape=jax.Sha...  26.2 us
    ppermute x22, starting transfers between devices, swapped(): return lax.ppermute(value, axis, pairs)  17.9 us
    pallas_call x3, Pallas kernels, out(): pl.pallas_call(out_kernel, out_shape=[jax.ShapeDtypeStruct((size, L, widt...  17.1 us
  transfers between devices with their start and end apart: 42, of which 17 were waited for; matrix products, arithmetic and copies ran while one was open for 7% of the time, Pallas kernels for 21%

profile of v3, /device:TPU:0, one launch (start us, length us, event | category | flops | bytes accessed | tf_op | source)
XLA Modules:
  0.0 215.4 jit_solution(3534418938036449229)
XLA Ops:
  2.6 3.1 %collective-permute-start = (bf16[392,640]{1,0:T(8,128)(2,1)S(1)}, bf16[392,640]{1,0:T(8,128)(2,1)S(1)}, u32[]{:S(2)}, u32[]{:S(2)}) collective-permute-start(bf16[392,640]{1,0:T(8,128)(2,1)S(1)} %slice_select_fusion.1.refs_0_.refs_3_), channel_id=1, source_target_pairs={{0,2},{1,3},{2,0},{3,1},{4,6},{5,7},{6,4},{7,5},{8,10},{9,11},{10,... | collective-permute-start | bytes 1505288 | tf_op jit(solution)/shard_map/ppermute | solution.py:75
  7.7 1.9 constant_dynamic-slice_fusion.3
  9.7 1.6 pad_maximum_fusion
  12.0 5.2 %collective-permute-done.refs_1_ = bf16[392,640]{1,0:T(8,128)(2,1)S(1)} collective-permute-done((bf16[392,640]{1,0:T(8,128)(2,1)S(1)}, bf16[392,640]{1,0:T(8,128)(2,1)S(1)}, u32[]{:S(2)}, u32[]{:S(2)}) %collective-permute-start) | collective-permute-done | bytes 501792 | tf_op jit(solution)/shard_map/ppermute | solution.py:75
  22.7 7.7 %collective-permute-start.5 = (bf16[4,16,640]{2,1,0:T(8,128)(2,1)S(1)}, bf16[4,16,640]{2,1,0:T(8,128)(2,1)S(1)}, u32[]{:S(2)}, u32[]{:S(2)}) collective-permute-start(bf16[4,16,640]{2,1,0:T(8,128)(2,1)S(1)} %pad_maximum_fusion.9), channel_id=1, source_target_pairs={{0,2},{1,3},{2,0},{3,1},{4,6},{5,7},{6,4},{7,5},{8,10},{9,11},{10,... | collective-permute-start | bytes 245768 | tf_op jit(solution)/shard_map/ppermute | solution.py:37
  31.1 10.6 %collective-permute-done.5 = bf16[4,16,640]{2,1,0:T(8,128)(2,1)S(1)} collective-permute-done((bf16[4,16,640]{2,1,0:T(8,128)(2,1)S(1)}, bf16[4,16,640]{2,1,0:T(8,128)(2,1)S(1)}, u32[]{:S(2)}, u32[]{:S(2)}) %collective-permute-start.5) | collective-permute-done | bytes 81952 | tf_op jit(solution)/shard_map/ppermute | solution.py:37
  44.1 8.4 %collective-permute-done.8.refs_1_ = bf16[392,640]{1,0:T(8,128)(2,1)S(1)} collective-permute-done((bf16[392,640]{1,0:T(8,128)(2,1)S(1)}, bf16[392,640]{1,0:T(8,128)(2,1)S(1)}, u32[]{:S(2)}, u32[]{:S(2)}) %collective-permute-start.8) | collective-permute-done | bytes 501792 | tf_op jit(solution)/shard_map/ppermute | solution.py:75
  53.0 9.8 %collective-permute-done.6 = bf16[392,640]{1,0:T(8,128)(2,1)S(1)} collective-permute-done((bf16[392,640]{1,0:T(8,128)(2,1)S(1)}, bf16[392,640]{1,0:T(8,128)(2,1)S(1)}, u32[]{:S(2)}, u32[]{:S(2)}) %collective-permute-start.6) | collective-permute-done | bytes 501792 | tf_op jit(solution)/shard_map/ppermute | solution.py:75
  66.7 13.1 %shard_map.140.own = bf16[2,196,512]{2,1,0:T(8,128)(2,1)} custom-call(s32[8]{0:T(128)} %pad_add_fusion.1.order, s32[2]{0:T(128)} %get-tuple-element.188.length, bf16[392,640]{1,0:T(8,128)(2,1)} %copy-done, bf16[392,640]{1,0:T(8,128)(2,1)} %copy-done.18, bf16[392,640]{1,0:T(8,128)(2,1)} %copy-done.8, bf16[392,640]{1,0:T(8,128)(2,1)} %copy-done.10, ...), custom_call_target="tpu_custom_call" | custom-call | flops 3082813440 | bytes 25165824 | tf_op jit(solution)/shard_map/pallas_call | solution.py:296
  83.3 6.7 %shard_map.141 = (bf16[2,196,640]{2,1,0:T(8,128)(2,1)}, bf16[2,196,640]{2,1,0:T(8,128)(2,1)}, bf16[2,196,640]{2,1,0:T(8,128)(2,1)}, bf16[2,196,640]{2,1,0:T(8,128)(2,1)}) custom-call(s32[4]{0:T(128)} %copy-done.32, s32[4]{0:T(128)} %copy-done.31, bf16[2,196,512]{2,1,0:T(8,128)(2,1)} %shard_map.140.own, bf16[2,196,512]{2,1,0:T(8,128)(2,1)} %copy-done.28, ...), custom_call_target="tpu_custom_call" | custom-call | flops 2055208960 | bytes 33554432 | tf_op jit(solution)/shard_map/pallas_call | solution.py:318
  90.0 5.8 %collective-permute-done.17 = bf16[392,640]{1,0:T(8,128)(2,1)S(1)} collective-permute-done((bf16[392,640]{1,0:T(8,128)(2,1)S(1)}, bf16[392,640]{1,0:T(8,128)(2,1)S(1)}, u32[]{:S(2)}, u32[]{:S(2)}) %collective-permute-start.17) | collective-permute-done | bytes 501792 | tf_op jit(solution)/shard_map/ppermute | solution.py:75
  99.0 13.1 %shard_map.142.own = bf16[2,196,512]{2,1,0:T(8,128)(2,1)} custom-call(s32[8]{0:T(128)} %pad_add_fusion.1.order, s32[2]{0:T(128)} %get-tuple-element.189.length, bf16[392,640]{1,0:T(8,128)(2,1)} %copy-done.2, bf16[392,640]{1,0:T(8,128)(2,1)} %copy-done.19, bf16[392,640]{1,0:T(8,128)(2,1)} %copy-done.7, bf16[392,640]{1,0:T(8,128)(2,1)} %copy-done.9, ...), custom_call_target="tpu_custom_call" | custom-call | flops 3082813440 | bytes 25165824 | tf_op jit(solution)/shard_map/pallas_call | solution.py:296
  112.6 3.3 %collective-permute-start.26 = (bf16[2,196,640]{2,1,0:T(8,128)(2,1)S(1)}, bf16[2,196,640]{2,1,0:T(8,128)(2,1)S(1)}, u32[]{:S(2)}, u32[]{:S(2)}) collective-permute-start(bf16[2,196,640]{2,1,0:T(8,128)(2,1)S(1)} %copy-done.14), channel_id=1, source_target_pairs={{6,4},{7,5},{0,2},{1,3},{14,12},{15,13},{8,10},{9,11},{22,20},{23,... | collective-permute-start | bytes 1505288 | tf_op jit(solution)/shard_map/ppermute | solution.py:75
  119.1 4.7 %shard_map.143 = bf16[2,196,640]{2,1,0:T(8,128)(2,1)} custom-call(s32[1]{0:T(128)} %bitcast.15.chips, s32[1]{0:T(128)} %slice.111.blocks, bf16[2,196,512]{2,1,0:T(8,128)(2,1)} %shard_map.142.own, bf16[2,196,512]{2,1,0:T(8,128)(2,1)} %copy-done.11, bf16[512,5120]{1,0:T(8,128)(2,1)} %w_own.5, bf16[512,2560]{1,0:T(8,128)(2,1)} %collective-permute-done.16.w_other), custom_call_target="tpu_custom_call" | custom-call | flops 513802240 | bytes 8388608 | tf_op jit(solution)/shard_map/pallas_call | solution.py:318
  123.8 4.5 %collective-permute-start.28 = (bf16[2,196,640]{2,1,0:T(8,128)(2,1)}, bf16[2,196,640]{2,1,0:T(8,128)(2,1)S(1)}, u32[]{:S(2)}, u32[]{:S(2)}) collective-permute-start(bf16[2,196,640]{2,1,0:T(8,128)(2,1)} %shard_map.143), channel_id=1, source_target_pairs={{6,4},{7,5},{0,2},{1,3},{14,12},{15,13},{8,10},{9,11},{22,20},{23,... | collective-permute-start | bytes 1505288 | tf_op jit(solution)/shard_map/ppermute | solution.py:75
  129.9 5.8 %shard_map.144 = (bf16[2,196,640]{2,1,0:T(8,128)(2,1)}, bf16[2,196,640]{2,1,0:T(8,128)(2,1)}, bf16[2,196,640]{2,1,0:T(8,128)(2,1)}) custom-call(s32[3]{0:T(128)} %pad_add_fusion.2.chips, s32[3]{0:T(128)} %bitcast.67, bf16[2,196,512]{2,1,0:T(8,128)(2,1)} %shard_map.142.own, bf16[2,196,512]{2,1,0:T(8,128)(2,1)} %copy-done.11, bf16[512,5120]{1,0:T(8,128)(2,1)} %w_own.5, ...), custom_call_target="tpu_custom_call" | custom-call | flops 1541406720 | bytes 25165824 | tf_op jit(solution)/shard_map/pallas_call | solution.py:318
  135.8 1.9 collective-permute-done.31
  137.7 1.6 collective-permute-done.28
  140.4 6.4 %collective-permute-start.34 = (bf16[2,196,640]{2,1,0:T(8,128)(2,1)S(1)}, bf16[2,196,640]{2,1,0:T(8,128)(2,1)S(1)}, u32[]{:S(2)}, u32[]{:S(2)}) collective-permute-start(bf16[2,196,640]{2,1,0:T(8,128)(2,1)S(1)} %copy-done.16), channel_id=1, source_target_pairs={{6,4},{7,5},{0,2},{1,3},{14,12},{15,13},{8,10},{9,11},{22,20},{23,... | collective-permute-start | bytes 1505288 | tf_op jit(solution)/shard_map/ppermute | solution.py:75
  149.4 9.5 %collective-permute-done.34 = bf16[2,196,640]{2,1,0:T(8,128)(2,1)S(1)} collective-permute-done((bf16[2,196,640]{2,1,0:T(8,128)(2,1)S(1)}, bf16[2,196,640]{2,1,0:T(8,128)(2,1)S(1)}, u32[]{:S(2)}, u32[]{:S(2)}) %collective-permute-start.34) | collective-permute-done | bytes 501792 | tf_op jit(solution)/shard_map/ppermute | solution.py:75
  160.5 4.9 %collective-permute-start.33 = (bf16[2,196,640]{2,1,0:T(8,128)(2,1)}, bf16[2,196,640]{2,1,0:T(8,128)(2,1)S(1)}, u32[]{:S(2)}, u32[]{:S(2)}) collective-permute-start(bf16[2,196,640]{2,1,0:T(8,128)(2,1)} %add_convert_fusion.1), channel_id=1, source_target_pairs={{0,2},{1,3},{2,0},{3,1},{4,6},{5,7},{6,4},{7,5},{8,10},{9,11},{10,... | collective-permute-start | bytes 1505288 | tf_op jit(solution)/shard_map/ppermute | solution.py:75
  165.6 4.4 %collective-permute-done.25.refs_1_ = bf16[2,196,640]{2,1,0:T(8,128)(2,1)S(1)} collective-permute-done((bf16[2,196,640]{2,1,0:T(8,128)(2,1)}, bf16[2,196,640]{2,1,0:T(8,128)(2,1)S(1)}, u32[]{:S(2)}, u32[]{:S(2)}) %collective-permute-start.25) | collective-permute-done | bytes 501792 | tf_op jit(solution)/shard_map/ppermute | solution.py:75
  170.0 1.7 shard_map.145
  171.8 7.5 %collective-permute-done.33.refs_1_ = bf16[2,196,640]{2,1,0:T(8,128)(2,1)S(1)} collective-permute-done((bf16[2,196,640]{2,1,0:T(8,128)(2,1)}, bf16[2,196,640]{2,1,0:T(8,128)(2,1)S(1)}, u32[]{:S(2)}, u32[]{:S(2)}) %collective-permute-start.33) | collective-permute-done | bytes 501792 | tf_op jit(solution)/shard_map/ppermute | solution.py:75
  179.3 1.7 shard_map.146
  181.2 2.1 collective-permute-done.36
  183.7 2.4 %collective-permute-start.37 = (bf16[2,80,1024]{2,1,0:T(8,128)(2,1)S(1)}, bf16[2,80,1024]{2,1,0:T(8,128)(2,1)S(1)}, u32[]{:S(2)}, u32[]{:S(2)}) collective-permute-start(bf16[2,80,1024]{2,1,0:T(8,128)(2,1)S(1)} %slice.139), channel_id=1, source_target_pairs={{0,2},{1,3},{2,0},{3,1},{4,6},{5,7},{6,4},{7,5},{8,10},{9,11},{10,... | collective-permute-start | bytes 983048 | tf_op jit(solution)/shard_map/ppermute | solution.py:37
  186.1 8.0 %collective-permute-done.37 = bf16[2,80,1024]{2,1,0:T(8,128)(2,1)S(1)} collective-permute-done((bf16[2,80,1024]{2,1,0:T(8,128)(2,1)S(1)}, bf16[2,80,1024]{2,1,0:T(8,128)(2,1)S(1)}, u32[]{:S(2)}, u32[]{:S(2)}) %collective-permute-start.37) | collective-permute-done | bytes 327712 | tf_op jit(solution)/shard_map/ppermute | solution.py:37
  194.3 1.8 collective-permute-start.38
  196.1 8.4 %collective-permute-done.38 = bf16[80,1024]{1,0:T(8,128)(2,1)S(1)} collective-permute-done((bf16[80,1024]{1,0:T(8,128)(2,1)S(1)}, bf16[80,1024]{1,0:T(8,128)(2,1)S(1)}, u32[]{:S(2)}, u32[]{:S(2)}) %collective-permute-start.38) | collective-permute-done | bytes 163872 | tf_op jit(solution)/shard_map/ppermute | solution.py:37
  206.1 3.6 %collective-permute-done.40 = f32[2,1024]{1,0:T(2,128)S(1)} collective-permute-done((f32[2,1024]{1,0:T(2,128)S(1)}, f32[2,1024]{1,0:T(2,128)S(1)}, u32[]{:S(2)}, u32[]{:S(2)}) %collective-permute-start.40) | collective-permute-done | bytes 8224 | tf_op jit(solution)/shard_map/ppermute | solution.py:37
  211.2 3.3 %collective-permute-done.41 = f32[2,1024]{1,0:T(2,128)S(1)} collective-permute-done((f32[2,1024]{1,0:T(2,128)S(1)}, f32[2,1024]{1,0:T(2,128)S(1)}, u32[]{:S(2)}, u32[]{:S(2)}) %collective-permute-start.41) | collective-permute-done | bytes 8224 | tf_op jit(solution)/shard_map/ppermute | solution.py:37
  (197 shorter events, 38.9 us)
Async XLA Ops:
  2.6 14.5 %collective-permute-start = (bf16[392,640]{1,0:T(8,128)(2,1)S(1)}, bf16[392,640]{1,0:T(8,128)(2,1)S(1)}, u32[]{:S(2)}, u32[]{:S(2)}) collective-permute-start(bf16[392,640]{1,0:T(8,128)(2,1)S(1)} %slice_select_fusion.1.refs_0_.refs_3_), channel_id=1, source_target_pairs={{0,2},{1,3},{2,0},{3,1},{4,6},{5,7},{6,4},{7,5},{8,10},{9,11},{10,... | collective-permute-start | bytes 1505288 | tf_op jit(solution)/shard_map/ppermute | solution.py:75
  5.7 11.4 %collective-permute-start.1 = (bf16[392,640]{1,0:T(8,128)(2,1)S(1)}, bf16[392,640]{1,0:T(8,128)(2,1)S(1)}, u32[]{:S(2)}, u32[]{:S(2)}) collective-permute-start(bf16[392,640]{1,0:T(8,128)(2,1)S(1)} %slice_select_fusion.1.refs_0_.refs_3_), channel_id=1, source_target_pairs={{2,4},{3,5},{4,2},{5,3},{10,12},{11,13},{12,10},{13,11},{18,20},{1... | collective-permute-start | bytes 1505288 | tf_op jit(solution)/shard_map/ppermute | solution.py:75
  17.2 65.5 %collective-permute-start.16 = (bf16[512,2560]{1,0:T(8,128)(2,1)}, bf16[512,2560]{1,0:T(8,128)(2,1)}, u32[]{:S(2)}, u32[]{:S(2)}) collective-permute-start(bf16[512,2560]{1,0:T(8,128)(2,1)} %pad_maximum_fusion), channel_id=1, source_target_pairs={{0,1},{1,0},{2,3},{3,2},{4,5},{5,4},{6,7},{7,6},{8,9},{9,8},{10,11... | collective-permute-start | bytes 7864328 | tf_op jit(solution)/shard_map/ppermute | solution.py:37
  18.1 23.6 %collective-permute-start.3 = (bf16[392,640]{1,0:T(8,128)(2,1)S(1)}, bf16[392,640]{1,0:T(8,128)(2,1)S(1)}, u32[]{:S(2)}, u32[]{:S(2)}) collective-permute-start(bf16[392,640]{1,0:T(8,128)(2,1)S(1)} %collective-permute-done.refs_1_), channel_id=1, source_target_pairs={{2,4},{3,5},{4,2},{5,3},{10,12},{11,13},{12,10},{13,11},{18,20},{1... | collective-permute-start | bytes 1505288 | tf_op jit(solution)/shard_map/ppermute | solution.py:75
  18.8 22.9 %collective-permute-start.4 = (bf16[392,640]{1,0:T(8,128)(2,1)S(1)}, bf16[392,640]{1,0:T(8,128)(2,1)S(1)}, u32[]{:S(2)}, u32[]{:S(2)}) collective-permute-start(bf16[392,640]{1,0:T(8,128)(2,1)S(1)} %collective-permute-done.1), channel_id=1, source_target_pairs={{4,6},{5,7},{2,0},{3,1},{12,14},{13,15},{10,8},{11,9},{20,22},{21,... | collective-permute-start | bytes 1505288 | tf_op jit(solution)/shard_map/ppermute | solution.py:75
  22.7 19.0 %collective-permute-start.5 = (bf16[4,16,640]{2,1,0:T(8,128)(2,1)S(1)}, bf16[4,16,640]{2,1,0:T(8,128)(2,1)S(1)}, u32[]{:S(2)}, u32[]{:S(2)}) collective-permute-start(bf16[4,16,640]{2,1,0:T(8,128)(2,1)S(1)} %pad_maximum_fusion.9), channel_id=1, source_target_pairs={{0,2},{1,3},{2,0},{3,1},{4,6},{5,7},{6,4},{7,5},{8,10},{9,11},{10,... | collective-permute-start | bytes 245768 | tf_op jit(solution)/shard_map/ppermute | solution.py:37
  31.1 21.4 %collective-permute-start.8 = (bf16[392,640]{1,0:T(8,128)(2,1)S(1)}, bf16[392,640]{1,0:T(8,128)(2,1)S(1)}, u32[]{:S(2)}, u32[]{:S(2)}) collective-permute-start(bf16[392,640]{1,0:T(8,128)(2,1)S(1)} %slice_select_fusion.refs_0_.refs_3_), channel_id=1, source_target_pairs={{0,2},{1,3},{2,0},{3,1},{4,6},{5,7},{6,4},{7,5},{8,10},{9,11},{10,... | collective-permute-start | bytes 1505288 | tf_op jit(solution)/shard_map/ppermute | solution.py:75
  41.7 10.8 %collective-permute-start.7 = (bf16[392,640]{1,0:T(8,128)(2,1)S(1)}, bf16[392,640]{1,0:T(8,128)(2,1)S(1)}, u32[]{:S(2)}, u32[]{:S(2)}) collective-permute-start(bf16[392,640]{1,0:T(8,128)(2,1)S(1)} %slice_select_fusion.refs_0_.refs_3_), channel_id=1, source_target_pairs={{2,4},{3,5},{4,2},{5,3},{10,12},{11,13},{12,10},{13,11},{18,20},{1... | collective-permute-start | bytes 1505288 | tf_op jit(solution)/shard_map/ppermute | solution.py:75
  42.6 20.3 %collective-permute-start.6 = (bf16[392,640]{1,0:T(8,128)(2,1)S(1)}, bf16[392,640]{1,0:T(8,128)(2,1)S(1)}, u32[]{:S(2)}, u32[]{:S(2)}) collective-permute-start(bf16[392,640]{1,0:T(8,128)(2,1)S(1)} %collective-permute-done.3), channel_id=1, source_target_pairs={{4,6},{5,7},{2,0},{3,1},{12,14},{13,15},{10,8},{11,9},{20,22},{21,... | collective-permute-start | bytes 1505288 | tf_op jit(solution)/shard_map/ppermute | solution.py:75
  43.9 19.2 %collective-permute-start.9 = (bf16[392,640]{1,0:T(8,128)(2,1)S(1)}, bf16[392,640]{1,0:T(8,128)(2,1)S(1)}, u32[]{:S(2)}, u32[]{:S(2)}) collective-permute-start(bf16[392,640]{1,0:T(8,128)(2,1)S(1)} %slice_select_fusion.1.refs_0_.refs_3_), channel_id=1, source_target_pairs={{0,1},{1,0},{2,3},{3,2},{4,5},{5,4},{6,7},{7,6},{8,9},{9,8},{10,11... | collective-permute-start | bytes 1505288 | tf_op jit(solution)/shard_map/ppermute | solution.py:37
  52.5 11.9 %collective-permute-start.10 = (bf16[392,640]{1,0:T(8,128)(2,1)S(1)}, bf16[392,640]{1,0:T(8,128)(2,1)S(1)}, u32[]{:S(2)}, u32[]{:S(2)}) collective-permute-start(bf16[392,640]{1,0:T(8,128)(2,1)S(1)} %collective-permute-done.refs_1_), channel_id=1, source_target_pairs={{0,1},{1,0},{2,3},{3,2},{4,5},{5,4},{6,7},{7,6},{8,9},{9,8},{10,11... | collective-permute-start | bytes 1505288 | tf_op jit(solution)/shard_map/ppermute | solution.py:37
  52.5 13.2 %collective-permute-start.11 = (bf16[392,640]{1,0:T(8,128)(2,1)S(1)}, bf16[392,640]{1,0:T(8,128)(2,1)S(1)}, u32[]{:S(2)}, u32[]{:S(2)}) collective-permute-start(bf16[392,640]{1,0:T(8,128)(2,1)S(1)} %add.183.refs_2_), channel_id=1, source_target_pairs={{0,1},{1,0},{2,3},{3,2},{4,5},{5,4},{6,7},{7,6},{8,9},{9,8},{10,11... | collective-permute-start | bytes 1505288 | tf_op jit(solution)/shard_map/ppermute | solution.py:37
  63.1 17.2 %collective-permute-start.14 = (bf16[392,640]{1,0:T(8,128)(2,1)S(1)}, bf16[392,640]{1,0:T(8,128)(2,1)S(1)}, u32[]{:S(2)}, u32[]{:S(2)}) collective-permute-start(bf16[392,640]{1,0:T(8,128)(2,1)S(1)} %collective-permute-done.8.refs_1_), channel_id=1, source_target_pairs={{2,4},{3,5},{4,2},{5,3},{10,12},{11,13},{12,10},{13,11},{18,20},{1... | collective-permute-start | bytes 1505288 | tf_op jit(solution)/shard_map/ppermute | solution.py:75
  64.4 17.5 %collective-permute-start.15 = (bf16[392,640]{1,0:T(8,128)(2,1)S(1)}, bf16[392,640]{1,0:T(8,128)(2,1)S(1)}, u32[]{:S(2)}, u32[]{:S(2)}) collective-permute-start(bf16[392,640]{1,0:T(8,128)(2,1)S(1)} %collective-permute-done.7), channel_id=1, source_target_pairs={{4,6},{5,7},{2,0},{3,1},{12,14},{13,15},{10,8},{11,9},{20,22},{21,... | collective-permute-start | bytes 1505288 | tf_op jit(solution)/shard_map/ppermute | solution.py:75
  80.3 15.6 %collective-permute-start.17 = (bf16[392,640]{1,0:T(8,128)(2,1)S(1)}, bf16[392,640]{1,0:T(8,128)(2,1)S(1)}, u32[]{:S(2)}, u32[]{:S(2)}) collective-permute-start(bf16[392,640]{1,0:T(8,128)(2,1)S(1)} %collective-permute-done.14), channel_id=1, source_target_pairs={{4,6},{5,7},{2,0},{3,1},{12,14},{13,15},{10,8},{11,9},{20,22},{21,... | collective-permute-start | bytes 1505288 | tf_op jit(solution)/shard_map/ppermute | solution.py:75
  81.8 15.9 %collective-permute-start.18 = (bf16[392,640]{1,0:T(8,128)(2,1)S(1)}, bf16[392,640]{1,0:T(8,128)(2,1)S(1)}, u32[]{:S(2)}, u32[]{:S(2)}) collective-permute-start(bf16[392,640]{1,0:T(8,128)(2,1)S(1)} %slice_select_fusion.refs_0_.refs_3_), channel_id=1, source_target_pairs={{0,1},{1,0},{2,3},{3,2},{4,5},{5,4},{6,7},{7,6},{8,9},{9,8},{10,11... | collective-permute-start | bytes 1505288 | tf_op jit(solution)/shard_map/ppermute | solution.py:37
  81.9 15.8 %collective-permute-start.19 = (bf16[392,640]{1,0:T(8,128)(2,1)S(1)}, bf16[392,640]{1,0:T(8,128)(2,1)S(1)}, u32[]{:S(2)}, u32[]{:S(2)}) collective-permute-start(bf16[392,640]{1,0:T(8,128)(2,1)S(1)} %collective-permute-done.8.refs_1_), channel_id=1, source_target_pairs={{0,1},{1,0},{2,3},{3,2},{4,5},{5,4},{6,7},{7,6},{8,9},{9,8},{10,11... | collective-permute-start | bytes 1505288 | tf_op jit(solution)/shard_map/ppermute | solution.py:37
  82.5 15.2 %collective-permute-start.20 = (bf16[392,640]{1,0:T(8,128)(2,1)S(1)}, bf16[392,640]{1,0:T(8,128)(2,1)S(1)}, u32[]{:S(2)}, u32[]{:S(2)}) collective-permute-start(bf16[392,640]{1,0:T(8,128)(2,1)S(1)} %add.185.refs_2_), channel_id=1, source_target_pairs={{0,1},{1,0},{2,3},{3,2},{4,5},{5,4},{6,7},{7,6},{8,9},{9,8},{10,11... | collective-permute-start | bytes 1505288 | tf_op jit(solution)/shard_map/ppermute | solution.py:37
  96.1 16.1 %collective-permute-start.22 = (bf16[2,196,640]{2,1,0:T(8,128)(2,1)S(1)}, bf16[2,196,640]{2,1,0:T(8,128)(2,1)S(1)}, u32[]{:S(2)}, u32[]{:S(2)}) collective-permute-start(bf16[2,196,640]{2,1,0:T(8,128)(2,1)S(1)} %copy-done.15), channel_id=1, source_target_pairs={{6,4},{7,5},{0,2},{1,3},{14,12},{15,13},{8,10},{9,11},{22,20},{23,... | collective-permute-start | bytes 1505288 | tf_op jit(solution)/shard_map/ppermute | solution.py:75
  97.6 18.2 %collective-permute-start.29 = (bf16[4,16,640]{2,1,0:T(8,128)(2,1)S(1)}, bf16[4,16,640]{2,1,0:T(8,128)(2,1)S(1)}, u32[]{:S(2)}, u32[]{:S(2)}) collective-permute-start(bf16[4,16,640]{2,1,0:T(8,128)(2,1)S(1)} %pad_maximum_fusion.10), channel_id=1, source_target_pairs={{0,4},{1,5},{2,6},{3,7},{4,0},{5,1},{6,2},{7,3},{8,12},{9,13},{10,... | collective-permute-start | bytes 245768 | tf_op jit(solution)/shard_map/ppermute | solution.py:37
  112.6 23.2 %collective-permute-start.26 = (bf16[2,196,640]{2,1,0:T(8,128)(2,1)S(1)}, bf16[2,196,640]{2,1,0:T(8,128)(2,1)S(1)}, u32[]{:S(2)}, u32[]{:S(2)}) collective-permute-start(bf16[2,196,640]{2,1,0:T(8,128)(2,1)S(1)} %copy-done.14), channel_id=1, source_target_pairs={{6,4},{7,5},{0,2},{1,3},{14,12},{15,13},{8,10},{9,11},{22,20},{23,... | collective-permute-start | bytes 1505288 | tf_op jit(solution)/shard_map/ppermute | solution.py:75
  115.9 12.3 %collective-permute-start.30 = (bf16[8,16,640]{2,1,0:T(8,128)(2,1)S(1)}, bf16[8,16,640]{2,1,0:T(8,128)(2,1)S(1)}, u32[]{:S(2)}, u32[]{:S(2)}) collective-permute-start(bf16[8,16,640]{2,1,0:T(8,128)(2,1)S(1)} %pad_maximum_fusion.7), channel_id=1, source_target_pairs={{0,8},{8,0},{16,24},{24,16},{1,9},{9,1},{17,25},{25,17},{2,10},{10... | collective-permute-start | bytes 491528 | tf_op jit(solution)/shard_map/ppermute | solution.py:37
  117.6 20.1 %collective-permute-start.23 = (bf16[2,196,640]{2,1,0:T(8,128)(2,1)S(1)}, bf16[2,196,640]{2,1,0:T(8,128)(2,1)S(1)}, u32[]{:S(2)}, u32[]{:S(2)}) collective-permute-start(bf16[2,196,640]{2,1,0:T(8,128)(2,1)S(1)} %add_convert_fusion.5), channel_id=1, source_target_pairs={{2,4},{3,5},{4,2},{5,3},{10,12},{11,13},{12,10},{13,11},{18,20},{1... | collective-permute-start | bytes 1505288 | tf_op jit(solution)/shard_map/ppermute | solution.py:75
  123.8 15.5 %collective-permute-start.28 = (bf16[2,196,640]{2,1,0:T(8,128)(2,1)}, bf16[2,196,640]{2,1,0:T(8,128)(2,1)S(1)}, u32[]{:S(2)}, u32[]{:S(2)}) collective-permute-start(bf16[2,196,640]{2,1,0:T(8,128)(2,1)} %shard_map.143), channel_id=1, source_target_pairs={{6,4},{7,5},{0,2},{1,3},{14,12},{15,13},{8,10},{9,11},{22,20},{23,... | collective-permute-start | bytes 1505288 | tf_op jit(solution)/shard_map/ppermute | solution.py:75
  128.4 9.3 %collective-permute-start.31 = (bf16[8,32,640]{2,1,0:T(8,128)(2,1)S(1)}, bf16[8,32,640]{2,1,0:T(8,128)(2,1)S(1)}, u32[]{:S(2)}, u32[]{:S(2)}) collective-permute-start(bf16[8,32,640]{2,1,0:T(8,128)(2,1)S(1)} %pad_maximum_fusion.5), channel_id=1, source_target_pairs={{0,16},{8,24},{16,0},{24,8},{1,17},{9,25},{17,1},{25,9},{2,18},{10... | collective-permute-start | bytes 983048 | tf_op jit(solution)/shard_map/ppermute | solution.py:37
  140.4 18.5 %collective-permute-start.34 = (bf16[2,196,640]{2,1,0:T(8,128)(2,1)S(1)}, bf16[2,196,640]{2,1,0:T(8,128)(2,1)S(1)}, u32[]{:S(2)}, u32[]{:S(2)}) collective-permute-start(bf16[2,196,640]{2,1,0:T(8,128)(2,1)S(1)} %copy-done.16), channel_id=1, source_target_pairs={{6,4},{7,5},{0,2},{1,3},{14,12},{15,13},{8,10},{9,11},{22,20},{23,... | collective-permute-start | bytes 1505288 | tf_op jit(solution)/shard_map/ppermute | solution.py:75
  147.8 22.2 %collective-permute-start.25 = (bf16[2,196,640]{2,1,0:T(8,128)(2,1)}, bf16[2,196,640]{2,1,0:T(8,128)(2,1)S(1)}, u32[]{:S(2)}, u32[]{:S(2)}) collective-permute-start(bf16[2,196,640]{2,1,0:T(8,128)(2,1)} %add_convert_fusion.4), channel_id=1, source_target_pairs={{0,2},{1,3},{2,0},{3,1},{4,6},{5,7},{6,4},{7,5},{8,10},{9,11},{10,... | collective-permute-start | bytes 1505288 | tf_op jit(solution)/shard_map/ppermute | solution.py:75
  147.8 17.8 %collective-permute-start.27 = (bf16[2,196,640]{2,1,0:T(8,128)(2,1)S(1)}, bf16[2,196,640]{2,1,0:T(8,128)(2,1)S(1)}, u32[]{:S(2)}, u32[]{:S(2)}) collective-permute-start(bf16[2,196,640]{2,1,0:T(8,128)(2,1)S(1)} %add_convert_fusion.3), channel_id=1, source_target_pairs={{2,4},{3,5},{4,2},{5,3},{10,12},{11,13},{12,10},{13,11},{18,20},{1... | collective-permute-start | bytes 1505288 | tf_op jit(solution)/shard_map/ppermute | solution.py:75
  159.8 11.9 %collective-permute-start.35 = (bf16[2,196,640]{2,1,0:T(8,128)(2,1)}, bf16[2,196,640]{2,1,0:T(8,128)(2,1)S(1)}, u32[]{:S(2)}, u32[]{:S(2)}) collective-permute-start(bf16[2,196,640]{2,1,0:T(8,128)(2,1)} %add_convert_fusion), channel_id=1, source_target_pairs={{2,4},{3,5},{4,2},{5,3},{10,12},{11,13},{12,10},{13,11},{18,20},{1... | collective-permute-start | bytes 1505288 | tf_op jit(solution)/shard_map/ppermute | solution.py:75
  160.5 18.7 %collective-permute-start.33 = (bf16[2,196,640]{2,1,0:T(8,128)(2,1)}, bf16[2,196,640]{2,1,0:T(8,128)(2,1)S(1)}, u32[]{:S(2)}, u32[]{:S(2)}) collective-permute-start(bf16[2,196,640]{2,1,0:T(8,128)(2,1)} %add_convert_fusion.1), channel_id=1, source_target_pairs={{0,2},{1,3},{2,0},{3,1},{4,6},{5,7},{6,4},{7,5},{8,10},{9,11},{10,... | collective-permute-start | bytes 1505288 | tf_op jit(solution)/shard_map/ppermute | solution.py:75
  183.7 10.5 %collective-permute-start.37 = (bf16[2,80,1024]{2,1,0:T(8,128)(2,1)S(1)}, bf16[2,80,1024]{2,1,0:T(8,128)(2,1)S(1)}, u32[]{:S(2)}, u32[]{:S(2)}) collective-permute-start(bf16[2,80,1024]{2,1,0:T(8,128)(2,1)S(1)} %slice.139), channel_id=1, source_target_pairs={{0,2},{1,3},{2,0},{3,1},{4,6},{5,7},{6,4},{7,5},{8,10},{9,11},{10,... | collective-permute-start | bytes 983048 | tf_op jit(solution)/shard_map/ppermute | solution.py:37
  194.3 10.2 %collective-permute-start.38 = (bf16[80,1024]{1,0:T(8,128)(2,1)S(1)}, bf16[80,1024]{1,0:T(8,128)(2,1)S(1)}, u32[]{:S(2)}, u32[]{:S(2)}) collective-permute-start(bf16[80,1024]{1,0:T(8,128)(2,1)S(1)} %slice_bitcast_fusion), channel_id=1, source_target_pairs={{0,4},{1,5},{2,6},{3,7},{4,0},{5,1},{6,2},{7,3},{8,12},{9,13},{10,... | collective-permute-start | bytes 491528 | tf_op jit(solution)/shard_map/ppermute | solution.py:37
  (46 other events, 459.6 us)

commit v4 on v3

--- a/solution.py
+++ b/solution.py
@@ -22,7 +22,7 @@
 FIRST_DEMAND = False
 DEMAND = True
 VMEM_A = 56
-STAGES = 2
+STAGES = 4
 VMEM_B = 56
 GROUPS = [(0, 2), (2, 4)]
 

time: 216 us -> 215 us (level)
  transfers between devices with their start and end apart: 42 -> 42, of which waited for: 17 -> 17; matrix products, arithmetic and copies ran while one was open for 7% -> 7% of each run, Pallas kernels for 21% -> 20%
where the time goes in v4:
time: 215 us; the launch traced here: 214 us
  waiting for transfers between devices  91.6 us (43%)
  starting transfers between devices  52.7 us (25%)
  Pallas kernels  45.2 us (21%)
  other arithmetic  12.8 us (6%)
  local copies, waits for them, and re-layouts  9.7 us (5%)
    ppermute x20, waiting for transfers between devices, permuted(): return lax.ppermute(value, 'tp', pairs)  52.3 us
    ppermute x22, waiting for transfers between devices, swapped(): return lax.ppermute(value, axis, pairs)  39.4 us
    ppermute x20, starting transfers between devices, permuted(): return lax.ppermute(value, 'tp', pairs)  34.7 us
    pallas_call x2, Pallas kernels, attend(): pl.pallas_call(functools.partial(attend_kernel, heads), out_shape=jax.Sha...  24.6 us
    ppermute x22, starting transfers between devices, swapped(): return lax.ppermute(value, axis, pairs)  17.9 us
    pallas_call x3, Pallas kernels, out(): pl.pallas_call(out_kernel, out_shape=[jax.ShapeDtypeStruct((size, L, widt...  17.1 us
  transfers between devices with their start and end apart: 42, of which 17 were waited for; matrix products, arithmetic and copies ran while one was open for 7% of the time, Pallas kernels for 20%

profile of v4, /device:TPU:0, one launch (start us, length us, event | category | flops | bytes accessed | tf_op | source)
XLA Modules:
  0.0 213.8 jit_solution(17211862093828700381)
XLA Ops:
  2.6 3.1 %collective-permute-start = (bf16[392,640]{1,0:T(8,128)(2,1)S(1)}, bf16[392,640]{1,0:T(8,128)(2,1)S(1)}, u32[]{:S(2)}, u32[]{:S(2)}) collective-permute-start(bf16[392,640]{1,0:T(8,128)(2,1)S(1)} %slice_select_fusion.1.refs_0_.refs_3_), channel_id=1, source_target_pairs={{0,2},{1,3},{2,0},{3,1},{4,6},{5,7},{6,4},{7,5},{8,10},{9,11},{10,... | collective-permute-start | bytes 1505288 | tf_op jit(solution)/shard_map/ppermute | solution.py:75
  7.7 1.9 constant_dynamic-slice_fusion.3
  9.7 1.6 pad_maximum_fusion
  12.0 5.2 %collective-permute-done.refs_1_ = bf16[392,640]{1,0:T(8,128)(2,1)S(1)} collective-permute-done((bf16[392,640]{1,0:T(8,128)(2,1)S(1)}, bf16[392,640]{1,0:T(8,128)(2,1)S(1)}, u32[]{:S(2)}, u32[]{:S(2)}) %collective-permute-start) | collective-permute-done | bytes 501792 | tf_op jit(solution)/shard_map/ppermute | solution.py:75
  22.7 7.7 %collective-permute-start.5 = (bf16[4,16,640]{2,1,0:T(8,128)(2,1)S(1)}, bf16[4,16,640]{2,1,0:T(8,128)(2,1)S(1)}, u32[]{:S(2)}, u32[]{:S(2)}) collective-permute-start(bf16[4,16,640]{2,1,0:T(8,128)(2,1)S(1)} %pad_maximum_fusion.9), channel_id=1, source_target_pairs={{0,2},{1,3},{2,0},{3,1},{4,6},{5,7},{6,4},{7,5},{8,10},{9,11},{10,... | collective-permute-start | bytes 245768 | tf_op jit(solution)/shard_map/ppermute | solution.py:37
  31.1 10.6 %collective-permute-done.5 = bf16[4,16,640]{2,1,0:T(8,128)(2,1)S(1)} collective-permute-done((bf16[4,16,640]{2,1,0:T(8,128)(2,1)S(1)}, bf16[4,16,640]{2,1,0:T(8,128)(2,1)S(1)}, u32[]{:S(2)}, u32[]{:S(2)}) %collective-permute-start.5) | collective-permute-done | bytes 81952 | tf_op jit(solution)/shard_map/ppermute | solution.py:37
  44.1 8.4 %collective-permute-done.8.refs_1_ = bf16[392,640]{1,0:T(8,128)(2,1)S(1)} collective-permute-done((bf16[392,640]{1,0:T(8,128)(2,1)S(1)}, bf16[392,640]{1,0:T(8,128)(2,1)S(1)}, u32[]{:S(2)}, u32[]{:S(2)}) %collective-permute-start.8) | collective-permute-done | bytes 501792 | tf_op jit(solution)/shard_map/ppermute | solution.py:75
  53.0 9.8 %collective-permute-done.6 = bf16[392,640]{1,0:T(8,128)(2,1)S(1)} collective-permute-done((bf16[392,640]{1,0:T(8,128)(2,1)S(1)}, bf16[392,640]{1,0:T(8,128)(2,1)S(1)}, u32[]{:S(2)}, u32[]{:S(2)}) %collective-permute-start.6) | collective-permute-done | bytes 501792 | tf_op jit(solution)/shard_map/ppermute | solution.py:75
  66.7 12.3 %shard_map.140.own = bf16[2,196,512]{2,1,0:T(8,128)(2,1)} custom-call(s32[8]{0:T(128)} %pad_add_fusion.1.order, s32[2]{0:T(128)} %get-tuple-element.188.length, bf16[392,640]{1,0:T(8,128)(2,1)} %copy-done, bf16[392,640]{1,0:T(8,128)(2,1)} %copy-done.18, bf16[392,640]{1,0:T(8,128)(2,1)} %copy-done.8, bf16[392,640]{1,0:T(8,128)(2,1)} %copy-done.10, ...), custom_call_target="tpu_custom_call" | custom-call | flops 3082813440 | bytes 25165824 | tf_op jit(solution)/shard_map/pallas_call | solution.py:296
  82.5 6.7 %shard_map.141 = (bf16[2,196,640]{2,1,0:T(8,128)(2,1)}, bf16[2,196,640]{2,1,0:T(8,128)(2,1)}, bf16[2,196,640]{2,1,0:T(8,128)(2,1)}, bf16[2,196,640]{2,1,0:T(8,128)(2,1)}) custom-call(s32[4]{0:T(128)} %copy-done.32, s32[4]{0:T(128)} %copy-done.31, bf16[2,196,512]{2,1,0:T(8,128)(2,1)} %shard_map.140.own, bf16[2,196,512]{2,1,0:T(8,128)(2,1)} %copy-done.28, ...), custom_call_target="tpu_custom_call" | custom-call | flops 2055208960 | bytes 33554432 | tf_op jit(solution)/shard_map/pallas_call | solution.py:318
  89.2 5.8 %collective-permute-done.17 = bf16[392,640]{1,0:T(8,128)(2,1)S(1)} collective-permute-done((bf16[392,640]{1,0:T(8,128)(2,1)S(1)}, bf16[392,640]{1,0:T(8,128)(2,1)S(1)}, u32[]{:S(2)}, u32[]{:S(2)}) %collective-permute-start.17) | collective-permute-done | bytes 501792 | tf_op jit(solution)/shard_map/ppermute | solution.py:75
  98.2 12.3 %shard_map.142.own = bf16[2,196,512]{2,1,0:T(8,128)(2,1)} custom-call(s32[8]{0:T(128)} %pad_add_fusion.1.order, s32[2]{0:T(128)} %get-tuple-element.189.length, bf16[392,640]{1,0:T(8,128)(2,1)} %copy-done.2, bf16[392,640]{1,0:T(8,128)(2,1)} %copy-done.19, bf16[392,640]{1,0:T(8,128)(2,1)} %copy-done.7, bf16[392,640]{1,0:T(8,128)(2,1)} %copy-done.9, ...), custom_call_target="tpu_custom_call" | custom-call | flops 3082813440 | bytes 25165824 | tf_op jit(solution)/shard_map/pallas_call | solution.py:296
  111.0 3.3 %collective-permute-start.26 = (bf16[2,196,640]{2,1,0:T(8,128)(2,1)S(1)}, bf16[2,196,640]{2,1,0:T(8,128)(2,1)S(1)}, u32[]{:S(2)}, u32[]{:S(2)}) collective-permute-start(bf16[2,196,640]{2,1,0:T(8,128)(2,1)S(1)} %copy-done.14), channel_id=1, source_target_pairs={{6,4},{7,5},{0,2},{1,3},{14,12},{15,13},{8,10},{9,11},{22,20},{23,... | collective-permute-start | bytes 1505288 | tf_op jit(solution)/shard_map/ppermute | solution.py:75
  117.5 4.7 %shard_map.143 = bf16[2,196,640]{2,1,0:T(8,128)(2,1)} custom-call(s32[1]{0:T(128)} %bitcast.15.chips, s32[1]{0:T(128)} %slice.111.blocks, bf16[2,196,512]{2,1,0:T(8,128)(2,1)} %shard_map.142.own, bf16[2,196,512]{2,1,0:T(8,128)(2,1)} %copy-done.11, bf16[512,5120]{1,0:T(8,128)(2,1)} %w_own.5, bf16[512,2560]{1,0:T(8,128)(2,1)} %collective-permute-done.16.w_other), custom_call_target="tpu_custom_call" | custom-call | flops 513802240 | bytes 8388608 | tf_op jit(solution)/shard_map/pallas_call | solution.py:318
  122.2 4.5 %collective-permute-start.28 = (bf16[2,196,640]{2,1,0:T(8,128)(2,1)}, bf16[2,196,640]{2,1,0:T(8,128)(2,1)S(1)}, u32[]{:S(2)}, u32[]{:S(2)}) collective-permute-start(bf16[2,196,640]{2,1,0:T(8,128)(2,1)} %shard_map.143), channel_id=1, source_target_pairs={{6,4},{7,5},{0,2},{1,3},{14,12},{15,13},{8,10},{9,11},{22,20},{23,... | collective-permute-start | bytes 1505288 | tf_op jit(solution)/shard_map/ppermute | solution.py:75
  128.3 5.8 %shard_map.144 = (bf16[2,196,640]{2,1,0:T(8,128)(2,1)}, bf16[2,196,640]{2,1,0:T(8,128)(2,1)}, bf16[2,196,640]{2,1,0:T(8,128)(2,1)}) custom-call(s32[3]{0:T(128)} %pad_add_fusion.2.chips, s32[3]{0:T(128)} %bitcast.67, bf16[2,196,512]{2,1,0:T(8,128)(2,1)} %shard_map.142.own, bf16[2,196,512]{2,1,0:T(8,128)(2,1)} %copy-done.11, bf16[512,5120]{1,0:T(8,128)(2,1)} %w_own.5, ...), custom_call_target="tpu_custom_call" | custom-call | flops 1541406720 | bytes 25165824 | tf_op jit(solution)/shard_map/pallas_call | solution.py:318
  134.1 1.9 collective-permute-done.31
  136.1 1.6 collective-permute-done.28
  138.8 6.4 %collective-permute-start.34 = (bf16[2,196,640]{2,1,0:T(8,128)(2,1)S(1)}, bf16[2,196,640]{2,1,0:T(8,128)(2,1)S(1)}, u32[]{:S(2)}, u32[]{:S(2)}) collective-permute-start(bf16[2,196,640]{2,1,0:T(8,128)(2,1)S(1)} %copy-done.16), channel_id=1, source_target_pairs={{6,4},{7,5},{0,2},{1,3},{14,12},{15,13},{8,10},{9,11},{22,20},{23,... | collective-permute-start | bytes 1505288 | tf_op jit(solution)/shard_map/ppermute | solution.py:75
  147.8 9.5 %collective-permute-done.34 = bf16[2,196,640]{2,1,0:T(8,128)(2,1)S(1)} collective-permute-done((bf16[2,196,640]{2,1,0:T(8,128)(2,1)S(1)}, bf16[2,196,640]{2,1,0:T(8,128)(2,1)S(1)}, u32[]{:S(2)}, u32[]{:S(2)}) %collective-permute-start.34) | collective-permute-done | bytes 501792 | tf_op jit(solution)/shard_map/ppermute | solution.py:75
  158.9 4.9 %collective-permute-start.33 = (bf16[2,196,640]{2,1,0:T(8,128)(2,1)}, bf16[2,196,640]{2,1,0:T(8,128)(2,1)S(1)}, u32[]{:S(2)}, u32[]{:S(2)}) collective-permute-start(bf16[2,196,640]{2,1,0:T(8,128)(2,1)} %add_convert_fusion.1), channel_id=1, source_target_pairs={{0,2},{1,3},{2,0},{3,1},{4,6},{5,7},{6,4},{7,5},{8,10},{9,11},{10,... | collective-permute-start | bytes 1505288 | tf_op jit(solution)/shard_map/ppermute | solution.py:75
  164.0 4.4 %collective-permute-done.25.refs_1_ = bf16[2,196,640]{2,1,0:T(8,128)(2,1)S(1)} collective-permute-done((bf16[2,196,640]{2,1,0:T(8,128)(2,1)}, bf16[2,196,640]{2,1,0:T(8,128)(2,1)S(1)}, u32[]{:S(2)}, u32[]{:S(2)}) %collective-permute-start.25) | collective-permute-done | bytes 501792 | tf_op jit(solution)/shard_map/ppermute | solution.py:75
  168.4 1.7 shard_map.145
  170.2 7.5 %collective-permute-done.33.refs_1_ = bf16[2,196,640]{2,1,0:T(8,128)(2,1)S(1)} collective-permute-done((bf16[2,196,640]{2,1,0:T(8,128)(2,1)}, bf16[2,196,640]{2,1,0:T(8,128)(2,1)S(1)}, u32[]{:S(2)}, u32[]{:S(2)}) %collective-permute-start.33) | collective-permute-done | bytes 501792 | tf_op jit(solution)/shard_map/ppermute | solution.py:75
  177.7 1.7 shard_map.146
  179.6 2.1 collective-permute-done.36
  182.0 2.4 %collective-permute-start.37 = (bf16[2,80,1024]{2,1,0:T(8,128)(2,1)S(1)}, bf16[2,80,1024]{2,1,0:T(8,128)(2,1)S(1)}, u32[]{:S(2)}, u32[]{:S(2)}) collective-permute-start(bf16[2,80,1024]{2,1,0:T(8,128)(2,1)S(1)} %slice.139), channel_id=1, source_target_pairs={{0,2},{1,3},{2,0},{3,1},{4,6},{5,7},{6,4},{7,5},{8,10},{9,11},{10,... | collective-permute-start | bytes 983048 | tf_op jit(solution)/shard_map/ppermute | solution.py:37
  184.5 8.0 %collective-permute-done.37 = bf16[2,80,1024]{2,1,0:T(8,128)(2,1)S(1)} collective-permute-done((bf16[2,80,1024]{2,1,0:T(8,128)(2,1)S(1)}, bf16[2,80,1024]{2,1,0:T(8,128)(2,1)S(1)}, u32[]{:S(2)}, u32[]{:S(2)}) %collective-permute-start.37) | collective-permute-done | bytes 327712 | tf_op jit(solution)/shard_map/ppermute | solution.py:37
  192.7 1.8 collective-permute-start.38
  194.5 8.4 %collective-permute-done.38 = bf16[80,1024]{1,0:T(8,128)(2,1)S(1)} collective-permute-done((bf16[80,1024]{1,0:T(8,128)(2,1)S(1)}, bf16[80,1024]{1,0:T(8,128)(2,1)S(1)}, u32[]{:S(2)}, u32[]{:S(2)}) %collective-permute-start.38) | collective-permute-done | bytes 163872 | tf_op jit(solution)/shard_map/ppermute | solution.py:37
  204.5 3.6 %collective-permute-done.40 = f32[2,1024]{1,0:T(2,128)S(1)} collective-permute-done((f32[2,1024]{1,0:T(2,128)S(1)}, f32[2,1024]{1,0:T(2,128)S(1)}, u32[]{:S(2)}, u32[]{:S(2)}) %collective-permute-start.40) | collective-permute-done | bytes 8224 | tf_op jit(solution)/shard_map/ppermute | solution.py:37
  209.6 3.3 %collective-permute-done.41 = f32[2,1024]{1,0:T(2,128)S(1)} collective-permute-done((f32[2,1024]{1,0:T(2,128)S(1)}, f32[2,1024]{1,0:T(2,128)S(1)}, u32[]{:S(2)}, u32[]{:S(2)}) %collective-permute-start.41) | collective-permute-done | bytes 8224 | tf_op jit(solution)/shard_map/ppermute | solution.py:37
  (197 shorter events, 38.9 us)
Async XLA Ops:
  2.6 14.5 %collective-permute-start = (bf16[392,640]{1,0:T(8,128)(2,1)S(1)}, bf16[392,640]{1,0:T(8,128)(2,1)S(1)}, u32[]{:S(2)}, u32[]{:S(2)}) collective-permute-start(bf16[392,640]{1,0:T(8,128)(2,1)S(1)} %slice_select_fusion.1.refs_0_.refs_3_), channel_id=1, source_target_pairs={{0,2},{1,3},{2,0},{3,1},{4,6},{5,7},{6,4},{7,5},{8,10},{9,11},{10,... | collective-permute-start | bytes 1505288 | tf_op jit(solution)/shard_map/ppermute | solution.py:75
  5.7 11.4 %collective-permute-start.1 = (bf16[392,640]{1,0:T(8,128)(2,1)S(1)}, bf16[392,640]{1,0:T(8,128)(2,1)S(1)}, u32[]{:S(2)}, u32[]{:S(2)}) collective-permute-start(bf16[392,640]{1,0:T(8,128)(2,1)S(1)} %slice_select_fusion.1.refs_0_.refs_3_), channel_id=1, source_target_pairs={{2,4},{3,5},{4,2},{5,3},{10,12},{11,13},{12,10},{13,11},{18,20},{1... | collective-permute-start | bytes 1505288 | tf_op jit(solution)/shard_map/ppermute | solution.py:75
  17.2 64.7 %collective-permute-start.16 = (bf16[512,2560]{1,0:T(8,128)(2,1)}, bf16[512,2560]{1,0:T(8,128)(2,1)}, u32[]{:S(2)}, u32[]{:S(2)}) collective-permute-start(bf16[512,2560]{1,0:T(8,128)(2,1)} %pad_maximum_fusion), channel_id=1, source_target_pairs={{0,1},{1,0},{2,3},{3,2},{4,5},{5,4},{6,7},{7,6},{8,9},{9,8},{10,11... | collective-permute-start | bytes 7864328 | tf_op jit(solution)/shard_map/ppermute | solution.py:37
  18.1 23.6 %collective-permute-start.3 = (bf16[392,640]{1,0:T(8,128)(2,1)S(1)}, bf16[392,640]{1,0:T(8,128)(2,1)S(1)}, u32[]{:S(2)}, u32[]{:S(2)}) collective-permute-start(bf16[392,640]{1,0:T(8,128)(2,1)S(1)} %collective-permute-done.refs_1_), channel_id=1, source_target_pairs={{2,4},{3,5},{4,2},{5,3},{10,12},{11,13},{12,10},{13,11},{18,20},{1... | collective-permute-start | bytes 1505288 | tf_op jit(solution)/shard_map/ppermute | solution.py:75
  18.8 22.9 %collective-permute-start.4 = (bf16[392,640]{1,0:T(8,128)(2,1)S(1)}, bf16[392,640]{1,0:T(8,128)(2,1)S(1)}, u32[]{:S(2)}, u32[]{:S(2)}) collective-permute-start(bf16[392,640]{1,0:T(8,128)(2,1)S(1)} %collective-permute-done.1), channel_id=1, source_target_pairs={{4,6},{5,7},{2,0},{3,1},{12,14},{13,15},{10,8},{11,9},{20,22},{21,... | collective-permute-start | bytes 1505288 | tf_op jit(solution)/shard_map/ppermute | solution.py:75
  22.7 19.0 %collective-permute-start.5 = (bf16[4,16,640]{2,1,0:T(8,128)(2,1)S(1)}, bf16[4,16,640]{2,1,0:T(8,128)(2,1)S(1)}, u32[]{:S(2)}, u32[]{:S(2)}) collective-permute-start(bf16[4,16,640]{2,1,0:T(8,128)(2,1)S(1)} %pad_maximum_fusion.9), channel_id=1, source_target_pairs={{0,2},{1,3},{2,0},{3,1},{4,6},{5,7},{6,4},{7,5},{8,10},{9,11},{10,... | collective-permute-start | bytes 245768 | tf_op jit(solution)/shard_map/ppermute | solution.py:37
  31.1 21.4 %collective-permute-start.8 = (bf16[392,640]{1,0:T(8,128)(2,1)S(1)}, bf16[392,640]{1,0:T(8,128)(2,1)S(1)}, u32[]{:S(2)}, u32[]{:S(2)}) collective-permute-start(bf16[392,640]{1,0:T(8,128)(2,1)S(1)} %slice_select_fusion.refs_0_.refs_3_), channel_id=1, source_target_pairs={{0,2},{1,3},{2,0},{3,1},{4,6},{5,7},{6,4},{7,5},{8,10},{9,11},{10,... | collective-permute-start | bytes 1505288 | tf_op jit(solution)/shard_map/ppermute | solution.py:75
  41.7 10.8 %collective-permute-start.7 = (bf16[392,640]{1,0:T(8,128)(2,1)S(1)}, bf16[392,640]{1,0:T(8,128)(2,1)S(1)}, u32[]{:S(2)}, u32[]{:S(2)}) collective-permute-start(bf16[392,640]{1,0:T(8,128)(2,1)S(1)} %slice_select_fusion.refs_0_.refs_3_), channel_id=1, source_target_pairs={{2,4},{3,5},{4,2},{5,3},{10,12},{11,13},{12,10},{13,11},{18,20},{1... | collective-permute-start | bytes 1505288 | tf_op jit(solution)/shard_map/ppermute | solution.py:75
  42.6 20.3 %collective-permute-start.6 = (bf16[392,640]{1,0:T(8,128)(2,1)S(1)}, bf16[392,640]{1,0:T(8,128)(2,1)S(1)}, u32[]{:S(2)}, u32[]{:S(2)}) collective-permute-start(bf16[392,640]{1,0:T(8,128)(2,1)S(1)} %collective-permute-done.3), channel_id=1, source_target_pairs={{4,6},{5,7},{2,0},{3,1},{12,14},{13,15},{10,8},{11,9},{20,22},{21,... | collective-permute-start | bytes 1505288 | tf_op jit(solution)/shard_map/ppermute | solution.py:75
  43.9 19.2 %collective-permute-start.9 = (bf16[392,640]{1,0:T(8,128)(2,1)S(1)}, bf16[392,640]{1,0:T(8,128)(2,1)S(1)}, u32[]{:S(2)}, u32[]{:S(2)}) collective-permute-start(bf16[392,640]{1,0:T(8,128)(2,1)S(1)} %slice_select_fusion.1.refs_0_.refs_3_), channel_id=1, source_target_pairs={{0,1},{1,0},{2,3},{3,2},{4,5},{5,4},{6,7},{7,6},{8,9},{9,8},{10,11... | collective-permute-start | bytes 1505288 | tf_op jit(solution)/shard_map/ppermute | solution.py:37
  52.5 11.9 %collective-permute-start.10 = (bf16[392,640]{1,0:T(8,128)(2,1)S(1)}, bf16[392,640]{1,0:T(8,128)(2,1)S(1)}, u32[]{:S(2)}, u32[]{:S(2)}) collective-permute-start(bf16[392,640]{1,0:T(8,128)(2,1)S(1)} %collective-permute-done.refs_1_), channel_id=1, source_target_pairs={{0,1},{1,0},{2,3},{3,2},{4,5},{5,4},{6,7},{7,6},{8,9},{9,8},{10,11... | collective-permute-start | bytes 1505288 | tf_op jit(solution)/shard_map/ppermute | solution.py:37
  52.5 13.2 %collective-permute-start.11 = (bf16[392,640]{1,0:T(8,128)(2,1)S(1)}, bf16[392,640]{1,0:T(8,128)(2,1)S(1)}, u32[]{:S(2)}, u32[]{:S(2)}) collective-permute-start(bf16[392,640]{1,0:T(8,128)(2,1)S(1)} %add.183.refs_2_), channel_id=1, source_target_pairs={{0,1},{1,0},{2,3},{3,2},{4,5},{5,4},{6,7},{7,6},{8,9},{9,8},{10,11... | collective-permute-start | bytes 1505288 | tf_op jit(solution)/shard_map/ppermute | solution.py:37
  63.1 16.4 %collective-permute-start.14 = (bf16[392,640]{1,0:T(8,128)(2,1)S(1)}, bf16[392,640]{1,0:T(8,128)(2,1)S(1)}, u32[]{:S(2)}, u32[]{:S(2)}) collective-permute-start(bf16[392,640]{1,0:T(8,128)(2,1)S(1)} %collective-permute-done.8.refs_1_), channel_id=1, source_target_pairs={{2,4},{3,5},{4,2},{5,3},{10,12},{11,13},{12,10},{13,11},{18,20},{1... | collective-permute-start | bytes 1505288 | tf_op jit(solution)/shard_map/ppermute | solution.py:75
  64.4 16.7 %collective-permute-start.15 = (bf16[392,640]{1,0:T(8,128)(2,1)S(1)}, bf16[392,640]{1,0:T(8,128)(2,1)S(1)}, u32[]{:S(2)}, u32[]{:S(2)}) collective-permute-start(bf16[392,640]{1,0:T(8,128)(2,1)S(1)} %collective-permute-done.7), channel_id=1, source_target_pairs={{4,6},{5,7},{2,0},{3,1},{12,14},{13,15},{10,8},{11,9},{20,22},{21,... | collective-permute-start | bytes 1505288 | tf_op jit(solution)/shard_map/ppermute | solution.py:75
  79.5 15.6 %collective-permute-start.17 = (bf16[392,640]{1,0:T(8,128)(2,1)S(1)}, bf16[392,640]{1,0:T(8,128)(2,1)S(1)}, u32[]{:S(2)}, u32[]{:S(2)}) collective-permute-start(bf16[392,640]{1,0:T(8,128)(2,1)S(1)} %collective-permute-done.14), channel_id=1, source_target_pairs={{4,6},{5,7},{2,0},{3,1},{12,14},{13,15},{10,8},{11,9},{20,22},{21,... | collective-permute-start | bytes 1505288 | tf_op jit(solution)/shard_map/ppermute | solution.py:75
  81.0 15.9 %collective-permute-start.18 = (bf16[392,640]{1,0:T(8,128)(2,1)S(1)}, bf16[392,640]{1,0:T(8,128)(2,1)S(1)}, u32[]{:S(2)}, u32[]{:S(2)}) collective-permute-start(bf16[392,640]{1,0:T(8,128)(2,1)S(1)} %slice_select_fusion.refs_0_.refs_3_), channel_id=1, source_target_pairs={{0,1},{1,0},{2,3},{3,2},{4,5},{5,4},{6,7},{7,6},{8,9},{9,8},{10,11... | collective-permute-start | bytes 1505288 | tf_op jit(solution)/shard_map/ppermute | solution.py:37
  81.1 15.8 %collective-permute-start.19 = (bf16[392,640]{1,0:T(8,128)(2,1)S(1)}, bf16[392,640]{1,0:T(8,128)(2,1)S(1)}, u32[]{:S(2)}, u32[]{:S(2)}) collective-permute-start(bf16[392,640]{1,0:T(8,128)(2,1)S(1)} %collective-permute-done.8.refs_1_), channel_id=1, source_target_pairs={{0,1},{1,0},{2,3},{3,2},{4,5},{5,4},{6,7},{7,6},{8,9},{9,8},{10,11... | collective-permute-start | bytes 1505288 | tf_op jit(solution)/shard_map/ppermute | solution.py:37
  81.7 15.2 %collective-permute-start.20 = (bf16[392,640]{1,0:T(8,128)(2,1)S(1)}, bf16[392,640]{1,0:T(8,128)(2,1)S(1)}, u32[]{:S(2)}, u32[]{:S(2)}) collective-permute-start(bf16[392,640]{1,0:T(8,128)(2,1)S(1)} %add.185.refs_2_), channel_id=1, source_target_pairs={{0,1},{1,0},{2,3},{3,2},{4,5},{5,4},{6,7},{7,6},{8,9},{9,8},{10,11... | collective-permute-start | bytes 1505288 | tf_op jit(solution)/shard_map/ppermute | solution.py:37
  95.3 15.3 %collective-permute-start.22 = (bf16[2,196,640]{2,1,0:T(8,128)(2,1)S(1)}, bf16[2,196,640]{2,1,0:T(8,128)(2,1)S(1)}, u32[]{:S(2)}, u32[]{:S(2)}) collective-permute-start(bf16[2,196,640]{2,1,0:T(8,128)(2,1)S(1)} %copy-done.15), channel_id=1, source_target_pairs={{6,4},{7,5},{0,2},{1,3},{14,12},{15,13},{8,10},{9,11},{22,20},{23,... | collective-permute-start | bytes 1505288 | tf_op jit(solution)/shard_map/ppermute | solution.py:75
  96.8 17.4 %collective-permute-start.29 = (bf16[4,16,640]{2,1,0:T(8,128)(2,1)S(1)}, bf16[4,16,640]{2,1,0:T(8,128)(2,1)S(1)}, u32[]{:S(2)}, u32[]{:S(2)}) collective-permute-start(bf16[4,16,640]{2,1,0:T(8,128)(2,1)S(1)} %pad_maximum_fusion.10), channel_id=1, source_target_pairs={{0,4},{1,5},{2,6},{3,7},{4,0},{5,1},{6,2},{7,3},{8,12},{9,13},{10,... | collective-permute-start | bytes 245768 | tf_op jit(solution)/shard_map/ppermute | solution.py:37
  111.0 23.2 %collective-permute-start.26 = (bf16[2,196,640]{2,1,0:T(8,128)(2,1)S(1)}, bf16[2,196,640]{2,1,0:T(8,128)(2,1)S(1)}, u32[]{:S(2)}, u32[]{:S(2)}) collective-permute-start(bf16[2,196,640]{2,1,0:T(8,128)(2,1)S(1)} %copy-done.14), channel_id=1, source_target_pairs={{6,4},{7,5},{0,2},{1,3},{14,12},{15,13},{8,10},{9,11},{22,20},{23,... | collective-permute-start | bytes 1505288 | tf_op jit(solution)/shard_map/ppermute | solution.py:75
  114.3 12.3 %collective-permute-start.30 = (bf16[8,16,640]{2,1,0:T(8,128)(2,1)S(1)}, bf16[8,16,640]{2,1,0:T(8,128)(2,1)S(1)}, u32[]{:S(2)}, u32[]{:S(2)}) collective-permute-start(bf16[8,16,640]{2,1,0:T(8,128)(2,1)S(1)} %pad_maximum_fusion.7), channel_id=1, source_target_pairs={{0,8},{8,0},{16,24},{24,16},{1,9},{9,1},{17,25},{25,17},{2,10},{10... | collective-permute-start | bytes 491528 | tf_op jit(solution)/shard_map/ppermute | solution.py:37
  116.0 20.1 %collective-permute-start.23 = (bf16[2,196,640]{2,1,0:T(8,128)(2,1)S(1)}, bf16[2,196,640]{2,1,0:T(8,128)(2,1)S(1)}, u32[]{:S(2)}, u32[]{:S(2)}) collective-permute-start(bf16[2,196,640]{2,1,0:T(8,128)(2,1)S(1)} %add_convert_fusion.5), channel_id=1, source_target_pairs={{2,4},{3,5},{4,2},{5,3},{10,12},{11,13},{12,10},{13,11},{18,20},{1... | collective-permute-start | bytes 1505288 | tf_op jit(solution)/shard_map/ppermute | solution.py:75
  122.2 15.5 %collective-permute-start.28 = (bf16[2,196,640]{2,1,0:T(8,128)(2,1)}, bf16[2,196,640]{2,1,0:T(8,128)(2,1)S(1)}, u32[]{:S(2)}, u32[]{:S(2)}) collective-permute-start(bf16[2,196,640]{2,1,0:T(8,128)(2,1)} %shard_map.143), channel_id=1, source_target_pairs={{6,4},{7,5},{0,2},{1,3},{14,12},{15,13},{8,10},{9,11},{22,20},{23,... | collective-permute-start | bytes 1505288 | tf_op jit(solution)/shard_map/ppermute | solution.py:75
  126.7 9.3 %collective-permute-start.31 = (bf16[8,32,640]{2,1,0:T(8,128)(2,1)S(1)}, bf16[8,32,640]{2,1,0:T(8,128)(2,1)S(1)}, u32[]{:S(2)}, u32[]{:S(2)}) collective-permute-start(bf16[8,32,640]{2,1,0:T(8,128)(2,1)S(1)} %pad_maximum_fusion.5), channel_id=1, source_target_pairs={{0,16},{8,24},{16,0},{24,8},{1,17},{9,25},{17,1},{25,9},{2,18},{10... | collective-permute-start | bytes 983048 | tf_op jit(solution)/shard_map/ppermute | solution.py:37
  138.8 18.5 %collective-permute-start.34 = (bf16[2,196,640]{2,1,0:T(8,128)(2,1)S(1)}, bf16[2,196,640]{2,1,0:T(8,128)(2,1)S(1)}, u32[]{:S(2)}, u32[]{:S(2)}) collective-permute-start(bf16[2,196,640]{2,1,0:T(8,128)(2,1)S(1)} %copy-done.16), channel_id=1, source_target_pairs={{6,4},{7,5},{0,2},{1,3},{14,12},{15,13},{8,10},{9,11},{22,20},{23,... | collective-permute-start | bytes 1505288 | tf_op jit(solution)/shard_map/ppermute | solution.py:75
  146.2 22.2 %collective-permute-start.25 = (bf16[2,196,640]{2,1,0:T(8,128)(2,1)}, bf16[2,196,640]{2,1,0:T(8,128)(2,1)S(1)}, u32[]{:S(2)}, u32[]{:S(2)}) collective-permute-start(bf16[2,196,640]{2,1,0:T(8,128)(2,1)} %add_convert_fusion.4), channel_id=1, source_target_pairs={{0,2},{1,3},{2,0},{3,1},{4,6},{5,7},{6,4},{7,5},{8,10},{9,11},{10,... | collective-permute-start | bytes 1505288 | tf_op jit(solution)/shard_map/ppermute | solution.py:75
  146.2 17.8 %collective-permute-start.27 = (bf16[2,196,640]{2,1,0:T(8,128)(2,1)S(1)}, bf16[2,196,640]{2,1,0:T(8,128)(2,1)S(1)}, u32[]{:S(2)}, u32[]{:S(2)}) collective-permute-start(bf16[2,196,640]{2,1,0:T(8,128)(2,1)S(1)} %add_convert_fusion.3), channel_id=1, source_target_pairs={{2,4},{3,5},{4,2},{5,3},{10,12},{11,13},{12,10},{13,11},{18,20},{1... | collective-permute-start | bytes 1505288 | tf_op jit(solution)/shard_map/ppermute | solution.py:75
  158.2 11.9 %collective-permute-start.35 = (bf16[2,196,640]{2,1,0:T(8,128)(2,1)}, bf16[2,196,640]{2,1,0:T(8,128)(2,1)S(1)}, u32[]{:S(2)}, u32[]{:S(2)}) collective-permute-start(bf16[2,196,640]{2,1,0:T(8,128)(2,1)} %add_convert_fusion), channel_id=1, source_target_pairs={{2,4},{3,5},{4,2},{5,3},{10,12},{11,13},{12,10},{13,11},{18,20},{1... | collective-permute-start | bytes 1505288 | tf_op jit(solution)/shard_map/ppermute | solution.py:75
  158.9 18.7 %collective-permute-start.33 = (bf16[2,196,640]{2,1,0:T(8,128)(2,1)}, bf16[2,196,640]{2,1,0:T(8,128)(2,1)S(1)}, u32[]{:S(2)}, u32[]{:S(2)}) collective-permute-start(bf16[2,196,640]{2,1,0:T(8,128)(2,1)} %add_convert_fusion.1), channel_id=1, source_target_pairs={{0,2},{1,3},{2,0},{3,1},{4,6},{5,7},{6,4},{7,5},{8,10},{9,11},{10,... | collective-permute-start | bytes 1505288 | tf_op jit(solution)/shard_map/ppermute | solution.py:75
  182.0 10.5 %collective-permute-start.37 = (bf16[2,80,1024]{2,1,0:T(8,128)(2,1)S(1)}, bf16[2,80,1024]{2,1,0:T(8,128)(2,1)S(1)}, u32[]{:S(2)}, u32[]{:S(2)}) collective-permute-start(bf16[2,80,1024]{2,1,0:T(8,128)(2,1)S(1)} %slice.139), channel_id=1, source_target_pairs={{0,2},{1,3},{2,0},{3,1},{4,6},{5,7},{6,4},{7,5},{8,10},{9,11},{10,... | collective-permute-start | bytes 983048 | tf_op jit(solution)/shard_map/ppermute | solution.py:37
  192.7 10.2 %collective-permute-start.38 = (bf16[80,1024]{1,0:T(8,128)(2,1)S(1)}, bf16[80,1024]{1,0:T(8,128)(2,1)S(1)}, u32[]{:S(2)}, u32[]{:S(2)}) collective-permute-start(bf16[80,1024]{1,0:T(8,128)(2,1)S(1)} %slice_bitcast_fusion), channel_id=1, source_target_pairs={{0,4},{1,5},{2,6},{3,7},{4,0},{5,1},{6,2},{7,3},{8,12},{9,13},{10,... | collective-permute-start | bytes 491528 | tf_op jit(solution)/shard_map/ppermute | solution.py:37
  (46 other events, 457.1 us)

commit v5 on v4

--- a/solution.py
+++ b/solution.py
@@ -80,9 +80,15 @@
 
 
 def attend_kernel(heads, order, length, *refs):
-    shards, (gain, w_q, w_k, w_v, q_bias, v_bias, context, normed, q_rows, kv_rows, sems) = refs[:8], refs[8:]
+    shards, (gain, w_q, w_k, w_v, q_bias, v_bias, context, normed, here_rows, q_rows, kv_rows, sems) = refs[:8], refs[8:]
     width = shards[0].shape[1]
     group, count = context.shape[:2]
+    loads = [
+        pltpu.make_async_copy(shard, here_rows.at[k], sems.at[3, k]) for k, shard in enumerate(shards)
+    ]
+    for load in loads:
+        load.start()
+    shards = [here_rows.at[k] for k in range(8)]
     copies = []
     for k in range(8):
         rows = pl.ds(pl.multiple_of(order[k] * width, width), width)
@@ -98,6 +104,7 @@
             copy.start()
     total = None
     for k in range(8):
+        loads[k].wait()
         wide = shards[k][...].astype(jnp.float32)
         part = jnp.sum(wide * wide, axis=1, keepdims=True)
         total = part if total is None else total + part
@@ -296,13 +303,14 @@
         return pl.pallas_call(
             functools.partial(attend_kernel, heads),
             out_shape=jax.ShapeDtypeStruct((sizes[i], L, heads * HS), jnp.bfloat16),
-            in_specs=[whole(pltpu.SMEM)] * 2 + [whole()] * 9 + [whole(pl.ANY)] * 3 + [whole()] * 2,
+            in_specs=[whole(pltpu.SMEM)] * 2 + [whole(pl.ANY)] * 8 + [whole()] + [whole(pl.ANY)] * 3 + [whole()] * 2,
             out_specs=whole(),
             scratch_shapes=[
                 pltpu.VMEM((sizes[i] * L, 8 * width), jnp.bfloat16),
+                pltpu.VMEM((8, sizes[i] * L, width), jnp.bfloat16),
                 pltpu.VMEM((8 * width, heads * HS), jnp.bfloat16),
                 pltpu.VMEM((8 * width, 2 * HS), jnp.bfloat16),
-                pltpu.SemaphoreType.DMA((3, 8)),
+                pltpu.SemaphoreType.DMA((4, 8)),
             ],
             compiler_params=pltpu.CompilerParams(vmem_limit_bytes=VMEM_A * 2**20),
             cost_estimate=pl.CostEstimate(

time: 215 us -> 215 us (level)
  transfers between devices with their start and end apart: 42 -> 42, of which waited for: 17 -> 17; matrix products, arithmetic and copies ran while one was open for 7% -> 7% of each run, Pallas kernels for 20% -> 21%
where the time goes in v5:
time: 215 us; the launch traced here: 214 us
  waiting for transfers between devices  90.8 us (42%)
  starting transfers between devices  53.4 us (25%)
  Pallas kernels  45.7 us (21%)
  other arithmetic  12.8 us (6%)
  local copies, waits for them, and re-layouts  9.72 us (5%)
    ppermute x20, waiting for transfers between devices, permuted(): return lax.ppermute(value, 'tp', pairs)  52.1 us
    ppermute x22, waiting for transfers between devices, swapped(): return lax.ppermute(value, axis, pairs)  38.6 us
    ppermute x20, starting transfers between devices, permuted(): return lax.ppermute(value, 'tp', pairs)  34.7 us
    pallas_call x2, Pallas kernels, attend(): pl.pallas_call(functools.partial(attend_kernel, heads), out_shape=jax.Sha...  25.1 us
    ppermute x22, starting transfers between devices, swapped(): return lax.ppermute(value, axis, pairs)  18.6 us
    pallas_call x3, Pallas kernels, out(): pl.pallas_call(out_kernel, out_shape=[jax.ShapeDtypeStruct((size, L, widt...  17.1 us
  transfers between devices with their start and end apart: 42, of which 17 were waited for; matrix products, arithmetic and copies ran while one was open for 7% of the time, Pallas kernels for 21%

profile of v5, /device:TPU:0, one launch (start us, length us, event | category | flops | bytes accessed | tf_op | source)
XLA Modules:
  0.0 214.1 jit_solution(9442810544966733583)
XLA Ops:
  2.6 3.1 %collective-permute-start = (bf16[392,640]{1,0:T(8,128)(2,1)S(1)}, bf16[392,640]{1,0:T(8,128)(2,1)S(1)}, u32[]{:S(2)}, u32[]{:S(2)}) collective-permute-start(bf16[392,640]{1,0:T(8,128)(2,1)S(1)} %slice_select_fusion.1.refs_0_.refs_3_), channel_id=1, source_target_pairs={{0,2},{1,3},{2,0},{3,1},{4,6},{5,7},{6,4},{7,5},{8,10},{9,11},{10,... | collective-permute-start | bytes 1505288 | tf_op jit(solution)/shard_map/ppermute | solution.py:75
  7.7 2.0 constant_dynamic-slice_fusion.3
  9.7 1.6 pad_maximum_fusion
  12.0 5.2 %collective-permute-done.refs_1_ = bf16[392,640]{1,0:T(8,128)(2,1)S(1)} collective-permute-done((bf16[392,640]{1,0:T(8,128)(2,1)S(1)}, bf16[392,640]{1,0:T(8,128)(2,1)S(1)}, u32[]{:S(2)}, u32[]{:S(2)}) %collective-permute-start) | collective-permute-done | bytes 501792 | tf_op jit(solution)/shard_map/ppermute | solution.py:75
  22.7 7.7 %collective-permute-start.5 = (bf16[4,16,640]{2,1,0:T(8,128)(2,1)S(1)}, bf16[4,16,640]{2,1,0:T(8,128)(2,1)S(1)}, u32[]{:S(2)}, u32[]{:S(2)}) collective-permute-start(bf16[4,16,640]{2,1,0:T(8,128)(2,1)S(1)} %pad_maximum_fusion.9), channel_id=1, source_target_pairs={{0,2},{1,3},{2,0},{3,1},{4,6},{5,7},{6,4},{7,5},{8,10},{9,11},{10,... | collective-permute-start | bytes 245768 | tf_op jit(solution)/shard_map/ppermute | solution.py:37
  31.1 10.6 %collective-permute-done.5 = bf16[4,16,640]{2,1,0:T(8,128)(2,1)S(1)} collective-permute-done((bf16[4,16,640]{2,1,0:T(8,128)(2,1)S(1)}, bf16[4,16,640]{2,1,0:T(8,128)(2,1)S(1)}, u32[]{:S(2)}, u32[]{:S(2)}) %collective-permute-start.5) | collective-permute-done | bytes 81952 | tf_op jit(solution)/shard_map/ppermute | solution.py:37
  44.1 8.4 %collective-permute-done.8.refs_1_ = bf16[392,640]{1,0:T(8,128)(2,1)S(1)} collective-permute-done((bf16[392,640]{1,0:T(8,128)(2,1)S(1)}, bf16[392,640]{1,0:T(8,128)(2,1)S(1)}, u32[]{:S(2)}, u32[]{:S(2)}) %collective-permute-start.8) | collective-permute-done | bytes 501792 | tf_op jit(solution)/shard_map/ppermute | solution.py:75
  53.0 9.8 %collective-permute-done.6 = bf16[392,640]{1,0:T(8,128)(2,1)S(1)} collective-permute-done((bf16[392,640]{1,0:T(8,128)(2,1)S(1)}, bf16[392,640]{1,0:T(8,128)(2,1)S(1)}, u32[]{:S(2)}, u32[]{:S(2)}) %collective-permute-start.6) | collective-permute-done | bytes 501792 | tf_op jit(solution)/shard_map/ppermute | solution.py:75
  66.7 12.6 %shard_map.140.own = bf16[2,196,512]{2,1,0:T(8,128)(2,1)} custom-call(s32[8]{0:T(128)} %pad_add_fusion.1.order, s32[2]{0:T(128)} %get-tuple-element.188.length, bf16[392,640]{1,0:T(8,128)(2,1)} %copy-done, bf16[392,640]{1,0:T(8,128)(2,1)} %copy-done.18, bf16[392,640]{1,0:T(8,128)(2,1)} %copy-done.8, bf16[392,640]{1,0:T(8,128)(2,1)} %copy-done.10, ...), custom_call_target="tpu_custom_call" | custom-call | flops 3082813440 | bytes 25165824 | tf_op jit(solution)/shard_map/pallas_call | solution.py:303
  82.8 6.7 %shard_map.141 = (bf16[2,196,640]{2,1,0:T(8,128)(2,1)}, bf16[2,196,640]{2,1,0:T(8,128)(2,1)}, bf16[2,196,640]{2,1,0:T(8,128)(2,1)}, bf16[2,196,640]{2,1,0:T(8,128)(2,1)}) custom-call(s32[4]{0:T(128)} %copy-done.32, s32[4]{0:T(128)} %copy-done.31, bf16[2,196,512]{2,1,0:T(8,128)(2,1)} %shard_map.140.own, bf16[2,196,512]{2,1,0:T(8,128)(2,1)} %copy-done.28, ...), custom_call_target="tpu_custom_call" | custom-call | flops 2055208960 | bytes 33554432 | tf_op jit(solution)/shard_map/pallas_call | solution.py:326
  89.5 5.8 %collective-permute-done.17 = bf16[392,640]{1,0:T(8,128)(2,1)S(1)} collective-permute-done((bf16[392,640]{1,0:T(8,128)(2,1)S(1)}, bf16[392,640]{1,0:T(8,128)(2,1)S(1)}, u32[]{:S(2)}, u32[]{:S(2)}) %collective-permute-start.17) | collective-permute-done | bytes 501792 | tf_op jit(solution)/shard_map/ppermute | solution.py:75
  98.5 12.6 %shard_map.142.own = bf16[2,196,512]{2,1,0:T(8,128)(2,1)} custom-call(s32[8]{0:T(128)} %pad_add_fusion.1.order, s32[2]{0:T(128)} %get-tuple-element.189.length, bf16[392,640]{1,0:T(8,128)(2,1)} %copy-done.2, bf16[392,640]{1,0:T(8,128)(2,1)} %copy-done.19, bf16[392,640]{1,0:T(8,128)(2,1)} %copy-done.7, bf16[392,640]{1,0:T(8,128)(2,1)} %copy-done.9, ...), custom_call_target="tpu_custom_call" | custom-call | flops 3082813440 | bytes 25165824 | tf_op jit(solution)/shard_map/pallas_call | solution.py:303
  111.5 3.3 %collective-permute-start.26 = (bf16[2,196,640]{2,1,0:T(8,128)(2,1)S(1)}, bf16[2,196,640]{2,1,0:T(8,128)(2,1)S(1)}, u32[]{:S(2)}, u32[]{:S(2)}) collective-permute-start(bf16[2,196,640]{2,1,0:T(8,128)(2,1)S(1)} %copy-done.14), channel_id=1, source_target_pairs={{6,4},{7,5},{0,2},{1,3},{14,12},{15,13},{8,10},{9,11},{22,20},{23,... | collective-permute-start | bytes 1505288 | tf_op jit(solution)/shard_map/ppermute | solution.py:75
  118.2 4.7 %shard_map.143 = bf16[2,196,640]{2,1,0:T(8,128)(2,1)} custom-call(s32[1]{0:T(128)} %bitcast.15.chips, s32[1]{0:T(128)} %slice.111.blocks, bf16[2,196,512]{2,1,0:T(8,128)(2,1)} %shard_map.142.own, bf16[2,196,512]{2,1,0:T(8,128)(2,1)} %copy-done.11, bf16[512,5120]{1,0:T(8,128)(2,1)} %w_own.5, bf16[512,2560]{1,0:T(8,128)(2,1)} %collective-permute-done.16.w_other), custom_call_target="tpu_custom_call" | custom-call | flops 513802240 | bytes 8388608 | tf_op jit(solution)/shard_map/pallas_call | solution.py:326
  122.9 4.2 %collective-permute-start.28 = (bf16[2,196,640]{2,1,0:T(8,128)(2,1)}, bf16[2,196,640]{2,1,0:T(8,128)(2,1)S(1)}, u32[]{:S(2)}, u32[]{:S(2)}) collective-permute-start(bf16[2,196,640]{2,1,0:T(8,128)(2,1)} %shard_map.143), channel_id=1, source_target_pairs={{6,4},{7,5},{0,2},{1,3},{14,12},{15,13},{8,10},{9,11},{22,20},{23,... | collective-permute-start | bytes 1505288 | tf_op jit(solution)/shard_map/ppermute | solution.py:75
  128.9 5.8 %shard_map.144 = (bf16[2,196,640]{2,1,0:T(8,128)(2,1)}, bf16[2,196,640]{2,1,0:T(8,128)(2,1)}, bf16[2,196,640]{2,1,0:T(8,128)(2,1)}) custom-call(s32[3]{0:T(128)} %pad_add_fusion.2.chips, s32[3]{0:T(128)} %bitcast.67, bf16[2,196,512]{2,1,0:T(8,128)(2,1)} %shard_map.142.own, bf16[2,196,512]{2,1,0:T(8,128)(2,1)} %copy-done.11, bf16[512,5120]{1,0:T(8,128)(2,1)} %w_own.5, ...), custom_call_target="tpu_custom_call" | custom-call | flops 1541406720 | bytes 25165824 | tf_op jit(solution)/shard_map/pallas_call | solution.py:326
  134.7 1.9 collective-permute-done.31
  136.6 1.8 collective-permute-done.28
  139.5 6.2 %collective-permute-start.34 = (bf16[2,196,640]{2,1,0:T(8,128)(2,1)S(1)}, bf16[2,196,640]{2,1,0:T(8,128)(2,1)S(1)}, u32[]{:S(2)}, u32[]{:S(2)}) collective-permute-start(bf16[2,196,640]{2,1,0:T(8,128)(2,1)S(1)} %copy-done.16), channel_id=1, source_target_pairs={{6,4},{7,5},{0,2},{1,3},{14,12},{15,13},{8,10},{9,11},{22,20},{23,... | collective-permute-start | bytes 1505288 | tf_op jit(solution)/shard_map/ppermute | solution.py:75
  148.3 9.5 %collective-permute-done.34 = bf16[2,196,640]{2,1,0:T(8,128)(2,1)S(1)} collective-permute-done((bf16[2,196,640]{2,1,0:T(8,128)(2,1)S(1)}, bf16[2,196,640]{2,1,0:T(8,128)(2,1)S(1)}, u32[]{:S(2)}, u32[]{:S(2)}) %collective-permute-start.34) | collective-permute-done | bytes 501792 | tf_op jit(solution)/shard_map/ppermute | solution.py:75
  159.4 5.1 %collective-permute-start.33 = (bf16[2,196,640]{2,1,0:T(8,128)(2,1)}, bf16[2,196,640]{2,1,0:T(8,128)(2,1)S(1)}, u32[]{:S(2)}, u32[]{:S(2)}) collective-permute-start(bf16[2,196,640]{2,1,0:T(8,128)(2,1)} %add_convert_fusion.1), channel_id=1, source_target_pairs={{0,2},{1,3},{2,0},{3,1},{4,6},{5,7},{6,4},{7,5},{8,10},{9,11},{10,... | collective-permute-start | bytes 1505288 | tf_op jit(solution)/shard_map/ppermute | solution.py:75
  164.7 4.2 %collective-permute-done.25.refs_1_ = bf16[2,196,640]{2,1,0:T(8,128)(2,1)S(1)} collective-permute-done((bf16[2,196,640]{2,1,0:T(8,128)(2,1)}, bf16[2,196,640]{2,1,0:T(8,128)(2,1)S(1)}, u32[]{:S(2)}, u32[]{:S(2)}) %collective-permute-start.25) | collective-permute-done | bytes 501792 | tf_op jit(solution)/shard_map/ppermute | solution.py:75
  168.9 1.7 shard_map.145
  170.7 7.4 %collective-permute-done.33.refs_1_ = bf16[2,196,640]{2,1,0:T(8,128)(2,1)S(1)} collective-permute-done((bf16[2,196,640]{2,1,0:T(8,128)(2,1)}, bf16[2,196,640]{2,1,0:T(8,128)(2,1)S(1)}, u32[]{:S(2)}, u32[]{:S(2)}) %collective-permute-start.33) | collective-permute-done | bytes 501792 | tf_op jit(solution)/shard_map/ppermute | solution.py:75
  178.0 1.7 shard_map.146
  179.9 2.1 collective-permute-done.36
  182.4 2.4 %collective-permute-start.37 = (bf16[2,80,1024]{2,1,0:T(8,128)(2,1)S(1)}, bf16[2,80,1024]{2,1,0:T(8,128)(2,1)S(1)}, u32[]{:S(2)}, u32[]{:S(2)}) collective-permute-start(bf16[2,80,1024]{2,1,0:T(8,128)(2,1)S(1)} %slice.139), channel_id=1, source_target_pairs={{0,2},{1,3},{2,0},{3,1},{4,6},{5,7},{6,4},{7,5},{8,10},{9,11},{10,... | collective-permute-start | bytes 983048 | tf_op jit(solution)/shard_map/ppermute | solution.py:37
  184.9 8.0 %collective-permute-done.37 = bf16[2,80,1024]{2,1,0:T(8,128)(2,1)S(1)} collective-permute-done((bf16[2,80,1024]{2,1,0:T(8,128)(2,1)S(1)}, bf16[2,80,1024]{2,1,0:T(8,128)(2,1)S(1)}, u32[]{:S(2)}, u32[]{:S(2)}) %collective-permute-start.37) | collective-permute-done | bytes 327712 | tf_op jit(solution)/shard_map/ppermute | solution.py:37
  193.1 2.2 %collective-permute-start.38 = (bf16[80,1024]{1,0:T(8,128)(2,1)S(1)}, bf16[80,1024]{1,0:T(8,128)(2,1)S(1)}, u32[]{:S(2)}, u32[]{:S(2)}) collective-permute-start(bf16[80,1024]{1,0:T(8,128)(2,1)S(1)} %slice_bitcast_fusion), channel_id=1, source_target_pairs={{0,4},{1,5},{2,6},{3,7},{4,0},{5,1},{6,2},{7,3},{8,12},{9,13},{10,... | collective-permute-start | bytes 491528 | tf_op jit(solution)/shard_map/ppermute | solution.py:37
  195.2 8.0 %collective-permute-done.38 = bf16[80,1024]{1,0:T(8,128)(2,1)S(1)} collective-permute-done((bf16[80,1024]{1,0:T(8,128)(2,1)S(1)}, bf16[80,1024]{1,0:T(8,128)(2,1)S(1)}, u32[]{:S(2)}, u32[]{:S(2)}) %collective-permute-start.38) | collective-permute-done | bytes 163872 | tf_op jit(solution)/shard_map/ppermute | solution.py:37
  204.9 3.6 %collective-permute-done.40 = f32[2,1024]{1,0:T(2,128)S(1)} collective-permute-done((f32[2,1024]{1,0:T(2,128)S(1)}, f32[2,1024]{1,0:T(2,128)S(1)}, u32[]{:S(2)}, u32[]{:S(2)}) %collective-permute-start.40) | collective-permute-done | bytes 8224 | tf_op jit(solution)/shard_map/ppermute | solution.py:37
  210.3 2.9 %collective-permute-done.41 = f32[2,1024]{1,0:T(2,128)S(1)} collective-permute-done((f32[2,1024]{1,0:T(2,128)S(1)}, f32[2,1024]{1,0:T(2,128)S(1)}, u32[]{:S(2)}, u32[]{:S(2)}) %collective-permute-start.41) | collective-permute-done | bytes 8224 | tf_op jit(solution)/shard_map/ppermute | solution.py:37
  (197 shorter events, 39.4 us)
Async XLA Ops:
  2.6 14.5 %collective-permute-start = (bf16[392,640]{1,0:T(8,128)(2,1)S(1)}, bf16[392,640]{1,0:T(8,128)(2,1)S(1)}, u32[]{:S(2)}, u32[]{:S(2)}) collective-permute-start(bf16[392,640]{1,0:T(8,128)(2,1)S(1)} %slice_select_fusion.1.refs_0_.refs_3_), channel_id=1, source_target_pairs={{0,2},{1,3},{2,0},{3,1},{4,6},{5,7},{6,4},{7,5},{8,10},{9,11},{10,... | collective-permute-start | bytes 1505288 | tf_op jit(solution)/shard_map/ppermute | solution.py:75
  5.7 11.4 %collective-permute-start.1 = (bf16[392,640]{1,0:T(8,128)(2,1)S(1)}, bf16[392,640]{1,0:T(8,128)(2,1)S(1)}, u32[]{:S(2)}, u32[]{:S(2)}) collective-permute-start(bf16[392,640]{1,0:T(8,128)(2,1)S(1)} %slice_select_fusion.1.refs_0_.refs_3_), channel_id=1, source_target_pairs={{2,4},{3,5},{4,2},{5,3},{10,12},{11,13},{12,10},{13,11},{18,20},{1... | collective-permute-start | bytes 1505288 | tf_op jit(solution)/shard_map/ppermute | solution.py:75
  17.2 65.0 %collective-permute-start.16 = (bf16[512,2560]{1,0:T(8,128)(2,1)}, bf16[512,2560]{1,0:T(8,128)(2,1)}, u32[]{:S(2)}, u32[]{:S(2)}) collective-permute-start(bf16[512,2560]{1,0:T(8,128)(2,1)} %pad_maximum_fusion), channel_id=1, source_target_pairs={{0,1},{1,0},{2,3},{3,2},{4,5},{5,4},{6,7},{7,6},{8,9},{9,8},{10,11... | collective-permute-start | bytes 7864328 | tf_op jit(solution)/shard_map/ppermute | solution.py:37
  18.1 23.6 %collective-permute-start.3 = (bf16[392,640]{1,0:T(8,128)(2,1)S(1)}, bf16[392,640]{1,0:T(8,128)(2,1)S(1)}, u32[]{:S(2)}, u32[]{:S(2)}) collective-permute-start(bf16[392,640]{1,0:T(8,128)(2,1)S(1)} %collective-permute-done.refs_1_), channel_id=1, source_target_pairs={{2,4},{3,5},{4,2},{5,3},{10,12},{11,13},{12,10},{13,11},{18,20},{1... | collective-permute-start | bytes 1505288 | tf_op jit(solution)/shard_map/ppermute | solution.py:75
  18.8 22.9 %collective-permute-start.4 = (bf16[392,640]{1,0:T(8,128)(2,1)S(1)}, bf16[392,640]{1,0:T(8,128)(2,1)S(1)}, u32[]{:S(2)}, u32[]{:S(2)}) collective-permute-start(bf16[392,640]{1,0:T(8,128)(2,1)S(1)} %collective-permute-done.1), channel_id=1, source_target_pairs={{4,6},{5,7},{2,0},{3,1},{12,14},{13,15},{10,8},{11,9},{20,22},{21,... | collective-permute-start | bytes 1505288 | tf_op jit(solution)/shard_map/ppermute | solution.py:75
  22.7 19.0 %collective-permute-start.5 = (bf16[4,16,640]{2,1,0:T(8,128)(2,1)S(1)}, bf16[4,16,640]{2,1,0:T(8,128)(2,1)S(1)}, u32[]{:S(2)}, u32[]{:S(2)}) collective-permute-start(bf16[4,16,640]{2,1,0:T(8,128)(2,1)S(1)} %pad_maximum_fusion.9), channel_id=1, source_target_pairs={{0,2},{1,3},{2,0},{3,1},{4,6},{5,7},{6,4},{7,5},{8,10},{9,11},{10,... | collective-permute-start | bytes 245768 | tf_op jit(solution)/shard_map/ppermute | solution.py:37
  31.1 21.4 %collective-permute-start.8 = (bf16[392,640]{1,0:T(8,128)(2,1)S(1)}, bf16[392,640]{1,0:T(8,128)(2,1)S(1)}, u32[]{:S(2)}, u32[]{:S(2)}) collective-permute-start(bf16[392,640]{1,0:T(8,128)(2,1)S(1)} %slice_select_fusion.refs_0_.refs_3_), channel_id=1, source_target_pairs={{0,2},{1,3},{2,0},{3,1},{4,6},{5,7},{6,4},{7,5},{8,10},{9,11},{10,... | collective-permute-start | bytes 1505288 | tf_op jit(solution)/shard_map/ppermute | solution.py:75
  41.7 10.8 %collective-permute-start.7 = (bf16[392,640]{1,0:T(8,128)(2,1)S(1)}, bf16[392,640]{1,0:T(8,128)(2,1)S(1)}, u32[]{:S(2)}, u32[]{:S(2)}) collective-permute-start(bf16[392,640]{1,0:T(8,128)(2,1)S(1)} %slice_select_fusion.refs_0_.refs_3_), channel_id=1, source_target_pairs={{2,4},{3,5},{4,2},{5,3},{10,12},{11,13},{12,10},{13,11},{18,20},{1... | collective-permute-start | bytes 1505288 | tf_op jit(solution)/shard_map/ppermute | solution.py:75
  42.6 20.3 %collective-permute-start.6 = (bf16[392,640]{1,0:T(8,128)(2,1)S(1)}, bf16[392,640]{1,0:T(8,128)(2,1)S(1)}, u32[]{:S(2)}, u32[]{:S(2)}) collective-permute-start(bf16[392,640]{1,0:T(8,128)(2,1)S(1)} %collective-permute-done.3), channel_id=1, source_target_pairs={{4,6},{5,7},{2,0},{3,1},{12,14},{13,15},{10,8},{11,9},{20,22},{21,... | collective-permute-start | bytes 1505288 | tf_op jit(solution)/shard_map/ppermute | solution.py:75
  43.9 19.2 %collective-permute-start.9 = (bf16[392,640]{1,0:T(8,128)(2,1)S(1)}, bf16[392,640]{1,0:T(8,128)(2,1)S(1)}, u32[]{:S(2)}, u32[]{:S(2)}) collective-permute-start(bf16[392,640]{1,0:T(8,128)(2,1)S(1)} %slice_select_fusion.1.refs_0_.refs_3_), channel_id=1, source_target_pairs={{0,1},{1,0},{2,3},{3,2},{4,5},{5,4},{6,7},{7,6},{8,9},{9,8},{10,11... | collective-permute-start | bytes 1505288 | tf_op jit(solution)/shard_map/ppermute | solution.py:37
  52.5 11.9 %collective-permute-start.10 = (bf16[392,640]{1,0:T(8,128)(2,1)S(1)}, bf16[392,640]{1,0:T(8,128)(2,1)S(1)}, u32[]{:S(2)}, u32[]{:S(2)}) collective-permute-start(bf16[392,640]{1,0:T(8,128)(2,1)S(1)} %collective-permute-done.refs_1_), channel_id=1, source_target_pairs={{0,1},{1,0},{2,3},{3,2},{4,5},{5,4},{6,7},{7,6},{8,9},{9,8},{10,11... | collective-permute-start | bytes 1505288 | tf_op jit(solution)/shard_map/ppermute | solution.py:37
  52.5 13.2 %collective-permute-start.11 = (bf16[392,640]{1,0:T(8,128)(2,1)S(1)}, bf16[392,640]{1,0:T(8,128)(2,1)S(1)}, u32[]{:S(2)}, u32[]{:S(2)}) collective-permute-start(bf16[392,640]{1,0:T(8,128)(2,1)S(1)} %add.183.refs_2_), channel_id=1, source_target_pairs={{0,1},{1,0},{2,3},{3,2},{4,5},{5,4},{6,7},{7,6},{8,9},{9,8},{10,11... | collective-permute-start | bytes 1505288 | tf_op jit(solution)/shard_map/ppermute | solution.py:37
  63.1 16.7 %collective-permute-start.14 = (bf16[392,640]{1,0:T(8,128)(2,1)S(1)}, bf16[392,640]{1,0:T(8,128)(2,1)S(1)}, u32[]{:S(2)}, u32[]{:S(2)}) collective-permute-start(bf16[392,640]{1,0:T(8,128)(2,1)S(1)} %collective-permute-done.8.refs_1_), channel_id=1, source_target_pairs={{2,4},{3,5},{4,2},{5,3},{10,12},{11,13},{12,10},{13,11},{18,20},{1... | collective-permute-start | bytes 1505288 | tf_op jit(solution)/shard_map/ppermute | solution.py:75
  64.4 16.9 %collective-permute-start.15 = (bf16[392,640]{1,0:T(8,128)(2,1)S(1)}, bf16[392,640]{1,0:T(8,128)(2,1)S(1)}, u32[]{:S(2)}, u32[]{:S(2)}) collective-permute-start(bf16[392,640]{1,0:T(8,128)(2,1)S(1)} %collective-permute-done.7), channel_id=1, source_target_pairs={{4,6},{5,7},{2,0},{3,1},{12,14},{13,15},{10,8},{11,9},{20,22},{21,... | collective-permute-start | bytes 1505288 | tf_op jit(solution)/shard_map/ppermute | solution.py:75
  79.8 15.6 %collective-permute-start.17 = (bf16[392,640]{1,0:T(8,128)(2,1)S(1)}, bf16[392,640]{1,0:T(8,128)(2,1)S(1)}, u32[]{:S(2)}, u32[]{:S(2)}) collective-permute-start(bf16[392,640]{1,0:T(8,128)(2,1)S(1)} %collective-permute-done.14), channel_id=1, source_target_pairs={{4,6},{5,7},{2,0},{3,1},{12,14},{13,15},{10,8},{11,9},{20,22},{21,... | collective-permute-start | bytes 1505288 | tf_op jit(solution)/shard_map/ppermute | solution.py:75
  81.3 15.9 %collective-permute-start.18 = (bf16[392,640]{1,0:T(8,128)(2,1)S(1)}, bf16[392,640]{1,0:T(8,128)(2,1)S(1)}, u32[]{:S(2)}, u32[]{:S(2)}) collective-permute-start(bf16[392,640]{1,0:T(8,128)(2,1)S(1)} %slice_select_fusion.refs_0_.refs_3_), channel_id=1, source_target_pairs={{0,1},{1,0},{2,3},{3,2},{4,5},{5,4},{6,7},{7,6},{8,9},{9,8},{10,11... | collective-permute-start | bytes 1505288 | tf_op jit(solution)/shard_map/ppermute | solution.py:37
  81.4 15.8 %collective-permute-start.19 = (bf16[392,640]{1,0:T(8,128)(2,1)S(1)}, bf16[392,640]{1,0:T(8,128)(2,1)S(1)}, u32[]{:S(2)}, u32[]{:S(2)}) collective-permute-start(bf16[392,640]{1,0:T(8,128)(2,1)S(1)} %collective-permute-done.8.refs_1_), channel_id=1, source_target_pairs={{0,1},{1,0},{2,3},{3,2},{4,5},{5,4},{6,7},{7,6},{8,9},{9,8},{10,11... | collective-permute-start | bytes 1505288 | tf_op jit(solution)/shard_map/ppermute | solution.py:37
  82.0 15.2 %collective-permute-start.20 = (bf16[392,640]{1,0:T(8,128)(2,1)S(1)}, bf16[392,640]{1,0:T(8,128)(2,1)S(1)}, u32[]{:S(2)}, u32[]{:S(2)}) collective-permute-start(bf16[392,640]{1,0:T(8,128)(2,1)S(1)} %add.185.refs_2_), channel_id=1, source_target_pairs={{0,1},{1,0},{2,3},{3,2},{4,5},{5,4},{6,7},{7,6},{8,9},{9,8},{10,11... | collective-permute-start | bytes 1505288 | tf_op jit(solution)/shard_map/ppermute | solution.py:37
  95.6 15.5 %collective-permute-start.22 = (bf16[2,196,640]{2,1,0:T(8,128)(2,1)S(1)}, bf16[2,196,640]{2,1,0:T(8,128)(2,1)S(1)}, u32[]{:S(2)}, u32[]{:S(2)}) collective-permute-start(bf16[2,196,640]{2,1,0:T(8,128)(2,1)S(1)} %copy-done.15), channel_id=1, source_target_pairs={{6,4},{7,5},{0,2},{1,3},{14,12},{15,13},{8,10},{9,11},{22,20},{23,... | collective-permute-start | bytes 1505288 | tf_op jit(solution)/shard_map/ppermute | solution.py:75
  97.1 17.7 %collective-permute-start.29 = (bf16[4,16,640]{2,1,0:T(8,128)(2,1)S(1)}, bf16[4,16,640]{2,1,0:T(8,128)(2,1)S(1)}, u32[]{:S(2)}, u32[]{:S(2)}) collective-permute-start(bf16[4,16,640]{2,1,0:T(8,128)(2,1)S(1)} %pad_maximum_fusion.10), channel_id=1, source_target_pairs={{0,4},{1,5},{2,6},{3,7},{4,0},{5,1},{6,2},{7,3},{8,12},{9,13},{10,... | collective-permute-start | bytes 245768 | tf_op jit(solution)/shard_map/ppermute | solution.py:37
  111.5 23.2 %collective-permute-start.26 = (bf16[2,196,640]{2,1,0:T(8,128)(2,1)S(1)}, bf16[2,196,640]{2,1,0:T(8,128)(2,1)S(1)}, u32[]{:S(2)}, u32[]{:S(2)}) collective-permute-start(bf16[2,196,640]{2,1,0:T(8,128)(2,1)S(1)} %copy-done.14), channel_id=1, source_target_pairs={{6,4},{7,5},{0,2},{1,3},{14,12},{15,13},{8,10},{9,11},{22,20},{23,... | collective-permute-start | bytes 1505288 | tf_op jit(solution)/shard_map/ppermute | solution.py:75
  114.8 12.3 %collective-permute-start.30 = (bf16[8,16,640]{2,1,0:T(8,128)(2,1)S(1)}, bf16[8,16,640]{2,1,0:T(8,128)(2,1)S(1)}, u32[]{:S(2)}, u32[]{:S(2)}) collective-permute-start(bf16[8,16,640]{2,1,0:T(8,128)(2,1)S(1)} %pad_maximum_fusion.7), channel_id=1, source_target_pairs={{0,8},{8,0},{16,24},{24,16},{1,9},{9,1},{17,25},{25,17},{2,10},{10... | collective-permute-start | bytes 491528 | tf_op jit(solution)/shard_map/ppermute | solution.py:37
  116.5 20.1 %collective-permute-start.23 = (bf16[2,196,640]{2,1,0:T(8,128)(2,1)S(1)}, bf16[2,196,640]{2,1,0:T(8,128)(2,1)S(1)}, u32[]{:S(2)}, u32[]{:S(2)}) collective-permute-start(bf16[2,196,640]{2,1,0:T(8,128)(2,1)S(1)} %add_convert_fusion.5), channel_id=1, source_target_pairs={{2,4},{3,5},{4,2},{5,3},{10,12},{11,13},{12,10},{13,11},{18,20},{1... | collective-permute-start | bytes 1505288 | tf_op jit(solution)/shard_map/ppermute | solution.py:75
  122.9 15.5 %collective-permute-start.28 = (bf16[2,196,640]{2,1,0:T(8,128)(2,1)}, bf16[2,196,640]{2,1,0:T(8,128)(2,1)S(1)}, u32[]{:S(2)}, u32[]{:S(2)}) collective-permute-start(bf16[2,196,640]{2,1,0:T(8,128)(2,1)} %shard_map.143), channel_id=1, source_target_pairs={{6,4},{7,5},{0,2},{1,3},{14,12},{15,13},{8,10},{9,11},{22,20},{23,... | collective-permute-start | bytes 1505288 | tf_op jit(solution)/shard_map/ppermute | solution.py:75
  127.3 9.3 %collective-permute-start.31 = (bf16[8,32,640]{2,1,0:T(8,128)(2,1)S(1)}, bf16[8,32,640]{2,1,0:T(8,128)(2,1)S(1)}, u32[]{:S(2)}, u32[]{:S(2)}) collective-permute-start(bf16[8,32,640]{2,1,0:T(8,128)(2,1)S(1)} %pad_maximum_fusion.5), channel_id=1, source_target_pairs={{0,16},{8,24},{16,0},{24,8},{1,17},{9,25},{17,1},{25,9},{2,18},{10... | collective-permute-start | bytes 983048 | tf_op jit(solution)/shard_map/ppermute | solution.py:37
  139.5 18.3 %collective-permute-start.34 = (bf16[2,196,640]{2,1,0:T(8,128)(2,1)S(1)}, bf16[2,196,640]{2,1,0:T(8,128)(2,1)S(1)}, u32[]{:S(2)}, u32[]{:S(2)}) collective-permute-start(bf16[2,196,640]{2,1,0:T(8,128)(2,1)S(1)} %copy-done.16), channel_id=1, source_target_pairs={{6,4},{7,5},{0,2},{1,3},{14,12},{15,13},{8,10},{9,11},{22,20},{23,... | collective-permute-start | bytes 1505288 | tf_op jit(solution)/shard_map/ppermute | solution.py:75
  146.7 22.2 %collective-permute-start.25 = (bf16[2,196,640]{2,1,0:T(8,128)(2,1)}, bf16[2,196,640]{2,1,0:T(8,128)(2,1)S(1)}, u32[]{:S(2)}, u32[]{:S(2)}) collective-permute-start(bf16[2,196,640]{2,1,0:T(8,128)(2,1)} %add_convert_fusion.4), channel_id=1, source_target_pairs={{0,2},{1,3},{2,0},{3,1},{4,6},{5,7},{6,4},{7,5},{8,10},{9,11},{10,... | collective-permute-start | bytes 1505288 | tf_op jit(solution)/shard_map/ppermute | solution.py:75
  146.7 18.0 %collective-permute-start.27 = (bf16[2,196,640]{2,1,0:T(8,128)(2,1)S(1)}, bf16[2,196,640]{2,1,0:T(8,128)(2,1)S(1)}, u32[]{:S(2)}, u32[]{:S(2)}) collective-permute-start(bf16[2,196,640]{2,1,0:T(8,128)(2,1)S(1)} %add_convert_fusion.3), channel_id=1, source_target_pairs={{2,4},{3,5},{4,2},{5,3},{10,12},{11,13},{12,10},{13,11},{18,20},{1... | collective-permute-start | bytes 1505288 | tf_op jit(solution)/shard_map/ppermute | solution.py:75
  158.8 11.9 %collective-permute-start.35 = (bf16[2,196,640]{2,1,0:T(8,128)(2,1)}, bf16[2,196,640]{2,1,0:T(8,128)(2,1)S(1)}, u32[]{:S(2)}, u32[]{:S(2)}) collective-permute-start(bf16[2,196,640]{2,1,0:T(8,128)(2,1)} %add_convert_fusion), channel_id=1, source_target_pairs={{2,4},{3,5},{4,2},{5,3},{10,12},{11,13},{12,10},{13,11},{18,20},{1... | collective-permute-start | bytes 1505288 | tf_op jit(solution)/shard_map/ppermute | solution.py:75
  159.4 18.6 %collective-permute-start.33 = (bf16[2,196,640]{2,1,0:T(8,128)(2,1)}, bf16[2,196,640]{2,1,0:T(8,128)(2,1)S(1)}, u32[]{:S(2)}, u32[]{:S(2)}) collective-permute-start(bf16[2,196,640]{2,1,0:T(8,128)(2,1)} %add_convert_fusion.1), channel_id=1, source_target_pairs={{0,2},{1,3},{2,0},{3,1},{4,6},{5,7},{6,4},{7,5},{8,10},{9,11},{10,... | collective-permute-start | bytes 1505288 | tf_op jit(solution)/shard_map/ppermute | solution.py:75
  182.4 10.5 %collective-permute-start.37 = (bf16[2,80,1024]{2,1,0:T(8,128)(2,1)S(1)}, bf16[2,80,1024]{2,1,0:T(8,128)(2,1)S(1)}, u32[]{:S(2)}, u32[]{:S(2)}) collective-permute-start(bf16[2,80,1024]{2,1,0:T(8,128)(2,1)S(1)} %slice.139), channel_id=1, source_target_pairs={{0,2},{1,3},{2,0},{3,1},{4,6},{5,7},{6,4},{7,5},{8,10},{9,11},{10,... | collective-permute-start | bytes 983048 | tf_op jit(solution)/shard_map/ppermute | solution.py:37
  193.1 10.2 %collective-permute-start.38 = (bf16[80,1024]{1,0:T(8,128)(2,1)S(1)}, bf16[80,1024]{1,0:T(8,128)(2,1)S(1)}, u32[]{:S(2)}, u32[]{:S(2)}) collective-permute-start(bf16[80,1024]{1,0:T(8,128)(2,1)S(1)} %slice_bitcast_fusion), channel_id=1, source_target_pairs={{0,4},{1,5},{2,6},{3,7},{4,0},{5,1},{6,2},{7,3},{8,12},{9,13},{10,... | collective-permute-start | bytes 491528 | tf_op jit(solution)/shard_map/ppermute | solution.py:37
  (46 other events, 456.9 us)
